TPU v7x, 32 devices: a whole 2x2x4 slice. The times are simulated.
32 devices in a mesh: grp: 4 (over y, x), feat: 8 (over z, core).
Axes of the slice: x: 2, y: 2, z: 4, core: 2. Of those that a mesh axis runs over, the one named last changes fastest.
Arguments:
- points: bfloat16 [8192, 32], P(('grp', 'feat')), may hold values from -6 to 6
- dual_weights: float32 [8192, 64], P(('grp', 'feat')), may hold values from -6 to 6
- velocity: float32 [8192, 64], P(('grp', 'feat')), may hold values from -1.75 to 1.75
- observed: float32 [8192], P(('grp', 'feat')), may hold values from -12 to 12
- noise_draws: float32 [8192, 64], P(('grp', 'feat')), may hold values from -3 to 3
- frequencies: bfloat16 [32, 16384], P(None, 'feat'), may hold values from -1.5 to 1.5
- phases: float32 [16384], P('feat'), may hold values from 0 to 6.2832
- prior_weights: bfloat16 [16384, 64], P('feat'), may hold values from -6 to 6
- batch_tiles: int32 [2, 4, 1], P(None, 'grp'), may hold values from 0 to 15, as said below
Outputs:
- new_duals: float32 [8192, 64], P(('grp', 'feat'))
- new_velocity: float32 [8192, 64], P(('grp', 'feat'))
Inputs may be any that keep to these rules, and one draw needn't show every extreme that they name: `batch_tiles`: in each step the 1 tile numbers of a group are distinct.
All inputs are finite; a program needn't handle non-finite values.
Results may differ from a plain program's by a relative error of at most 0.0012.
Values may be sent and summed in bfloat16 or wider, within the bound.
No kernel may reach another device: no remote copies, remote signals or barrier semaphores. Data moves between devices by JAX's collectives and lax.ppermute only.
A program may use at most 64 MiB of HBM per device.

v0:
```python
import math

import jax
import jax.numpy as jnp
from jax import lax
from jax.sharding import PartitionSpec as P

RFF = 16384
TILE = 128
STEPS = 2


amplitude = 4.0
signal = 2.0
momentum = 0.9
step_size = 0.5


def kernel_values(picked, point_block, norm_block):
    row_sq = jnp.sum(jnp.square(picked.astype(jnp.float32)), axis=1)
    inner_prod = lax.dot_general(
        picked, point_block, (((1,), (1,)), ((), ())), preferred_element_type=jnp.float32
    )
    distance = row_sq[:, None] + norm_block[None, :] - 2.0 * inner_prod
    return (amplitude * jnp.exp(-distance / point_block.shape[1])).astype(jnp.bfloat16)


def kernel_block(picked, points, local_sq, duals_bf):
    total_rows = picked.shape[0]
    block_rows = math.gcd(total_rows, 1024)
    blocks = picked.reshape(total_rows // block_rows, block_rows, picked.shape[1])

    def one_block(part_rows):
        kernel_tile = kernel_values(part_rows, points, local_sq)
        return jnp.dot(kernel_tile, duals_bf, preferred_element_type=jnp.float32)

    return lax.map(one_block, blocks).reshape(total_rows, duals_bf.shape[1])


def tile_layout(tile_ids, tiles_per, feat_index):
    owner_rank = tile_ids // tiles_per
    offsets = (tile_ids % tiles_per)[:, None] * TILE + jnp.arange(TILE, dtype=jnp.int32)[None, :]
    owned_mask = jnp.broadcast_to((owner_rank == feat_index)[:, None], offsets.shape)
    return (offsets.reshape(-1), owned_mask.reshape(-1))


def masked_rows(points, offsets, owned_mask):
    picked = points[offsets].astype(jnp.float32)
    return jnp.where(owned_mask[:, None], picked, 0.0)


def local(
    points,
    dual_weights,
    velocity,
    observed,
    noise_draws,
    frequencies,
    phases,
    prior_weights,
    batch_tiles,
):
    group_count = lax.axis_size("grp")
    feat_count = lax.axis_size("feat")
    feat_index = lax.axis_index("feat")
    local_points = points.shape[0]
    tiles_per = local_points // TILE
    inv_root = 1.0 / math.sqrt(local_points * group_count * feat_count)
    prior_scale = signal * math.sqrt(2.0 / RFF)
    local_sq = jnp.sum(jnp.square(points.astype(jnp.float32)), axis=1)
    layouts = [
        tile_layout(batch_tiles[step_index, 0], tiles_per, feat_index)
        for step_index in range(STEPS)
    ]
    for step_index in range(STEPS):
        offsets, owned_mask = layouts[step_index]
        batch_local = lax.psum(
            masked_rows(points, offsets, owned_mask).astype(jnp.bfloat16), "feat"
        )
        duals_bf = dual_weights.astype(jnp.bfloat16)
        phase_arg = (
            jnp.dot(batch_local, frequencies, preferred_element_type=jnp.float32) + phases[None, :]
        )
        features = jnp.cos(phase_arg).astype(jnp.bfloat16)
        prior_part = (
            jnp.dot(features, prior_weights, preferred_element_type=jnp.float32) * prior_scale
        )
        everyone = lax.all_gather(batch_local, "grp", axis=0, tiled=True)
        own_sum = lax.psum_scatter(
            kernel_block(everyone, points, local_sq, duals_bf),
            "grp",
            scatter_dimension=0,
            tiled=True,
        )
        combined = lax.psum(own_sum * inv_root + prior_part, "feat")
        gradient = combined - observed[offsets][:, None] + noise_draws[offsets]
        new_vel = momentum * velocity[offsets] - step_size * gradient
        new_duals = dual_weights[offsets] + new_vel
        target_rows = jnp.where(owned_mask, offsets, local_points)
        dual_weights = dual_weights.at[target_rows].set(new_duals, mode="drop")
        velocity = velocity.at[target_rows].set(new_vel, mode="drop")
    return (dual_weights, velocity)


def solution(mesh):
    return jax.shard_map(
        local,
        mesh=mesh,
        in_specs=(
            P(("grp", "feat"), None),
            P(("grp", "feat"), None),
            P(("grp", "feat"), None),
            P(("grp", "feat")),
            P(("grp", "feat"), None),
            P(None, "feat"),
            P("feat"),
            P("feat", None),
            P(None, "grp", None),
        ),
        out_specs=(P(("grp", "feat"), None), P(("grp", "feat"), None)),
        check_vma=False,
    )
```

profile of v0, /device:TPU:0, one launch (start us, length us, event | category | flops | bytes accessed | tf_op | source)
XLA Modules:
  0.0 177.0 jit_solution(3456499322961534248)
XLA Ops:
  7.2 1.3 fusion.52
  13.8 0.1 copy.30
  14.0 0.7 gather_fusion.7
  14.8 0.7 gather_fusion.2
  15.5 30.7 %all-reduce = (bf16[128,32]{1,0:T(8,128)(2,1)S(1)}, bf16[128,32]{1,0:T(8,128)(2,1)S(1)}) all-reduce(bf16[128,32]{1,0:T(8,128)(2,1)S(1)} %get-tuple-element.51, bf16[128,32]{1,0:T(8,128)(2,1)S(1)} %get-tuple-element.50), channel_id=1, replica_groups=mesh['grp'=4,'feat'=8] {'feat'}, use_global_device_ids=true, to_apply=%region_0.0 | all-reduce | flops 8192 | bytes 32768 | tf_op jit(solution)/shard_map/psum | solution.py:77
  46.2 8.5 %all_gather.6 = bf16[512,32]{1,0:T(8,128)(2,1)S(1)} all-gather(bf16[128,32]{1,0:T(8,128)(2,1)S(1)} %get-tuple-element.36), channel_id=1, replica_groups=mesh['grp'=4,'feat'=8] {'grp'}, dimensions={0}, use_global_device_ids=true | all-gather | bytes 40960 | tf_op jit(solution)/shard_map/all_gather | solution.py:88
  54.7 0.1 multiply_reduce_fusion.1
  54.9 0.7 copy-done.2
  55.5 1.0 fusion.18
  56.6 0.0 reduce-scatter.5.cloned.1.call-start
  56.6 0.1 copy.34
  56.7 0.6 gather_fusion
  57.4 0.1 copy.33
  57.5 0.8 copy-done.3
  58.2 0.1 copy.31
  58.3 0.7 gather_fusion.4
  59.0 0.1 copy.32
  59.1 0.6 copy-done.1
  59.7 1.3 gather_fusion.3
  60.9 0.1 copy.28
  61.0 0.7 gather_fusion.1
  61.7 0.1 copy.29
  61.8 8.6 %all_gather.7 = bf16[512,32]{1,0:T(8,128)(2,1)S(1)} all-gather(bf16[128,32]{1,0:T(8,128)(2,1)S(1)} %get-tuple-element.37), channel_id=1, replica_groups=mesh['grp'=4,'feat'=8] {'grp'}, dimensions={0}, use_global_device_ids=true | all-gather | bytes 40960 | tf_op jit(solution)/shard_map/all_gather | solution.py:88
  70.4 0.1 multiply_reduce_fusion
  70.5 7.4 %reduce-scatter.3.cloned.1.call-done = f32[128,64]{0,1:T(8,128)} async-done(((f32[512,64]{0,1:T(8,128)}), f32[128,64]{0,1:T(8,128)}) %reduce-scatter.3.cloned.1.call-update) | async-done | bytes 32784 | tf_op jit(solution)/shard_map/reduce_scatter | solution.py:89
  77.9 4.6 %fusion.21 = f32[128,64]{0,1:T(8,128)S(1)} fusion(bf16[2048,64]{0,1:T(8,128)(2,1)S(1)} %copy-done, bf16[128,32]{1,0:T(8,128)(2,1)S(1)} %get-tuple-element.36, bf16[32,2048]{1,0:T(8,128)(2,1)S(1)} %copy-done.6, f32[2048]{0:T(1024)S(1)} %copy-done.7, f32[128,64]{0,1:T(8,128)} %reduce-scatter.3.cloned.1.call-done), kind=kOutput, calls=%fused_computation.39 | convolution fusion | flops 50880512 | bytes 475136 | tf_op jit(solution)/shard_map/dot_general | solution.py:86
  82.5 28.1 %psum.29 = f32[128,64]{0,1:T(8,128)S(1)} all-reduce(f32[128,64]{0,1:T(8,128)S(1)} %fusion.21), channel_id=1, replica_groups=mesh['grp'=4,'feat'=8] {'feat'}, use_global_device_ids=true, to_apply=%region_4.5 | all-reduce | flops 8192 | bytes 65536 | tf_op jit(solution)/shard_map/psum | solution.py:95
  110.5 0.1 copy.35
  110.6 1.0 scatter_fusion
  111.6 1.0 fusion.19
  112.7 0.7 gather_fusion.9
  113.3 1.3 gather_fusion.8
  114.6 0.1 copy.41
  114.7 0.6 gather_fusion.5
  115.3 0.1 copy.42
  115.4 0.1 copy.37
  115.5 1.1 scatter_fusion.1
  116.6 0.7 gather_fusion.6
  117.3 0.1 copy.38
  117.4 16.6 %reduce-scatter.5.cloned.1.call-done = f32[128,64]{0,1:T(8,128)} async-done(((f32[512,64]{0,1:T(8,128)}), f32[128,64]{0,1:T(8,128)}) %reduce-scatter.5.cloned.1.call-update) | async-done | bytes 32784 | tf_op jit(solution)/shard_map/reduce_scatter | solution.py:89
  133.9 4.6 %fusion.23 = f32[128,64]{0,1:T(8,128)S(1)} fusion(bf16[2048,64]{0,1:T(8,128)(2,1)S(1)} %copy-done, bf16[128,32]{1,0:T(8,128)(2,1)S(1)} %get-tuple-element.37, bf16[32,2048]{1,0:T(8,128)(2,1)S(1)} %copy-done.6, f32[2048]{0:T(1024)S(1)} %copy-done.7, f32[128,64]{0,1:T(8,128)} %reduce-scatter.5.cloned.1.call-done), kind=kOutput, calls=%fused_computation.41 | convolution fusion | flops 50880512 | bytes 475136 | tf_op jit(solution)/shard_map/dot_general | solution.py:86
  138.5 28.1 %psum.31 = f32[128,64]{0,1:T(8,128)S(1)} all-reduce(f32[128,64]{0,1:T(8,128)S(1)} %fusion.23), channel_id=1, replica_groups=mesh['grp'=4,'feat'=8] {'feat'}, use_global_device_ids=true, to_apply=%region_10.11 | all-reduce | flops 8192 | bytes 65536 | tf_op jit(solution)/shard_map/psum | solution.py:95
  166.6 0.1 copy.43
  166.7 1.0 scatter_fusion.2
  167.6 0.7 copy.45
  168.3 0.1 copy.44
  168.4 1.0 scatter_fusion.3
  169.4 0.7 copy.46
  (26 shorter events, 0.2 us)
Async XLA Ops:
  7.2 70.7 %copy-start = (bf16[2048,64]{0,1:T(8,128)(2,1)S(1)}, bf16[2048,64]{0,1:T(8,128)(2,1)}, u32[]{:S(2)}) copy-start(bf16[2048,64]{0,1:T(8,128)(2,1)} %param.16) | copy-start | bytes 786436
  7.2 70.7 %reduce-scatter.3.cloned.1.call-start = ((), (), s32[]{:S(2)}) async-start(), calls=%async_computation.2 | async-start | bytes 163840 | tf_op jit(solution)/shard_map/reduce_scatter | solution.py:89
  11.1 2.6 %copy-start.5 = (bf16[256,32]{0,1:T(8,128)(2,1)S(1)}, bf16[256,32]{0,1:T(8,128)(2,1)}, u32[]{:S(2)}) copy-start(bf16[256,32]{0,1:T(8,128)(2,1)} %param.9) | copy-start | bytes 49156
  54.7 0.8 copy-start.2
  56.6 77.3 %reduce-scatter.5.cloned.1.call-start = ((), (), s32[]{:S(2)}) async-start(), calls=%async_computation.3 | async-start | bytes 163840 | tf_op jit(solution)/shard_map/reduce_scatter | solution.py:89
  57.4 0.8 copy-start.3
  59.0 0.7 copy-start.1
  59.7 1.3 copy-start.4
  61.8 16.1 %copy-start.6 = (bf16[32,2048]{1,0:T(8,128)(2,1)S(1)}, bf16[32,2048]{1,0:T(8,128)(2,1)}, u32[]{:S(2)}) copy-start(bf16[32,2048]{1,0:T(8,128)(2,1)} %param.14) | copy-start | bytes 393220
  70.4 7.5 %copy-start.7 = (f32[2048]{0:T(1024)S(1)}, f32[2048]{0:T(1024)}, u32[]{:S(2)}) copy-start(f32[2048]{0:T(1024)} %param.15) | copy-start | bytes 24580
Sparse Core Ops, SparseCore 0:
  56.7 21.1 reduce-scatter.2
  112.8 21.0 reduce-scatter.4
where the time goes:
time: 178 us; the launch traced here: 177 us
  blocking collectives  104 us (58%)
  waiting for transfers between devices  23.9 us (13%)
  between operations  19.6 us (11%)
  local copies, waits for them, and re-layouts  17.9 us (10%)
  matrix products  11.2 us (6%)
    psum x2, blocking collectives, local(): combined = lax.psum(own_sum * inv_root + prior_part, 'feat')  56.2 us
    psum x1, blocking collectives, local(): lax.psum(masked_rows(points, offsets, owned_mask).astype(jnp.bfloat16), '...  30.7 us
    reduce_scatter x2, waiting for transfers between devices, local(): lax.psum_scatter(kernel_block(everyone, points, local_sq, duals_bf), 'grp...  23.9 us
    all_gather x2, blocking collectives, local(): everyone = lax.all_gather(batch_local, 'grp', axis=0, tiled=True)  17.1 us
    dot_general x2, matrix products, local(): jnp.dot(features, prior_weights, preferred_element_type=jnp.float32)  9.1 us
    gather x6, local copies, waits for them, and re-layouts, local(): gradient = combined - observed[offsets][:, None] + noise_draws[offsets]  3.96 us
    unnamed x22, local copies, waits for them, and re-layouts  3.93 us
  transfers between devices with their start and end apart: 2, of which 2 were waited for; matrix products, arithmetic and copies ran while one was open for 5% of the time, Pallas kernels for 0%

commit v1 on v0

v1 whole, which is shorter than its diff:
```python
import functools
import math

import jax
import jax.numpy as jnp
import numpy as np
from jax import lax
from jax.experimental import pallas as pl
from jax.experimental.pallas import tpu as pltpu
from jax.sharding import PartitionSpec as P

TILE = 128
CHUNK = 256

amplitude = 4.0
signal = 2.0
momentum = 0.9
step_size = 0.5

f32 = jnp.float32
bf16 = jnp.bfloat16

def cos_terms():
    degree = 6
    nodes = np.cos(np.pi * (np.arange(64) + 0.5) / 64)
    top = math.pi * math.pi * 1.0001
    squares = (nodes + 1.0) * 0.5 * top
    fit = np.polynomial.chebyshev.Chebyshev.fit(
        squares, np.cos(np.sqrt(squares)), degree, domain=[0.0, top]
    )
    return [float(c) for c in fit.convert(kind=np.polynomial.Polynomial).coef]


COS = cos_terms()
TURN_HIGH = 6.28125
TURN_LOW = 2.0 * math.pi - TURN_HIGH


def cosine(angle):
    turns = jnp.round(angle * (0.5 / math.pi))
    rest = (angle - turns * TURN_HIGH) - turns * TURN_LOW
    square = rest * rest
    total = jnp.full_like(square, COS[-1])
    for term in COS[-2::-1]:
        total = total * square + term
    return total


def rows_of(batch_ref, step, depth):
    turned = batch_ref[depth * step : depth * (step + 1), :]
    return turned, turned.astype(f32).T


def across(left, right):
    return lax.dot_general(left, right, (((1,), (1,)), ((), ())), preferred_element_type=f32)


def kernel_sum(rows, blocks, depth):
    rows_bf = rows.astype(bf16)
    row_sq = jnp.sum(rows * rows, axis=1, keepdims=True)
    total = None
    for block_ref in blocks:
        values = block_ref.shape[0] - depth
        size = block_ref.shape[1]
        step = min(size, CHUNK)
        for start in range(0, size, step):
            cut = slice(start, start + step)
            points = block_ref[values:, cut]
            wide = points.astype(f32)
            norm = jnp.sum(wide * wide, axis=0, keepdims=True)
            inner = jnp.dot(rows_bf, points, preferred_element_type=f32)
            distance = row_sq + norm - 2.0 * inner
            kern = (amplitude * jnp.exp(distance * (-1.0 / depth))).astype(bf16)
            part = across(block_ref[:values, cut], kern)
            total = part if total is None else total + part
    return total


def prior_sum(rows, freq_ref, phase_ref, weight_ref):
    rows_bf = rows.astype(bf16)
    total = None
    for start in range(0, freq_ref.shape[1], CHUNK):
        cut = slice(start, start + CHUNK)
        angle = jnp.dot(rows_bf, freq_ref[:, cut], preferred_element_type=f32) + phase_ref[0:1, cut]
        part = across(weight_ref[:, cut], cosine(angle).astype(bf16))
        total = part if total is None else total + part
    return total


def place_of(tiles_ref, step, tiles_per):
    tile = tiles_ref[step]
    mine = lax.div(tile, tiles_per) == lax.axis_index("feat")
    return mine, pl.ds(pl.multiple_of(lax.rem(tile, tiles_per) * TILE, TILE), TILE)


def data_term(tiles_ref, step, observed_ref, noise_ref):
    mine, where = place_of(tiles_ref, step, noise_ref.shape[1] // TILE)
    return mine, where, step_size * (observed_ref[0:1, where] - noise_ref[:, where])


def pack_kernel(tiles_ref, points_ref, duals_ref, batch_ref, static_ref):
    depth, count = points_ref.shape
    values = duals_ref.shape[0]
    for step in range(2):
        mine, where = place_of(tiles_ref, step, count // TILE)
        rows = points_ref[:, where]
        batch_ref[depth * step : depth * (step + 1), :] = jnp.where(mine, rows, jnp.zeros_like(rows))
    static_ref[:values, :] = duals_ref[...].astype(bf16)
    static_ref[values:, :] = points_ref[...]


def first_kernel(scales, tiles_ref, batch_ref, freq_ref, phase_ref, weight_ref, observed_ref, noise_ref, velocity_ref, *rest):
    blocks, (share_ref, send_ref) = rest[:-2], rest[-2:]
    inv_root, prior_scale = scales
    depth = freq_ref.shape[0]
    turned, rows = rows_of(batch_ref, 0, depth)
    kernel_part = kernel_sum(rows, blocks, depth)
    prior_part = prior_sum(rows, freq_ref, phase_ref, weight_ref)
    mine, where, data = data_term(tiles_ref, 0, observed_ref, noise_ref)
    base = momentum * velocity_ref[:, where] + data
    share = jnp.where(mine, base, 0.0) - step_size * (kernel_part * inv_root + prior_part * prior_scale)
    share_ref[...] = share
    send_ref[: share.shape[0], :] = share.astype(bf16)
    send_ref[share.shape[0] :, :] = turned


def second_kernel(scales, tiles_ref, batch_ref, freq_ref, phase_ref, weight_ref, observed_ref, noise_ref, *rest):
    blocks, share_ref = rest[:-1], rest[-1]
    inv_root, prior_scale = scales
    depth = freq_ref.shape[0]
    _, rows = rows_of(batch_ref, 1, depth)
    kernel_part = kernel_sum(rows, blocks, depth)
    prior_part = prior_sum(rows, freq_ref, phase_ref, weight_ref)
    mine, _, data = data_term(tiles_ref, 1, observed_ref, noise_ref)
    share_ref[...] = jnp.where(mine, data, 0.0) - step_size * (kernel_part * inv_root + prior_part * prior_scale)


def correct_kernel(scales, depth, batch_ref, first_ref, second_ref, *rest):
    blocks, total_ref = rest[:-1], rest[-1]
    _, rows = rows_of(batch_ref, 1, depth)
    moved = kernel_sum(rows, blocks, depth)
    values = first_ref.shape[0]
    total_ref[:values, :] = first_ref[...]
    total_ref[values:, :] = second_ref[...] - (step_size * scales[0]) * moved


def finish_kernel(tiles_ref, mine_ref, other_ref, duals_ref, velocity_ref, new_duals_ref, new_velocity_ref):
    values, count = duals_ref.shape
    total = mine_ref[...] + other_ref[...]
    new_duals_ref[...] = duals_ref[...]
    new_velocity_ref[...] = velocity_ref[...]
    own, where = place_of(tiles_ref, 0, count // TILE)

    @pl.when(own)
    def _():
        moved = total[:values, :]
        new_velocity_ref[:, where] = moved
        new_duals_ref[:, where] = new_duals_ref[:, where] + moved

    own_later, later = place_of(tiles_ref, 1, count // TILE)

    @pl.when(own_later)
    def _():
        moved = momentum * new_velocity_ref[:, later] + total[values:, :]
        new_velocity_ref[:, later] = moved
        new_duals_ref[:, later] = new_duals_ref[:, later] + moved


def call(kernel, outs, *args, flops=0, name=None):
    specs = [pl.BlockSpec(memory_space=pltpu.SMEM if a.dtype == jnp.int32 else pltpu.VMEM) for a in args]
    out_shape = [jax.ShapeDtypeStruct(shape, dtype) for shape, dtype in outs]
    return pl.pallas_call(
        kernel,
        out_shape=out_shape,
        in_specs=specs,
        out_specs=[pl.BlockSpec(memory_space=pltpu.VMEM)] * len(outs),
        compiler_params=pltpu.CompilerParams(vmem_limit_bytes=24 * 1024 * 1024),
        cost_estimate=pl.CostEstimate(
            flops=flops, bytes_accessed=sum(a.size * a.dtype.itemsize for a in args), transcendentals=0
        ),
        name=name,
    )(*args)


def swap(array, axis, count, bit):
    return lax.ppermute(array, axis, [(i, i ^ bit) for i in range(count)])


def over_feat(array, count):
    bit = 1
    other = None
    while bit < count:
        if other is not None:
            array = array + other
        other = swap(array, "feat", count, bit)
        bit *= 2
    return array, other


def local(points, dual_weights, velocity, observed, noise_draws, frequencies, phases, prior_weights, batch_tiles):
    groups = lax.axis_size("grp")
    members = lax.axis_size("feat")
    count, depth = points.shape
    samples = dual_weights.shape[1]
    inv_root = 1.0 / math.sqrt(count * groups * members)
    prior_scale = signal * math.sqrt(2.0 / (frequencies.shape[1] * members))
    scales = (inv_root, prior_scale)
    tiles = batch_tiles.reshape(2)
    observed = observed.reshape(1, count)
    phases = phases.reshape(1, phases.shape[0])
    points, duals, velocity, noise, weights = (a.T for a in (points, dual_weights, velocity, noise_draws, prior_weights))

    batch, static = call(
        pack_kernel, [((2 * depth, TILE), bf16), ((samples + depth, count), bf16)], tiles, points, duals, name="pack"
    )
    fixed = [static] + [swap(static, "grp", groups, k) for k in range(1, groups)]
    mine, other = over_feat(batch, members)
    batch = mine + other

    share, send = call(
        functools.partial(first_kernel, scales), [((samples, TILE), f32), ((samples + depth, TILE), bf16)],
        tiles, batch, frequencies, phases, weights, observed, noise, velocity, *fixed,
        flops=10**9, name="first",
    )
    moves = [send] + [swap(send, "grp", groups, k) for k in range(1, groups)]
    (later,) = call(
        functools.partial(second_kernel, scales), [((samples, TILE), f32)],
        tiles, batch, frequencies, phases, weights, observed, noise, *fixed,
        flops=10**9, name="second",
    )
    (total,) = call(
        functools.partial(correct_kernel, scales, depth), [((2 * samples, TILE), f32)],
        batch, share, later, *moves, flops=10**8, name="correct",
    )
    mine, other = over_feat(total, members)
    new_duals, new_velocity = call(
        finish_kernel, [((samples, count), f32)] * 2, tiles, mine, other, duals, velocity, name="finish"
    )
    return new_duals.T, new_velocity.T


def solution(mesh):
    return jax.shard_map(
        local,
        mesh=mesh,
        in_specs=(
            P(("grp", "feat"), None),
            P(("grp", "feat"), None),
            P(("grp", "feat"), None),
            P(("grp", "feat")),
            P(("grp", "feat"), None),
            P(None, "feat"),
            P("feat"),
            P("feat", None),
            P(None, "grp", None),
        ),
        out_specs=(P(("grp", "feat"), None), P(("grp", "feat"), None)),
        check_vma=False,
    )
```

time: 178 us -> 41.4 us (0.23)
  blocking collectives: 104 us -> 0 us
  between operations: 19.6 us -> 0.79 us
  starting transfers between devices: 0.08 us -> 17.7 us
  local copies, waits for them, and re-layouts: 17.9 us -> 4.67 us
  waiting for transfers between devices: 23.9 us -> 11.7 us
  matrix products: 11.2 us -> 0 us
  Pallas kernels: 0 us -> 6.1 us
    psum x3 -> x0, blocking collectives: 86.9 us -> none  [the longest x2 56.2 us: local(): combined = lax.psum(own_sum * inv_root + prior_part, 'feat')]
    reduce_scatter x2 -> x0, waiting for transfers between devices: 23.9 us -> none  [local(): lax.psum_scatter(kernel_block(everyone, points, local_sq, duals_bf), 'grp...]
    ppermute x0 -> x12, starting transfers between devices: none -> 17.7 us  [swap(): return lax.ppermute(array, axis, [(i, i ^ bit) for i in range(count)])]
    all_gather x2 -> x0, blocking collectives: 17.1 us -> none  [local(): everyone = lax.all_gather(batch_local, 'grp', axis=0, tiled=True)]
    ppermute x0 -> x12, waiting for transfers between devices: none -> 11.7 us  [swap(): return lax.ppermute(array, axis, [(i, i ^ bit) for i in range(count)])]
    dot_general x4 -> x0, matrix products: 11.2 us -> none  [the longest x2 9.1 us: local(): jnp.dot(features, prior_weights, preferred_element_type=jnp.float32)]
    gather x16 -> x0, local copies, waits for them, and re-layouts: 8.22 us -> none  [the longest x6 3.96 us: local(): gradient = combined - observed[offsets][:, None] + noise_draws[offsets]]
    pallas_call x0 -> x5, Pallas kernels: none -> 6.1 us  [call(): pl.pallas_call(kernel, out_shape=out_shape, in_specs=specs, out_specs=[pl...]
  transfers between devices with their start and end apart: 2 -> 12, of which waited for: 2 -> 7; matrix products, arithmetic and copies ran while one was open for 5% -> 0% of each run, Pallas kernels for 0% -> 5%
where the time goes in v1:
time: 41.4 us; the launch traced here: 41 us
  starting transfers between devices  17.7 us (43%)
  waiting for transfers between devices  11.7 us (28%)
  Pallas kernels  6.1 us (15%)
  local copies, waits for them, and re-layouts  4.67 us (11%)
  between operations  0.79 us (2%)
    ppermute x12, starting transfers between devices, swap(): return lax.ppermute(array, axis, [(i, i ^ bit) for i in range(count)])  17.7 us
    ppermute x12, waiting for transfers between devices, swap(): return lax.ppermute(array, axis, [(i, i ^ bit) for i in range(count)])  11.7 us
    pallas_call x5, Pallas kernels, call(): pl.pallas_call(kernel, out_shape=out_shape, in_specs=specs, out_specs=[pl...  6.1 us
    unnamed x20, local copies, waits for them, and re-layouts  4.67 us
  transfers between devices with their start and end apart: 12, of which 7 were waited for; matrix products, arithmetic and copies ran while one was open for 0% of the time, Pallas kernels for 5%

profile of v1, /device:TPU:0, one launch (start us, length us, event | category | flops | bytes accessed | tf_op | source)
XLA Modules:
  0.0 41.0 jit_solution(1569680223463940834)
XLA Ops:
  0.6 0.0 copy-start.4
  0.6 0.6 %copy-done.4 = s32[2,1,1]{0,2,1:T(1,128)S(1)} copy-done((s32[2,1,1]{0,2,1:T(1,128)S(1)}, s32[2,1,1]{0,2,1:T(1,128)}, u32[]{:S(2)}) %copy-start.4) | copy-done | bytes 32
  1.3 0.0 copy-start
  1.3 0.8 %copy-done = f32[256,64]{0,1:T(8,128)S(1)} copy-done((f32[256,64]{0,1:T(8,128)S(1)}, f32[256,64]{0,1:T(8,128)}, u32[]{:S(2)}) %copy-start) | copy-done | bytes 65560
  2.1 0.0 copy-start.3
  2.1 0.7 %copy-done.3 = bf16[256,32]{0,1:T(8,128)(2,1)S(1)} copy-done((bf16[256,32]{0,1:T(8,128)(2,1)S(1)}, bf16[256,32]{0,1:T(8,128)(2,1)}, u32[]{:S(2)}) %copy-start.3) | copy-done | bytes 16408
  2.8 0.0 copy-start.6
  2.8 0.6 %pack.1 = (bf16[64,128]{1,0:T(8,128)(2,1)S(1)}, bf16[96,256]{1,0:T(8,128)(2,1)S(1)}) custom-call(s32[2]{0:T(128)S(1)} %bitcast.15, bf16[32,256]{1,0:T(8,128)(2,1)S(1)} %bitcast.14, f32[64,256]{1,0:T(8,128)S(1)} %bitcast.10), custom_call_target="tpu_custom_call" | custom-call | bytes 81928 | tf_op jit(solution)/shard_map/pack/pallas_call | solution.py:172
  3.4 0.5 %collective-permute-start = (bf16[64,128]{1,0:T(8,128)(2,1)S(1)}, bf16[64,128]{1,0:T(8,128)(2,1)S(1)}, u32[]{:S(2)}, u32[]{:S(2)}) collective-permute-start(bf16[64,128]{1,0:T(8,128)(2,1)S(1)} %get-tuple-element.8), channel_id=1, source_target_pairs={{0,1},{1,0},{2,3},{3,2},{4,5},{5,4},{6,7},{7,6},{8,9},{9,8},{10,11... | collective-permute-start | bytes 49160 | tf_op jit(solution)/shard_map/ppermute | solution.py:186
  3.9 3.5 %collective-permute-start.5 = (bf16[96,256]{1,0:T(8,128)(2,1)S(1)}, bf16[96,256]{1,0:T(8,128)(2,1)S(1)}, u32[]{:S(2)}, u32[]{:S(2)}) collective-permute-start(bf16[96,256]{1,0:T(8,128)(2,1)S(1)} %get-tuple-element.9.rest_0_), channel_id=1, source_target_pairs={{0,24},{8,16},{16,8},{24,0},{1,25},{9,17},{17,9},{25,1},{2,26},{10... | collective-permute-start | bytes 147464 | tf_op jit(solution)/shard_map/ppermute | solution.py:186
  7.5 0.5 %collective-permute-start.4 = (bf16[96,256]{1,0:T(8,128)(2,1)S(1)}, bf16[96,256]{1,0:T(8,128)(2,1)S(1)}, u32[]{:S(2)}, u32[]{:S(2)}) collective-permute-start(bf16[96,256]{1,0:T(8,128)(2,1)S(1)} %get-tuple-element.9.rest_0_), channel_id=1, source_target_pairs={{0,16},{8,24},{16,0},{24,8},{1,17},{9,25},{17,1},{25,9},{2,18},{10... | collective-permute-start | bytes 147464 | tf_op jit(solution)/shard_map/ppermute | solution.py:186
  8.0 0.1 collective-permute-start.3
  8.1 0.0 collective-permute-done
  8.1 0.0 copy-start.2
  8.1 2.0 %collective-permute-start.1 = (bf16[64,128]{1,0:T(8,128)(2,1)S(1)}, bf16[64,128]{1,0:T(8,128)(2,1)S(1)}, u32[]{:S(2)}, u32[]{:S(2)}) collective-permute-start(bf16[64,128]{1,0:T(8,128)(2,1)S(1)} %add.15), channel_id=1, source_target_pairs={{0,2},{1,3},{2,0},{3,1},{4,6},{5,7},{6,4},{7,5},{8,10},{9,11},{10,... | collective-permute-start | bytes 49160 | tf_op jit(solution)/shard_map/ppermute | solution.py:186
  10.2 1.8 %collective-permute-done.1 = bf16[64,128]{1,0:T(8,128)(2,1)S(1)} collective-permute-done((bf16[64,128]{1,0:T(8,128)(2,1)S(1)}, bf16[64,128]{1,0:T(8,128)(2,1)S(1)}, u32[]{:S(2)}, u32[]{:S(2)}) %collective-permute-start.1) | collective-permute-done | bytes 16416 | tf_op jit(solution)/shard_map/ppermute | solution.py:186
  11.9 3.1 %collective-permute-start.2 = (bf16[64,128]{1,0:T(8,128)(2,1)S(1)}, bf16[64,128]{1,0:T(8,128)(2,1)S(1)}, u32[]{:S(2)}, u32[]{:S(2)}) collective-permute-start(bf16[64,128]{1,0:T(8,128)(2,1)S(1)} %add.16), channel_id=1, source_target_pairs={{0,4},{1,5},{2,6},{3,7},{4,0},{5,1},{6,2},{7,3},{8,12},{9,13},{10,... | collective-permute-start | bytes 49160 | tf_op jit(solution)/shard_map/ppermute | solution.py:186
  15.0 1.7 %collective-permute-done.2 = bf16[64,128]{1,0:T(8,128)(2,1)S(1)} collective-permute-done((bf16[64,128]{1,0:T(8,128)(2,1)S(1)}, bf16[64,128]{1,0:T(8,128)(2,1)S(1)}, u32[]{:S(2)}, u32[]{:S(2)}) %collective-permute-start.2) | collective-permute-done | bytes 16416 | tf_op jit(solution)/shard_map/ppermute | solution.py:186
  16.7 0.0 copy-start.8
  16.7 0.0 collective-permute-done.5.rest_3_
  16.7 0.0 collective-permute-done.4.rest_2_
  16.8 0.0 collective-permute-done.3.rest_1_
  16.8 0.0 copy-start.9
  16.8 0.0 copy-done.6
  16.8 0.0 copy-done.2
  16.8 0.6 %copy-done.8 = f32[2048]{0:T(1024)S(1)} copy-done((f32[2048]{0:T(1024)S(1)}, f32[2048]{0:T(1024)}, u32[]{:S(2)}) %copy-start.8) | copy-done | bytes 8216
  17.4 0.0 copy-done.9
  17.5 0.0 copy-start.5
  17.5 0.9 %copy-done.5 = bf16[2048,64]{0,1:T(8,128)(2,1)S(1)} copy-done((bf16[2048,64]{0,1:T(8,128)(2,1)S(1)}, bf16[2048,64]{0,1:T(8,128)(2,1)}, u32[]{:S(2)}) %copy-start.5) | copy-done | bytes 262168
  18.4 0.8 %copy-done.7 = f32[256,64]{0,1:T(8,128)S(1)} copy-done((f32[256,64]{0,1:T(8,128)S(1)}, f32[256,64]{0,1:T(8,128)}, u32[]{:S(2)}) %copy-start.7) | copy-done | bytes 65560
  19.2 1.9 %first.1 = (f32[64,128]{1,0:T(8,128)S(1)}, bf16[96,128]{1,0:T(8,128)(2,1)S(1)}) custom-call(s32[2]{0:T(128)S(1)} %bitcast.16, bf16[64,128]{1,0:T(8,128)(2,1)S(1)} %add.17.batch_ref, bf16[32,2048]{1,0:T(8,128)(2,1)S(1)} %copy-done.6, f32[1,2048]{1,0:T(1,128)S(1)} %bitcast.23, bf16[64,2048]{1,0:T(8,128)(2,1)S(1)} %bitcast.19, f32[1,256]{1,0:T(1,128)S(1)} %bitcast.25, ...), custom_call_target="tpu_custom_call" | custom-call | flops 1000000000 | bytes 746504 | tf_op jit(solution)/shard_map/first/pallas_call | solution.py:172
  21.1 2.8 %collective-permute-start.8 = (bf16[96,128]{1,0:T(8,128)(2,1)S(1)}, bf16[96,128]{1,0:T(8,128)(2,1)S(1)}, u32[]{:S(2)}, u32[]{:S(2)}) collective-permute-start(bf16[96,128]{1,0:T(8,128)(2,1)S(1)} %get-tuple-element.11.rest_0_), channel_id=1, source_target_pairs={{0,24},{8,16},{16,8},{24,0},{1,25},{9,17},{17,9},{25,1},{2,26},{10... | collective-permute-start | bytes 73736 | tf_op jit(solution)/shard_map/ppermute | solution.py:186
  24.0 0.5 %collective-permute-start.7 = (bf16[96,128]{1,0:T(8,128)(2,1)S(1)}, bf16[96,128]{1,0:T(8,128)(2,1)S(1)}, u32[]{:S(2)}, u32[]{:S(2)}) collective-permute-start(bf16[96,128]{1,0:T(8,128)(2,1)S(1)} %get-tuple-element.11.rest_0_), channel_id=1, source_target_pairs={{0,16},{8,24},{16,0},{24,8},{1,17},{9,25},{17,1},{25,9},{2,18},{10... | collective-permute-start | bytes 73736 | tf_op jit(solution)/shard_map/ppermute | solution.py:186
  24.5 0.2 collective-permute-start.6
  24.7 1.9 %second.1.second_ref = f32[64,128]{1,0:T(8,128)S(1)} custom-call(s32[2]{0:T(128)S(1)} %bitcast.17, bf16[64,128]{1,0:T(8,128)(2,1)S(1)} %add.17.batch_ref, bf16[32,2048]{1,0:T(8,128)(2,1)S(1)} %copy-done.6, f32[1,2048]{1,0:T(1,128)S(1)} %bitcast.24, bf16[64,2048]{1,0:T(8,128)(2,1)S(1)} %bitcast.20, f32[1,256]{1,0:T(1,128)S(1)} %bitcast.26, ...), custom_call_target="tpu_custom_call" | custom-call | flops 1000000000 | bytes 680968 | tf_op jit(solution)/shard_map/second/pallas_call | solution.py:172
  26.6 0.0 collective-permute-done.8.rest_3_
  26.6 1.2 %collective-permute-done.7.rest_2_ = bf16[96,128]{1,0:T(8,128)(2,1)S(1)} collective-permute-done((bf16[96,128]{1,0:T(8,128)(2,1)S(1)}, bf16[96,128]{1,0:T(8,128)(2,1)S(1)}, u32[]{:S(2)}, u32[]{:S(2)}) %collective-permute-start.7) | collective-permute-done | bytes 24608 | tf_op jit(solution)/shard_map/ppermute | solution.py:186
  27.8 0.5 %collective-permute-done.6.rest_1_ = bf16[96,128]{1,0:T(8,128)(2,1)S(1)} collective-permute-done((bf16[96,128]{1,0:T(8,128)(2,1)S(1)}, bf16[96,128]{1,0:T(8,128)(2,1)S(1)}, u32[]{:S(2)}, u32[]{:S(2)}) %collective-permute-start.6) | collective-permute-done | bytes 24608 | tf_op jit(solution)/shard_map/ppermute | solution.py:186
  28.3 0.6 %correct.1 = f32[128,128]{1,0:T(8,128)S(1)} custom-call(bf16[64,128]{1,0:T(8,128)(2,1)S(1)} %add.17.batch_ref, f32[64,128]{1,0:T(8,128)S(1)} %get-tuple-element.10.first_ref, f32[64,128]{1,0:T(8,128)S(1)} %second.1.second_ref, bf16[96,128]{1,0:T(8,128)(2,1)S(1)} %get-tuple-element.11.rest_0_, bf16[96,128]{1,0:T(8,128)(2,1)S(1)} %collective-permute-done.6.rest_1_, ...), custom_call_target="tpu_custom_call" | custom-call | flops 100000000 | bytes 180224 | tf_op jit(solution)/shard_map/correct/pallas_call | solution.py:172
  28.9 0.1 collective-permute-start.9
  29.0 1.2 %collective-permute-done.9 = f32[128,128]{1,0:T(8,128)S(1)} collective-permute-done((f32[128,128]{1,0:T(8,128)S(1)}, f32[128,128]{1,0:T(8,128)S(1)}, u32[]{:S(2)}, u32[]{:S(2)}) %collective-permute-start.9) | collective-permute-done | bytes 65568 | tf_op jit(solution)/shard_map/ppermute | solution.py:186
  30.2 0.0 copy-start.1
  30.2 1.6 %collective-permute-start.10 = (f32[128,128]{1,0:T(8,128)S(1)}, f32[128,128]{1,0:T(8,128)S(1)}, u32[]{:S(2)}, u32[]{:S(2)}) collective-permute-start(f32[128,128]{1,0:T(8,128)S(1)} %add.18), channel_id=1, source_target_pairs={{0,2},{1,3},{2,0},{3,1},{4,6},{5,7},{6,4},{7,5},{8,10},{9,11},{10,... | collective-permute-start | bytes 196616 | tf_op jit(solution)/shard_map/ppermute | solution.py:186
  31.9 2.7 %collective-permute-done.10 = f32[128,128]{1,0:T(8,128)S(1)} collective-permute-done((f32[128,128]{1,0:T(8,128)S(1)}, f32[128,128]{1,0:T(8,128)S(1)}, u32[]{:S(2)}, u32[]{:S(2)}) %collective-permute-start.10) | collective-permute-done | bytes 65568 | tf_op jit(solution)/shard_map/ppermute | solution.py:186
  34.6 2.7 %collective-permute-start.11 = (f32[128,128]{1,0:T(8,128)S(1)}, f32[128,128]{1,0:T(8,128)S(1)}, u32[]{:S(2)}, u32[]{:S(2)}) collective-permute-start(f32[128,128]{1,0:T(8,128)S(1)} %add.19.mine_ref), channel_id=1, source_target_pairs={{0,4},{1,5},{2,6},{3,7},{4,0},{5,1},{6,2},{7,3},{8,12},{9,13},{10,... | collective-permute-start | bytes 196616 | tf_op jit(solution)/shard_map/ppermute | solution.py:186
  37.2 2.6 %collective-permute-done.11.other_ref = f32[128,128]{1,0:T(8,128)S(1)} collective-permute-done((f32[128,128]{1,0:T(8,128)S(1)}, f32[128,128]{1,0:T(8,128)S(1)}, u32[]{:S(2)}, u32[]{:S(2)}) %collective-permute-start.11) | collective-permute-done | bytes 65568 | tf_op jit(solution)/shard_map/ppermute | solution.py:186
  39.8 0.0 copy-done.1
  39.8 1.2 %finish.1 = (f32[64,256]{1,0:T(8,128)}, f32[64,256]{1,0:T(8,128)}) custom-call(s32[2]{0:T(128)S(1)} %bitcast.18, f32[128,128]{1,0:T(8,128)S(1)} %add.19.mine_ref, f32[128,128]{1,0:T(8,128)S(1)} %collective-permute-done.11.other_ref, f32[64,256]{1,0:T(8,128)S(1)} %bitcast.11, f32[64,256]{1,0:T(8,128)S(1)} %bitcast.13), custom_call_target="tpu_custom_call" | custom-call | bytes 262152 | tf_op jit(solution)/shard_map/finish/pallas_call | solution.py:172
  (6 shorter events, 0.0 us)
Async XLA Ops:
  0.6 0.7 %copy-start.4 = (s32[2,1,1]{0,2,1:T(1,128)S(1)}, s32[2,1,1]{0,2,1:T(1,128)}, u32[]{:S(2)}) copy-start(s32[2,1,1]{0,2,1:T(1,128)} %param.17) | copy-start | bytes 28
  1.3 0.8 %copy-start = (f32[256,64]{0,1:T(8,128)S(1)}, f32[256,64]{0,1:T(8,128)}, u32[]{:S(2)}) copy-start(f32[256,64]{0,1:T(8,128)} %param.10) | copy-start | bytes 196612
  2.1 0.7 %copy-start.3 = (bf16[256,32]{0,1:T(8,128)(2,1)S(1)}, bf16[256,32]{0,1:T(8,128)(2,1)}, u32[]{:S(2)}) copy-start(bf16[256,32]{0,1:T(8,128)(2,1)} %param.9) | copy-start | bytes 49156
  2.8 13.9 %copy-start.6 = (bf16[32,2048]{1,0:T(8,128)(2,1)S(1)}, bf16[32,2048]{1,0:T(8,128)(2,1)}, u32[]{:S(2)}) copy-start(bf16[32,2048]{1,0:T(8,128)(2,1)} %freq_ref.3) | copy-start | bytes 393220
  3.4 4.7 %collective-permute-start = (bf16[64,128]{1,0:T(8,128)(2,1)S(1)}, bf16[64,128]{1,0:T(8,128)(2,1)S(1)}, u32[]{:S(2)}, u32[]{:S(2)}) collective-permute-start(bf16[64,128]{1,0:T(8,128)(2,1)S(1)} %get-tuple-element.8), channel_id=1, source_target_pairs={{0,1},{1,0},{2,3},{3,2},{4,5},{5,4},{6,7},{7,6},{8,9},{9,8},{10,11... | collective-permute-start | bytes 49160 | tf_op jit(solution)/shard_map/ppermute | solution.py:186
  3.9 12.8 %collective-permute-start.5 = (bf16[96,256]{1,0:T(8,128)(2,1)S(1)}, bf16[96,256]{1,0:T(8,128)(2,1)S(1)}, u32[]{:S(2)}, u32[]{:S(2)}) collective-permute-start(bf16[96,256]{1,0:T(8,128)(2,1)S(1)} %get-tuple-element.9.rest_0_), channel_id=1, source_target_pairs={{0,24},{8,16},{16,8},{24,0},{1,25},{9,17},{17,9},{25,1},{2,26},{10... | collective-permute-start | bytes 147464 | tf_op jit(solution)/shard_map/ppermute | solution.py:186
  7.5 9.3 %collective-permute-start.4 = (bf16[96,256]{1,0:T(8,128)(2,1)S(1)}, bf16[96,256]{1,0:T(8,128)(2,1)S(1)}, u32[]{:S(2)}, u32[]{:S(2)}) collective-permute-start(bf16[96,256]{1,0:T(8,128)(2,1)S(1)} %get-tuple-element.9.rest_0_), channel_id=1, source_target_pairs={{0,16},{8,24},{16,0},{24,8},{1,17},{9,25},{17,1},{25,9},{2,18},{10... | collective-permute-start | bytes 147464 | tf_op jit(solution)/shard_map/ppermute | solution.py:186
  8.0 8.8 %collective-permute-start.3 = (bf16[96,256]{1,0:T(8,128)(2,1)S(1)}, bf16[96,256]{1,0:T(8,128)(2,1)S(1)}, u32[]{:S(2)}, u32[]{:S(2)}) collective-permute-start(bf16[96,256]{1,0:T(8,128)(2,1)S(1)} %get-tuple-element.9.rest_0_), channel_id=1, source_target_pairs={{0,8},{8,0},{16,24},{24,16},{1,9},{9,1},{17,25},{25,17},{2,10},{10... | collective-permute-start | bytes 147464 | tf_op jit(solution)/shard_map/ppermute | solution.py:186
  8.1 8.7 %copy-start.2 = (f32[256,64]{0,1:T(8,128)S(1)}, f32[256,64]{0,1:T(8,128)}, u32[]{:S(2)}) copy-start(f32[256,64]{0,1:T(8,128)} %param.11) | copy-start | bytes 196612
  8.1 3.8 %collective-permute-start.1 = (bf16[64,128]{1,0:T(8,128)(2,1)S(1)}, bf16[64,128]{1,0:T(8,128)(2,1)S(1)}, u32[]{:S(2)}, u32[]{:S(2)}) collective-permute-start(bf16[64,128]{1,0:T(8,128)(2,1)S(1)} %add.15), channel_id=1, source_target_pairs={{0,2},{1,3},{2,0},{3,1},{4,6},{5,7},{6,4},{7,5},{8,10},{9,11},{10,... | collective-permute-start | bytes 49160 | tf_op jit(solution)/shard_map/ppermute | solution.py:186
  11.9 4.8 %collective-permute-start.2 = (bf16[64,128]{1,0:T(8,128)(2,1)S(1)}, bf16[64,128]{1,0:T(8,128)(2,1)S(1)}, u32[]{:S(2)}, u32[]{:S(2)}) collective-permute-start(bf16[64,128]{1,0:T(8,128)(2,1)S(1)} %add.16), channel_id=1, source_target_pairs={{0,4},{1,5},{2,6},{3,7},{4,0},{5,1},{6,2},{7,3},{8,12},{9,13},{10,... | collective-permute-start | bytes 49160 | tf_op jit(solution)/shard_map/ppermute | solution.py:186
  16.7 0.7 %copy-start.8 = (f32[2048]{0:T(1024)S(1)}, f32[2048]{0:T(1024)}, u32[]{:S(2)}) copy-start(f32[2048]{0:T(1024)} %param.15) | copy-start | bytes 24580
  16.8 0.7 %copy-start.9 = (f32[256]{0:T(256)S(1)}, f32[256]{0:T(256)}, u32[]{:S(2)}) copy-start(f32[256]{0:T(256)} %param.12) | copy-start | bytes 3076
  17.5 0.9 %copy-start.5 = (bf16[2048,64]{0,1:T(8,128)(2,1)S(1)}, bf16[2048,64]{0,1:T(8,128)(2,1)}, u32[]{:S(2)}) copy-start(bf16[2048,64]{0,1:T(8,128)(2,1)} %param.16) | copy-start | bytes 786436
  18.4 0.8 %copy-start.7 = (f32[256,64]{0,1:T(8,128)S(1)}, f32[256,64]{0,1:T(8,128)}, u32[]{:S(2)}) copy-start(f32[256,64]{0,1:T(8,128)} %param.13) | copy-start | bytes 196612
  21.1 5.4 %collective-permute-start.8 = (bf16[96,128]{1,0:T(8,128)(2,1)S(1)}, bf16[96,128]{1,0:T(8,128)(2,1)S(1)}, u32[]{:S(2)}, u32[]{:S(2)}) collective-permute-start(bf16[96,128]{1,0:T(8,128)(2,1)S(1)} %get-tuple-element.11.rest_0_), channel_id=1, source_target_pairs={{0,24},{8,16},{16,8},{24,0},{1,25},{9,17},{17,9},{25,1},{2,26},{10... | collective-permute-start | bytes 73736 | tf_op jit(solution)/shard_map/ppermute | solution.py:186
  24.0 3.8 %collective-permute-start.7 = (bf16[96,128]{1,0:T(8,128)(2,1)S(1)}, bf16[96,128]{1,0:T(8,128)(2,1)S(1)}, u32[]{:S(2)}, u32[]{:S(2)}) collective-permute-start(bf16[96,128]{1,0:T(8,128)(2,1)S(1)} %get-tuple-element.11.rest_0_), channel_id=1, source_target_pairs={{0,16},{8,24},{16,0},{24,8},{1,17},{9,25},{17,1},{25,9},{2,18},{10... | collective-permute-start | bytes 73736 | tf_op jit(solution)/shard_map/ppermute | solution.py:186
  24.5 3.8 %collective-permute-start.6 = (bf16[96,128]{1,0:T(8,128)(2,1)S(1)}, bf16[96,128]{1,0:T(8,128)(2,1)S(1)}, u32[]{:S(2)}, u32[]{:S(2)}) collective-permute-start(bf16[96,128]{1,0:T(8,128)(2,1)S(1)} %get-tuple-element.11.rest_0_), channel_id=1, source_target_pairs={{0,8},{8,0},{16,24},{24,16},{1,9},{9,1},{17,25},{25,17},{2,10},{10... | collective-permute-start | bytes 73736 | tf_op jit(solution)/shard_map/ppermute | solution.py:186
  28.9 1.3 %collective-permute-start.9 = (f32[128,128]{1,0:T(8,128)S(1)}, f32[128,128]{1,0:T(8,128)S(1)}, u32[]{:S(2)}, u32[]{:S(2)}) collective-permute-start(f32[128,128]{1,0:T(8,128)S(1)} %correct.1), channel_id=1, source_target_pairs={{0,1},{1,0},{2,3},{3,2},{4,5},{5,4},{6,7},{7,6},{8,9},{9,8},{10,11... | collective-permute-start | bytes 196616 | tf_op jit(solution)/shard_map/ppermute | solution.py:186
  30.2 9.6 %copy-start.1 = (f32[256,64]{0,1:T(8,128)S(1)}, f32[256,64]{0,1:T(8,128)}, u32[]{:S(2)}) copy-start(f32[256,64]{0,1:T(8,128)} %param.10) | copy-start | bytes 196612
  30.2 4.3 %collective-permute-start.10 = (f32[128,128]{1,0:T(8,128)S(1)}, f32[128,128]{1,0:T(8,128)S(1)}, u32[]{:S(2)}, u32[]{:S(2)}) collective-permute-start(f32[128,128]{1,0:T(8,128)S(1)} %add.18), channel_id=1, source_target_pairs={{0,2},{1,3},{2,0},{3,1},{4,6},{5,7},{6,4},{7,5},{8,10},{9,11},{10,... | collective-permute-start | bytes 196616 | tf_op jit(solution)/shard_map/ppermute | solution.py:186
  34.6 5.2 %collective-permute-start.11 = (f32[128,128]{1,0:T(8,128)S(1)}, f32[128,128]{1,0:T(8,128)S(1)}, u32[]{:S(2)}, u32[]{:S(2)}) collective-permute-start(f32[128,128]{1,0:T(8,128)S(1)} %add.19.mine_ref), channel_id=1, source_target_pairs={{0,4},{1,5},{2,6},{3,7},{4,0},{5,1},{6,2},{7,3},{8,12},{9,13},{10,... | collective-permute-start | bytes 196616 | tf_op jit(solution)/shard_map/ppermute | solution.py:186

commit v2 on v1

v2 whole, which is shorter than its diff:
```python
import functools
import math

import jax
import jax.numpy as jnp
import numpy as np
from jax import lax
from jax.experimental import pallas as pl
from jax.experimental.pallas import tpu as pltpu
from jax.sharding import PartitionSpec as P

TILE = 128
CHUNK = 256

amplitude = 4.0
signal = 2.0
momentum = 0.9
step_size = 0.5

f32 = jnp.float32
bf16 = jnp.bfloat16

SHRINK = 0.25

def cos_terms():
    nodes = np.cos(np.pi * (np.arange(64) + 0.5) / 64)
    squares = (nodes + 1.0) * 0.125
    fit = np.polynomial.chebyshev.Chebyshev.fit(
        squares, np.cos(2.0 * np.pi * np.sqrt(squares)), 6, domain=[0.0, 0.25]
    )
    return [float(c) for c in fit.convert(kind=np.polynomial.Polynomial).coef]


COS = cos_terms()
ANGLE_ROWS = 128


def cosine(turns):
    rest = turns - jnp.round(turns)
    square = rest * rest
    total = COS[-1] * square + COS[-2]
    for term in COS[-3::-1]:
        total = total * square + term
    return total


def three_parts(wide):
    high = wide.astype(bf16)
    rest = wide - high.astype(f32)
    middle = rest.astype(bf16)
    return high, middle, (rest - middle.astype(f32)).astype(bf16)


def rows_of(turned):
    wide = turned.astype(f32)
    depth, tile = wide.shape
    ids = lax.broadcasted_iota(jnp.int32, (ANGLE_ROWS - 3 * depth, tile), 0)
    upright = jnp.concatenate([wide, wide, wide, jnp.where(ids < 3, 1.0, 0.0)], axis=0).T
    return upright.astype(bf16), upright[:, :depth]


def across(left, right):
    return lax.dot_general(left, right, (((1,), (1,)), ((), ())), preferred_element_type=f32)


def kernel_sum(rows, blocks, depth):
    rows_bf = rows.astype(bf16)
    scale = -math.log2(math.e) / depth
    row_part = jnp.sum(rows * rows, axis=1, keepdims=True) * scale + math.log2(amplitude)
    total = None
    for block_ref in blocks:
        values = block_ref.shape[0] - depth
        size = block_ref.shape[1]
        step = min(size, CHUNK)
        for start in range(0, size, step):
            cut = slice(start, start + step)
            points = block_ref[values:, cut]
            wide = points.astype(f32)
            norm_part = jnp.sum(wide * wide, axis=0, keepdims=True) * scale
            inner = jnp.dot(rows_bf, points, preferred_element_type=f32)
            kern = jnp.exp2(inner * (-2.0 * scale) + (row_part + norm_part)).astype(bf16)
            part = across(block_ref[:values, cut], kern)
            total = part if total is None else total + part
    return total


def prior_sum(upright, angle_ref, weight_ref):
    total = None
    for start in range(0, angle_ref.shape[1], CHUNK):
        cut = slice(start, start + CHUNK)
        turns = jnp.dot(upright, angle_ref[:, cut], preferred_element_type=f32)
        part = across(weight_ref[:, cut], cosine(turns).astype(bf16))
        total = part if total is None else total + part
    return total


def place_of(tiles_ref, step, tiles_per):
    tile = tiles_ref[step]
    mine = lax.div(tile, tiles_per) == lax.axis_index("feat")
    return mine, pl.ds(pl.multiple_of(lax.rem(tile, tiles_per) * TILE, TILE), TILE)


def fetch(pairs, sems):
    copies = [pltpu.make_async_copy(src, dst, sems.at[k]) for k, (src, dst) in enumerate(pairs)]
    for copy in copies:
        copy.start()
    for copy in copies:
        copy.wait()


def pack_kernel(tiles_hbm, points_hbm, duals_hbm, batch_ref, static_ref, tiles_ref, points_ref, duals_ref, sems):
    fetch([(tiles_hbm, tiles_ref), (points_hbm, points_ref), (duals_hbm, duals_ref)], sems)
    depth, count = points_ref.shape
    values = duals_ref.shape[0]
    for step in range(2):
        mine, where = place_of(tiles_ref, step, count // TILE)
        rows = points_ref[:, where]
        batch_ref[depth * step : depth * (step + 1), :] = jnp.where(mine, rows, jnp.zeros_like(rows))
    static_ref[:values, :] = duals_ref[...].astype(bf16)
    static_ref[values:, :] = points_ref[...]


def prepare_kernel(
    tiles_hbm, freq_hbm, phase_hbm, weight_hbm, observed_hbm, noise_hbm, velocity_hbm, duals_hbm,
    angle_ref, weight_ref, base_ref, later_ref, marks_ref, velocity_ref, duals_ref,
    tiles_ref, freq_ref, phase_ref, observed_ref, noise_ref, sems,
):
    fetch(
        [
            (freq_hbm, freq_ref), (phase_hbm, phase_ref), (weight_hbm, weight_ref), (tiles_hbm, tiles_ref),
            (observed_hbm, observed_ref), (noise_hbm, noise_ref), (velocity_hbm, velocity_ref), (duals_hbm, duals_ref),
        ],
        sems,
    )
    depth, count = freq_ref.shape
    a_turn = 0.5 / math.pi
    for k, part in enumerate(three_parts(freq_ref[...].astype(f32) * a_turn)):
        angle_ref[depth * k : depth * (k + 1), :] = part
    pad = ANGLE_ROWS - 3 * depth
    ids = lax.broadcasted_iota(jnp.int32, (pad, count), 0)
    tail = jnp.zeros((pad, count), f32)
    for k, part in enumerate(three_parts(phase_ref[...] * a_turn)):
        tail = jnp.where(ids == k, part.astype(f32), tail)
    angle_ref[3 * depth :, :] = tail.astype(bf16)

    count = velocity_ref.shape[1]
    columns = lax.broadcasted_iota(jnp.int32, (8, count), 1)
    for step, share_ref in enumerate((base_ref, later_ref)):
        mine, where = place_of(tiles_ref, step, count // TILE)
        share = step_size * (observed_ref[0:1, where] - noise_ref[:, where])
        if step == 0:
            share = share + momentum * velocity_ref[:, where]
        share_ref[...] = jnp.where(mine, share, 0.0)
        inside = (columns >= where.start) & (columns < where.start + TILE)
        marks_ref[8 * step : 8 * (step + 1), :] = jnp.where(mine & inside, 1.0, 0.0)


def share_of(scales, upright, rows, angle_ref, weight_ref, base_ref, blocks):
    inv_root, prior_scale = scales
    kernel_part = kernel_sum(rows, blocks, rows.shape[1])
    prior_part = prior_sum(upright, angle_ref, weight_ref)
    return base_ref[...] - (step_size * inv_root) * kernel_part - (step_size * prior_scale) * prior_part


def first_kernel(scales, parts, angle_ref, weight_ref, base_ref, *rest):
    terms, blocks, (share_ref, send_ref, batch_ref) = rest[:parts], rest[parts:-3], rest[-3:]
    batch = terms[0][...]
    for term_ref in terms[1:]:
        batch = batch + term_ref[...]
    batch_ref[...] = batch
    depth = batch.shape[0] // 2
    upright, rows = rows_of(batch[:depth])
    share = share_of(scales, upright, rows, angle_ref, weight_ref, base_ref, blocks)
    share_ref[...] = share
    send_ref[: share.shape[0], :] = share.astype(bf16)
    send_ref[share.shape[0] :, :] = batch[:depth]


def second_kernel(scales, angle_ref, weight_ref, later_ref, batch_ref, *rest):
    blocks, share_ref = rest[:-1], rest[-1]
    upright, rows = rows_of(batch_ref[batch_ref.shape[0] // 2 :, :])
    share_ref[...] = share_of(scales, upright, rows, angle_ref, weight_ref, later_ref, blocks)


def correct_kernel(scales, batch_ref, first_ref, second_ref, *rest):
    blocks, total_ref = rest[:-1], rest[-1]
    _, rows = rows_of(batch_ref[batch_ref.shape[0] // 2 :, :])
    moved = kernel_sum(rows, blocks, rows.shape[1])
    values = first_ref.shape[0]
    total_ref[:values, :] = first_ref[...]
    total_ref[values:, :] = second_ref[...] - (step_size * scales[0]) * moved


def finish_kernel(marks_ref, total_ref, duals_ref, velocity_ref, new_duals_ref, new_velocity_ref):
    values, count = duals_ref.shape
    repeats = count // TILE
    total = jnp.concatenate([total_ref[...]] * repeats, axis=1)
    first, second = marks_ref[0:1, :] > 0.0, marks_ref[8:9, :] > 0.0
    velocity, duals = velocity_ref[...], duals_ref[...]
    moved = total[:values, :]
    velocity = jnp.where(first, moved, velocity)
    duals = jnp.where(first, duals + moved, duals)
    moved = momentum * velocity + total[values:, :]
    new_velocity_ref[...] = jnp.where(second, moved, velocity)
    new_duals_ref[...] = jnp.where(second, duals + moved, duals)


def call(kernel, outs, *args, flops=0, name=None, from_hbm=False):
    small, large = pltpu.SMEM, pltpu.VMEM
    scratch = []
    if from_hbm:
        small = large = pltpu.HBM
        args = [pltpu.with_memory_space_constraint(a, pltpu.HBM) for a in args]
        scratch = [
            (pltpu.SMEM if a.dtype == jnp.int32 else pltpu.VMEM)(a.shape, a.dtype) for k, a in enumerate(args) if k not in from_hbm
        ] + [pltpu.SemaphoreType.DMA((len(args),))]
    return pl.pallas_call(
        kernel,
        out_shape=[jax.ShapeDtypeStruct(shape, dtype) for shape, dtype in outs],
        in_specs=[pl.BlockSpec(memory_space=small if a.dtype == jnp.int32 else large) for a in args],
        out_specs=[pl.BlockSpec(memory_space=pltpu.VMEM)] * len(outs),
        scratch_shapes=scratch,
        compiler_params=pltpu.CompilerParams(vmem_limit_bytes=24 * 1024 * 1024),
        cost_estimate=pl.CostEstimate(
            flops=flops, bytes_accessed=sum(a.size * a.dtype.itemsize for a in args), transcendentals=0
        ),
        name=name,
    )(*args)


def swap(array, groups, members, group_bits, member_bits):
    pairs = [
        (g * members + m, (g ^ group_bits) * members + (m ^ member_bits)) for g in range(groups) for m in range(members)
    ]
    return lax.ppermute(array, ("grp", "feat"), pairs)


def local(points, dual_weights, velocity, observed, noise_draws, frequencies, phases, prior_weights, batch_tiles):
    groups = lax.axis_size("grp")
    members = lax.axis_size("feat")
    count, depth = points.shape
    samples = dual_weights.shape[1]
    features = frequencies.shape[1]
    scales = (1.0 / math.sqrt(count * groups * members), signal * math.sqrt(2.0 / (features * members)))
    tiles = batch_tiles.reshape(2)
    observed = observed.reshape(1, count)
    phases = phases.reshape(1, features)
    points, duals, velocity, noise, weights = (a.T for a in (points, dual_weights, velocity, noise_draws, prior_weights))
    part = (samples, TILE)

    def other_core(array):
        return swap(array, groups, members, 0, 1)

    def other_chips(array):
        return [swap(array, groups, members, 0, 2 * k + 1) for k in range(1, members // 2)]

    def other_groups(array):
        return [swap(array, groups, members, k, 1) for k in range(1, groups)]

    batch, static = call(
        pack_kernel, [((2 * depth, TILE), bf16), ((samples + depth, count), bf16)], tiles, points, duals,
        name="pack", from_hbm=(-1,),
    )
    fixed = [static] + other_groups(static)
    batch = batch + other_core(batch)
    batch = [batch] + other_chips(batch)
    whole = (samples, count)
    angles, weights, base, later, marks, velocity, duals = call(
        prepare_kernel,
        [((ANGLE_ROWS, features), bf16), ((samples, features), bf16), (part, f32), (part, f32),
         ((16, count), f32), (whole, f32), (whole, f32)],
        tiles, frequencies, phases, weights, observed, noise, velocity, duals,
        name="prepare", from_hbm=(3, 6, 7), flops=10**8,
    )
    share, send, batch = call(
        functools.partial(first_kernel, scales, len(batch)),
        [(part, f32), ((samples + depth, TILE), bf16), ((2 * depth, TILE), bf16)],
        angles, weights, base, *batch, *fixed,
        flops=10**9, name="first",
    )
    moves = [send] + other_groups(send)
    (later,) = call(
        functools.partial(second_kernel, scales), [(part, f32)], angles, weights, later, batch, *fixed,
        flops=10**9, name="second",
    )
    (total,) = call(
        functools.partial(correct_kernel, scales), [((2 * samples, TILE), f32)],
        batch, share, later, *moves, flops=10**8, name="correct",
    )
    total = total + other_core(total)
    for term in other_chips((total * SHRINK).astype(jnp.float16)):
        total = total + term.astype(f32) * (1.0 / SHRINK)
    new_duals, new_velocity = call(
        finish_kernel, [(whole, f32)] * 2, marks, total, duals, velocity, name="finish"
    )
    return new_duals.T, new_velocity.T


def solution(mesh):
    return jax.shard_map(
        local,
        mesh=mesh,
        in_specs=(
            P(("grp", "feat"), None),
            P(("grp", "feat"), None),
            P(("grp", "feat"), None),
            P(("grp", "feat")),
            P(("grp", "feat"), None),
            P(None, "feat"),
            P("feat"),
            P("feat", None),
            P(None, "grp", None),
        ),
        out_specs=(P(("grp", "feat"), None), P(("grp", "feat"), None)),
        check_vma=False,
    )
```

time: 41.4 us -> 32.2 us (0.78)
  local copies, waits for them, and re-layouts: 4.67 us -> 0 us
  starting transfers between devices: 17.7 us -> 15.8 us
  waiting for transfers between devices: 11.7 us -> 9.82 us
    unnamed x20 -> x0, local copies, waits for them, and re-layouts: 4.67 us -> none
    ppermute x12 -> x14, starting transfers between devices: 17.7 us -> 15.8 us  [swap(): return lax.ppermute(array, ('grp', 'feat'), pairs)]
    ppermute x12 -> x14, waiting for transfers between devices: 11.7 us -> 9.82 us  [swap(): return lax.ppermute(array, ('grp', 'feat'), pairs)]
    pallas_call x5 -> x6, Pallas kernels: 6.1 us -> 5.7 us  [call(): pl.pallas_call(kernel, out_shape=[jax.ShapeDtypeStruct(shape, dtype) for...]
  transfers between devices with their start and end apart: 12 -> 14, of which waited for: 7 -> 8; matrix products, arithmetic and copies ran while one was open for 0% -> 0% of each run, Pallas kernels for 5% -> 8%
where the time goes in v2:
time: 32.2 us; the launch traced here: 32 us
  starting transfers between devices  15.8 us (49%)
  waiting for transfers between devices  9.82 us (30%)
  Pallas kernels  5.7 us (18%)
  between operations  0.7 us (2%)
    ppermute x14, starting transfers between devices, swap(): return lax.ppermute(array, ('grp', 'feat'), pairs)  15.8 us
    ppermute x14, waiting for transfers between devices, swap(): return lax.ppermute(array, ('grp', 'feat'), pairs)  9.82 us
    pallas_call x6, Pallas kernels, call(): pl.pallas_call(kernel, out_shape=[jax.ShapeDtypeStruct(shape, dtype) for...  5.7 us
  transfers between devices with their start and end apart: 14, of which 8 were waited for; matrix products, arithmetic and copies ran while one was open for 0% of the time, Pallas kernels for 8%

profile of v2, /device:TPU:0, one launch (start us, length us, event | category | flops | bytes accessed | tf_op | source)
XLA Modules:
  0.0 32.0 jit_solution(1096947833443939301)
XLA Ops:
  0.6 0.9 %pack.1 = (bf16[64,128]{1,0:T(8,128)(2,1)S(1)}, bf16[96,256]{1,0:T(8,128)(2,1)S(1)}) custom-call(s32[2]{0:T(128)} %bitcast.17, bf16[32,256]{1,0:T(8,128)(2,1)} %bitcast.15, f32[64,256]{1,0:T(8,128)} %bitcast.11), custom_call_target="tpu_custom_call" | custom-call | bytes 81928 | tf_op jit(solution)/shard_map/pack/pallas_call | solution.py:217
  1.5 0.5 %collective-permute-start = (bf16[64,128]{1,0:T(8,128)(2,1)S(1)}, bf16[64,128]{1,0:T(8,128)(2,1)S(1)}, u32[]{:S(2)}, u32[]{:S(2)}) collective-permute-start(bf16[64,128]{1,0:T(8,128)(2,1)S(1)} %get-tuple-element.20), channel_id=1, source_target_pairs={{0,1},{1,0},{2,3},{3,2},{4,5},{5,4},{6,7},{7,6},{8,9},{9,8},{10,11... | collective-permute-start | bytes 49160 | tf_op jit(solution)/shard_map/ppermute | solution.py:235
  2.1 3.6 %collective-permute-start.6 = (bf16[96,256]{1,0:T(8,128)(2,1)S(1)}, bf16[96,256]{1,0:T(8,128)(2,1)S(1)}, u32[]{:S(2)}, u32[]{:S(2)}) collective-permute-start(bf16[96,256]{1,0:T(8,128)(2,1)S(1)} %get-tuple-element.21.rest_4_.rest_0_), channel_id=1, source_target_pairs={{0,25},{1,24},{2,27},{3,26},{4,29},{5,28},{6,31},{7,30},{8,17},{9,... | collective-permute-start | bytes 147464 | tf_op jit(solution)/shard_map/ppermute | solution.py:235
  5.6 0.2 collective-permute-start.5
  5.8 0.1 collective-permute-start.4
  5.9 0.0 collective-permute-done
  6.0 3.8 %collective-permute-start.3 = (bf16[64,128]{1,0:T(8,128)(2,1)S(1)}, bf16[64,128]{1,0:T(8,128)(2,1)S(1)}, u32[]{:S(2)}, u32[]{:S(2)}) collective-permute-start(bf16[64,128]{1,0:T(8,128)(2,1)S(1)} %add.15.rest_0_), channel_id=1, source_target_pairs={{0,7},{1,6},{2,5},{3,4},{4,3},{5,2},{6,1},{7,0},{8,15},{9,14},{10,... | collective-permute-start | bytes 49160 | tf_op jit(solution)/shard_map/ppermute | solution.py:235
  9.7 0.0 collective-permute-start.2
  9.7 1.4 %collective-permute-done.3.rest_3_ = bf16[64,128]{1,0:T(8,128)(2,1)S(1)} collective-permute-done((bf16[64,128]{1,0:T(8,128)(2,1)S(1)}, bf16[64,128]{1,0:T(8,128)(2,1)S(1)}, u32[]{:S(2)}, u32[]{:S(2)}) %collective-permute-start.3) | collective-permute-done | bytes 16416 | tf_op jit(solution)/shard_map/ppermute | solution.py:235
  11.2 0.0 collective-permute-start.1
  11.2 1.3 %prepare.1 = (bf16[128,2048]{1,0:T(8,128)(2,1)S(1)}, bf16[64,2048]{1,0:T(8,128)(2,1)S(1)}, f32[64,128]{1,0:T(8,128)S(1)}, f32[64,128]{1,0:T(8,128)S(1)}, f32[16,...) custom-call(s32[2]{0:T(128)} %bitcast.18, bf16[32,2048]{1,0:T(8,128)(2,1)} %freq_hbm.1, ...), custom_call_target="tpu_custom_call" | custom-call | flops 100000000 | bytes 599048 | tf_op jit(solution)/shard_map/prepare/pallas_call | solution.py:217
  12.5 1.3 %collective-permute-done.2.rest_2_ = bf16[64,128]{1,0:T(8,128)(2,1)S(1)} collective-permute-done((bf16[64,128]{1,0:T(8,128)(2,1)S(1)}, bf16[64,128]{1,0:T(8,128)(2,1)S(1)}, u32[]{:S(2)}, u32[]{:S(2)}) %collective-permute-start.2) | collective-permute-done | bytes 16416 | tf_op jit(solution)/shard_map/ppermute | solution.py:235
  13.8 0.6 %collective-permute-done.1.rest_1_ = bf16[64,128]{1,0:T(8,128)(2,1)S(1)} collective-permute-done((bf16[64,128]{1,0:T(8,128)(2,1)S(1)}, bf16[64,128]{1,0:T(8,128)(2,1)S(1)}, u32[]{:S(2)}, u32[]{:S(2)}) %collective-permute-start.1) | collective-permute-done | bytes 16416 | tf_op jit(solution)/shard_map/ppermute | solution.py:235
  14.4 0.0 collective-permute-done.6.rest_7_.rest_3_
  14.4 0.0 collective-permute-done.5.rest_6_.rest_2_
  14.4 0.0 collective-permute-done.4.rest_5_.rest_1_
  14.4 1.2 %first.1 = (f32[64,128]{1,0:T(8,128)S(1)}, bf16[96,128]{1,0:T(8,128)(2,1)S(1)}, bf16[64,128]{1,0:T(8,128)(2,1)S(1)}) custom-call(bf16[128,2048]{1,0:T(8,128)(2,1)S(1)} %get-tuple-element.17.angle_ref, bf16[64,2048]{1,0:T(8,128)(2,1)S(1)} %get-tuple-element.18.weight_ref, f32[64,128]{1,0:T(8,128)S(1)} %get-tuple-element.19.base_ref, ...), custom_call_target="tpu_custom_call" | custom-call | flops 1000000000 | bytes 1081344 | tf_op jit(solution)/shard_map/first/pallas_call | solution.py:217
  15.5 2.5 %collective-permute-start.9 = (bf16[96,128]{1,0:T(8,128)(2,1)S(1)}, bf16[96,128]{1,0:T(8,128)(2,1)S(1)}, u32[]{:S(2)}, u32[]{:S(2)}) collective-permute-start(bf16[96,128]{1,0:T(8,128)(2,1)S(1)} %get-tuple-element.25.rest_0_), channel_id=1, source_target_pairs={{0,25},{1,24},{2,27},{3,26},{4,29},{5,28},{6,31},{7,30},{8,17},{9,... | collective-permute-start | bytes 73736 | tf_op jit(solution)/shard_map/ppermute | solution.py:235
  18.1 0.5 %collective-permute-start.8 = (bf16[96,128]{1,0:T(8,128)(2,1)S(1)}, bf16[96,128]{1,0:T(8,128)(2,1)S(1)}, u32[]{:S(2)}, u32[]{:S(2)}) collective-permute-start(bf16[96,128]{1,0:T(8,128)(2,1)S(1)} %get-tuple-element.25.rest_0_), channel_id=1, source_target_pairs={{0,17},{1,16},{2,19},{3,18},{4,21},{5,20},{6,23},{7,22},{8,25},{9,... | collective-permute-start | bytes 73736 | tf_op jit(solution)/shard_map/ppermute | solution.py:235
  18.5 0.3 %collective-permute-start.7 = (bf16[96,128]{1,0:T(8,128)(2,1)S(1)}, bf16[96,128]{1,0:T(8,128)(2,1)S(1)}, u32[]{:S(2)}, u32[]{:S(2)}) collective-permute-start(bf16[96,128]{1,0:T(8,128)(2,1)S(1)} %get-tuple-element.25.rest_0_), channel_id=1, source_target_pairs={{0,9},{1,8},{2,11},{3,10},{4,13},{5,12},{6,15},{7,14},{8,1},{9,0},... | collective-permute-start | bytes 73736 | tf_op jit(solution)/shard_map/ppermute | solution.py:235
  18.9 1.2 %second.1.second_ref = f32[64,128]{1,0:T(8,128)S(1)} custom-call(bf16[128,2048]{1,0:T(8,128)(2,1)S(1)} %get-tuple-element.17.angle_ref, bf16[64,2048]{1,0:T(8,128)(2,1)S(1)} %get-tuple-element.18.weight_ref, f32[64,128]{1,0:T(8,128)S(1)} %get-tuple-element.24.later_ref, bf16[64,128]{1,0:T(8,128)(2,1)S(1)} %get-tuple-element.22.batch_ref, ...), custom_call_target="tpu_custom_call" | custom-call | flops 1000000000 | bytes 1032192 | tf_op jit(solution)/shard_map/second/pallas_call | solution.py:217
  20.0 0.0 collective-permute-done.9.rest_3_
  20.0 1.3 %collective-permute-done.8.rest_2_ = bf16[96,128]{1,0:T(8,128)(2,1)S(1)} collective-permute-done((bf16[96,128]{1,0:T(8,128)(2,1)S(1)}, bf16[96,128]{1,0:T(8,128)(2,1)S(1)}, u32[]{:S(2)}, u32[]{:S(2)}) %collective-permute-start.8) | collective-permute-done | bytes 24608 | tf_op jit(solution)/shard_map/ppermute | solution.py:235
  21.3 0.5 %collective-permute-done.7.rest_1_ = bf16[96,128]{1,0:T(8,128)(2,1)S(1)} collective-permute-done((bf16[96,128]{1,0:T(8,128)(2,1)S(1)}, bf16[96,128]{1,0:T(8,128)(2,1)S(1)}, u32[]{:S(2)}, u32[]{:S(2)}) %collective-permute-start.7) | collective-permute-done | bytes 24608 | tf_op jit(solution)/shard_map/ppermute | solution.py:235
  21.8 0.5 %correct.1 = f32[128,128]{1,0:T(8,128)S(1)} custom-call(bf16[64,128]{1,0:T(8,128)(2,1)S(1)} %get-tuple-element.22.batch_ref, f32[64,128]{1,0:T(8,128)S(1)} %get-tuple-element.23.first_ref, f32[64,128]{1,0:T(8,128)S(1)} %second.1.second_ref, bf16[96,128]{1,0:T(8,128)(2,1)S(1)} %get-tuple-element.25.rest_0_, ...), custom_call_target="tpu_custom_call" | custom-call | flops 100000000 | bytes 180224 | tf_op jit(solution)/shard_map/correct/pallas_call | solution.py:217
  22.3 0.2 collective-permute-start.10
  22.6 1.1 %collective-permute-done.10 = f32[128,128]{1,0:T(8,128)S(1)} collective-permute-done((f32[128,128]{1,0:T(8,128)S(1)}, f32[128,128]{1,0:T(8,128)S(1)}, u32[]{:S(2)}, u32[]{:S(2)}) %collective-permute-start.10) | collective-permute-done | bytes 65568 | tf_op jit(solution)/shard_map/ppermute | solution.py:235
  23.7 3.4 %collective-permute-start.13 = (f16[128,128]{1,0:T(8,128)(2,1)S(1)}, f16[128,128]{1,0:T(8,128)(2,1)S(1)}, u32[]{:S(2)}, u32[]{:S(2)}) collective-permute-start(f16[128,128]{1,0:T(8,128)(2,1)S(1)} %get-tuple-element.30), channel_id=1, source_target_pairs={{0,7},{1,6},{2,5},{3,4},{4,3},{5,2},{6,1},{7,0},{8,15},{9,14},{10,... | collective-permute-start | bytes 98312 | tf_op jit(solution)/shard_map/ppermute | solution.py:235
  27.1 0.0 collective-permute-start.12
  27.1 0.6 %collective-permute-start.11 = (f16[128,128]{1,0:T(8,128)(2,1)S(1)}, f16[128,128]{1,0:T(8,128)(2,1)S(1)}, u32[]{:S(2)}, u32[]{:S(2)}) collective-permute-start(f16[128,128]{1,0:T(8,128)(2,1)S(1)} %get-tuple-element.30), channel_id=1, source_target_pairs={{0,3},{1,2},{2,1},{3,0},{4,7},{5,6},{6,5},{7,4},{8,11},{9,10},{10,... | collective-permute-start | bytes 98312 | tf_op jit(solution)/shard_map/ppermute | solution.py:235
  27.7 1.2 %collective-permute-done.13 = f16[128,128]{1,0:T(8,128)(2,1)S(1)} collective-permute-done((f16[128,128]{1,0:T(8,128)(2,1)S(1)}, f16[128,128]{1,0:T(8,128)(2,1)S(1)}, u32[]{:S(2)}, u32[]{:S(2)}) %collective-permute-start.13) | collective-permute-done | bytes 32800 | tf_op jit(solution)/shard_map/ppermute | solution.py:235
  28.9 2.5 %collective-permute-done.12 = f16[128,128]{1,0:T(8,128)(2,1)S(1)} collective-permute-done((f16[128,128]{1,0:T(8,128)(2,1)S(1)}, f16[128,128]{1,0:T(8,128)(2,1)S(1)}, u32[]{:S(2)}, u32[]{:S(2)}) %collective-permute-start.12) | collective-permute-done | bytes 32800 | tf_op jit(solution)/shard_map/ppermute | solution.py:235
  31.3 0.0 collective-permute-done.11
  31.4 0.7 %finish.1 = (f32[64,256]{1,0:T(8,128)}, f32[64,256]{1,0:T(8,128)}) custom-call(f32[16,256]{1,0:T(8,128)S(1)} %get-tuple-element.16.marks_ref, f32[128,128]{1,0:T(8,128)S(1)} %multiply_add_fusion.total_ref, f32[64,256]{1,0:T(8,128)S(1)} %get-tuple-element.26.duals_ref, f32[64,256]{1,0:T(8,128)S(1)} %get-tuple-element.27.velocity_ref), custom_call_target="tpu_custom_call" | custom-call | bytes 212992 | tf_op jit(solution)/shard_map/finish/pallas_call | solution.py:217
  (3 shorter events, 0.0 us)
Async XLA Ops:
  1.5 4.4 %collective-permute-start = (bf16[64,128]{1,0:T(8,128)(2,1)S(1)}, bf16[64,128]{1,0:T(8,128)(2,1)S(1)}, u32[]{:S(2)}, u32[]{:S(2)}) collective-permute-start(bf16[64,128]{1,0:T(8,128)(2,1)S(1)} %get-tuple-element.20), channel_id=1, source_target_pairs={{0,1},{1,0},{2,3},{3,2},{4,5},{5,4},{6,7},{7,6},{8,9},{9,8},{10,11... | collective-permute-start | bytes 49160 | tf_op jit(solution)/shard_map/ppermute | solution.py:235
  2.1 12.3 %collective-permute-start.6 = (bf16[96,256]{1,0:T(8,128)(2,1)S(1)}, bf16[96,256]{1,0:T(8,128)(2,1)S(1)}, u32[]{:S(2)}, u32[]{:S(2)}) collective-permute-start(bf16[96,256]{1,0:T(8,128)(2,1)S(1)} %get-tuple-element.21.rest_4_.rest_0_), channel_id=1, source_target_pairs={{0,25},{1,24},{2,27},{3,26},{4,29},{5,28},{6,31},{7,30},{8,17},{9,... | collective-permute-start | bytes 147464 | tf_op jit(solution)/shard_map/ppermute | solution.py:235
  5.6 8.7 %collective-permute-start.5 = (bf16[96,256]{1,0:T(8,128)(2,1)S(1)}, bf16[96,256]{1,0:T(8,128)(2,1)S(1)}, u32[]{:S(2)}, u32[]{:S(2)}) collective-permute-start(bf16[96,256]{1,0:T(8,128)(2,1)S(1)} %get-tuple-element.21.rest_4_.rest_0_), channel_id=1, source_target_pairs={{0,17},{1,16},{2,19},{3,18},{4,21},{5,20},{6,23},{7,22},{8,25},{9,... | collective-permute-start | bytes 147464 | tf_op jit(solution)/shard_map/ppermute | solution.py:235
  5.8 8.6 %collective-permute-start.4 = (bf16[96,256]{1,0:T(8,128)(2,1)S(1)}, bf16[96,256]{1,0:T(8,128)(2,1)S(1)}, u32[]{:S(2)}, u32[]{:S(2)}) collective-permute-start(bf16[96,256]{1,0:T(8,128)(2,1)S(1)} %get-tuple-element.21.rest_4_.rest_0_), channel_id=1, source_target_pairs={{0,9},{1,8},{2,11},{3,10},{4,13},{5,12},{6,15},{7,14},{8,1},{9,0},... | collective-permute-start | bytes 147464 | tf_op jit(solution)/shard_map/ppermute | solution.py:235
  6.0 5.2 %collective-permute-start.3 = (bf16[64,128]{1,0:T(8,128)(2,1)S(1)}, bf16[64,128]{1,0:T(8,128)(2,1)S(1)}, u32[]{:S(2)}, u32[]{:S(2)}) collective-permute-start(bf16[64,128]{1,0:T(8,128)(2,1)S(1)} %add.15.rest_0_), channel_id=1, source_target_pairs={{0,7},{1,6},{2,5},{3,4},{4,3},{5,2},{6,1},{7,0},{8,15},{9,14},{10,... | collective-permute-start | bytes 49160 | tf_op jit(solution)/shard_map/ppermute | solution.py:235
  9.7 4.1 %collective-permute-start.2 = (bf16[64,128]{1,0:T(8,128)(2,1)S(1)}, bf16[64,128]{1,0:T(8,128)(2,1)S(1)}, u32[]{:S(2)}, u32[]{:S(2)}) collective-permute-start(bf16[64,128]{1,0:T(8,128)(2,1)S(1)} %add.15.rest_0_), channel_id=1, source_target_pairs={{0,5},{1,4},{2,7},{3,6},{4,1},{5,0},{6,3},{7,2},{8,13},{9,12},{10,... | collective-permute-start | bytes 49160 | tf_op jit(solution)/shard_map/ppermute | solution.py:235
  11.2 3.2 %collective-permute-start.1 = (bf16[64,128]{1,0:T(8,128)(2,1)S(1)}, bf16[64,128]{1,0:T(8,128)(2,1)S(1)}, u32[]{:S(2)}, u32[]{:S(2)}) collective-permute-start(bf16[64,128]{1,0:T(8,128)(2,1)S(1)} %add.15.rest_0_), channel_id=1, source_target_pairs={{0,3},{1,2},{2,1},{3,0},{4,7},{5,6},{6,5},{7,4},{8,11},{9,10},{10,... | collective-permute-start | bytes 49160 | tf_op jit(solution)/shard_map/ppermute | solution.py:235
  15.5 4.5 %collective-permute-start.9 = (bf16[96,128]{1,0:T(8,128)(2,1)S(1)}, bf16[96,128]{1,0:T(8,128)(2,1)S(1)}, u32[]{:S(2)}, u32[]{:S(2)}) collective-permute-start(bf16[96,128]{1,0:T(8,128)(2,1)S(1)} %get-tuple-element.25.rest_0_), channel_id=1, source_target_pairs={{0,25},{1,24},{2,27},{3,26},{4,29},{5,28},{6,31},{7,30},{8,17},{9,... | collective-permute-start | bytes 73736 | tf_op jit(solution)/shard_map/ppermute | solution.py:235
  18.1 3.3 %collective-permute-start.8 = (bf16[96,128]{1,0:T(8,128)(2,1)S(1)}, bf16[96,128]{1,0:T(8,128)(2,1)S(1)}, u32[]{:S(2)}, u32[]{:S(2)}) collective-permute-start(bf16[96,128]{1,0:T(8,128)(2,1)S(1)} %get-tuple-element.25.rest_0_), channel_id=1, source_target_pairs={{0,17},{1,16},{2,19},{3,18},{4,21},{5,20},{6,23},{7,22},{8,25},{9,... | collective-permute-start | bytes 73736 | tf_op jit(solution)/shard_map/ppermute | solution.py:235
  18.5 3.3 %collective-permute-start.7 = (bf16[96,128]{1,0:T(8,128)(2,1)S(1)}, bf16[96,128]{1,0:T(8,128)(2,1)S(1)}, u32[]{:S(2)}, u32[]{:S(2)}) collective-permute-start(bf16[96,128]{1,0:T(8,128)(2,1)S(1)} %get-tuple-element.25.rest_0_), channel_id=1, source_target_pairs={{0,9},{1,8},{2,11},{3,10},{4,13},{5,12},{6,15},{7,14},{8,1},{9,0},... | collective-permute-start | bytes 73736 | tf_op jit(solution)/shard_map/ppermute | solution.py:235
  22.3 1.3 %collective-permute-start.10 = (f32[128,128]{1,0:T(8,128)S(1)}, f32[128,128]{1,0:T(8,128)S(1)}, u32[]{:S(2)}, u32[]{:S(2)}) collective-permute-start(f32[128,128]{1,0:T(8,128)S(1)} %correct.1), channel_id=1, source_target_pairs={{0,1},{1,0},{2,3},{3,2},{4,5},{5,4},{6,7},{7,6},{8,9},{9,8},{10,11... | collective-permute-start | bytes 196616 | tf_op jit(solution)/shard_map/ppermute | solution.py:235
  23.7 5.2 %collective-permute-start.13 = (f16[128,128]{1,0:T(8,128)(2,1)S(1)}, f16[128,128]{1,0:T(8,128)(2,1)S(1)}, u32[]{:S(2)}, u32[]{:S(2)}) collective-permute-start(f16[128,128]{1,0:T(8,128)(2,1)S(1)} %get-tuple-element.30), channel_id=1, source_target_pairs={{0,7},{1,6},{2,5},{3,4},{4,3},{5,2},{6,1},{7,0},{8,15},{9,14},{10,... | collective-permute-start | bytes 98312 | tf_op jit(solution)/shard_map/ppermute | solution.py:235
  27.1 4.2 %collective-permute-start.12 = (f16[128,128]{1,0:T(8,128)(2,1)S(1)}, f16[128,128]{1,0:T(8,128)(2,1)S(1)}, u32[]{:S(2)}, u32[]{:S(2)}) collective-permute-start(f16[128,128]{1,0:T(8,128)(2,1)S(1)} %get-tuple-element.30), channel_id=1, source_target_pairs={{0,5},{1,4},{2,7},{3,6},{4,1},{5,0},{6,3},{7,2},{8,13},{9,12},{10,... | collective-permute-start | bytes 98312 | tf_op jit(solution)/shard_map/ppermute | solution.py:235
  27.1 4.2 %collective-permute-start.11 = (f16[128,128]{1,0:T(8,128)(2,1)S(1)}, f16[128,128]{1,0:T(8,128)(2,1)S(1)}, u32[]{:S(2)}, u32[]{:S(2)}) collective-permute-start(f16[128,128]{1,0:T(8,128)(2,1)S(1)} %get-tuple-element.30), channel_id=1, source_target_pairs={{0,3},{1,2},{2,1},{3,0},{4,7},{5,6},{6,5},{7,4},{8,11},{9,10},{10,... | collective-permute-start | bytes 98312 | tf_op jit(solution)/shard_map/ppermute | solution.py:235

commit v3 on v2

--- a/solution.py
+++ b/solution.py
@@ -26,7 +26,7 @@
     nodes = np.cos(np.pi * (np.arange(64) + 0.5) / 64)
     squares = (nodes + 1.0) * 0.125
     fit = np.polynomial.chebyshev.Chebyshev.fit(
-        squares, np.cos(2.0 * np.pi * np.sqrt(squares)), 6, domain=[0.0, 0.25]
+        squares, np.cos(2.0 * np.pi * np.sqrt(squares)), 5, domain=[0.0, 0.25]
     )
     return [float(c) for c in fit.convert(kind=np.polynomial.Polynomial).coef]
 
@@ -94,9 +94,9 @@
     return total
 
 
-def place_of(tiles_ref, step, tiles_per):
+def place_of(tiles_ref, step, tiles_per, core=0):
     tile = tiles_ref[step]
-    mine = lax.div(tile, tiles_per) == lax.axis_index("feat")
+    mine = lax.div(tile, tiles_per) == lax.bitwise_xor(lax.axis_index("feat"), core)
     return mine, pl.ds(pl.multiple_of(lax.rem(tile, tiles_per) * TILE, TILE), TILE)
 
 
@@ -108,27 +108,32 @@
         copy.wait()
 
 
-def pack_kernel(tiles_hbm, points_hbm, duals_hbm, batch_ref, static_ref, tiles_ref, points_ref, duals_ref, sems):
-    fetch([(tiles_hbm, tiles_ref), (points_hbm, points_ref), (duals_hbm, duals_ref)], sems)
+def pack_kernel(marks_ref, points_ref, other_ref, duals_ref, batch_ref, static_ref):
     depth, count = points_ref.shape
     values = duals_ref.shape[0]
     for step in range(2):
-        mine, where = place_of(tiles_ref, step, count // TILE)
-        rows = points_ref[:, where]
-        batch_ref[depth * step : depth * (step + 1), :] = jnp.where(mine, rows, jnp.zeros_like(rows))
+        rows = None
+        for core, from_ref in enumerate((points_ref, other_ref)):
+            row = 8 * (step + 2 * core)
+            kept = jnp.where(marks_ref[row : row + 1, :] > 0.0, from_ref[...].astype(f32), 0.0)
+            for start in range(0, count, TILE):
+                piece = kept[:, start : start + TILE]
+                rows = piece if rows is None else rows + piece
+        batch_ref[depth * step : depth * (step + 1), :] = rows.astype(bf16)
     static_ref[:values, :] = duals_ref[...].astype(bf16)
     static_ref[values:, :] = points_ref[...]
 
 
 def prepare_kernel(
-    tiles_hbm, freq_hbm, phase_hbm, weight_hbm, observed_hbm, noise_hbm, velocity_hbm, duals_hbm,
-    angle_ref, weight_ref, base_ref, later_ref, marks_ref, velocity_ref, duals_ref,
+    tiles_hbm, freq_hbm, phase_hbm, weight_hbm, observed_hbm, noise_hbm, velocity_hbm, duals_hbm, points_hbm,
+    angle_ref, weight_ref, base_ref, later_ref, marks_ref, velocity_ref, duals_ref, points_ref,
     tiles_ref, freq_ref, phase_ref, observed_ref, noise_ref, sems,
 ):
     fetch(
         [
             (freq_hbm, freq_ref), (phase_hbm, phase_ref), (weight_hbm, weight_ref), (tiles_hbm, tiles_ref),
             (observed_hbm, observed_ref), (noise_hbm, noise_ref), (velocity_hbm, velocity_ref), (duals_hbm, duals_ref),
+            (points_hbm, points_ref),
         ],
         sems,
     )
@@ -153,6 +158,8 @@
         share_ref[...] = jnp.where(mine, share, 0.0)
         inside = (columns >= where.start) & (columns < where.start + TILE)
         marks_ref[8 * step : 8 * (step + 1), :] = jnp.where(mine & inside, 1.0, 0.0)
+        mine, _ = place_of(tiles_ref, step, count // TILE, 1)
+        marks_ref[8 * (step + 2) : 8 * (step + 3), :] = jnp.where(mine & inside, 1.0, 0.0)
 
 
 def share_of(scales, upright, rows, angle_ref, weight_ref, base_ref, blocks):
@@ -257,21 +264,32 @@
     def other_groups(array):
         return [swap(array, groups, members, k, 1) for k in range(1, groups)]
 
-    batch, static = call(
-        pack_kernel, [((2 * depth, TILE), bf16), ((samples + depth, count), bf16)], tiles, points, duals,
-        name="pack", from_hbm=(-1,),
-    )
-    fixed = [static] + other_groups(static)
-    batch = batch + other_core(batch)
-    batch = [batch] + other_chips(batch)
     whole = (samples, count)
-    angles, weights, base, later, marks, velocity, duals = call(
+    other_points = other_core(points)
+    angles, weights, base, later, marks, velocity, duals, points = call(
         prepare_kernel,
         [((ANGLE_ROWS, features), bf16), ((samples, features), bf16), (part, f32), (part, f32),
-         ((16, count), f32), (whole, f32), (whole, f32)],
-        tiles, frequencies, phases, weights, observed, noise, velocity, duals,
-        name="prepare", from_hbm=(3, 6, 7), flops=10**8,
-    )
+         ((32, count), f32), (whole, f32), (whole, f32), ((depth, count), bf16)],
+        tiles, frequencies, phases, weights, observed, noise, velocity, duals, points,
+        name="prepare", from_hbm=(3, 6, 7, 8), flops=10**8,
+    )
+    batch, static = call(
+        pack_kernel, [((2 * depth, TILE), bf16), ((samples + depth, count), bf16)], marks, points, other_points, duals,
+        name="pack",
+    )
+    batch, fixed = [batch], [static]
+    chip_bit, group_bit = 2, 1
+    while chip_bit < members or group_bit < groups:
+        if group_bit < groups:
+            wide = jnp.concatenate(fixed, axis=1) if len(fixed) > 1 else static
+            fixed.append(swap(wide, groups, members, group_bit, 1))
+        if chip_bit < members:
+            whole_batch = sum(batch[1:], batch[0])
+            batch = [whole_batch, swap(whole_batch, groups, members, 0, chip_bit + 1)]
+        if 2 * group_bit < groups and 2 * chip_bit < members:
+            fixed[-1], batch[1] = lax.optimization_barrier((fixed[-1], batch[1]))
+        chip_bit, group_bit = 2 * chip_bit, 2 * group_bit
+
     share, send, batch = call(
         functools.partial(first_kernel, scales, len(batch)),
         [(part, f32), ((samples + depth, TILE), bf16), ((2 * depth, TILE), bf16)],
@@ -288,8 +306,10 @@
         batch, share, later, *moves, flops=10**8, name="correct",
     )
     total = total + other_core(total)
-    for term in other_chips((total * SHRINK).astype(jnp.float16)):
-        total = total + term.astype(f32) * (1.0 / SHRINK)
+    bit = 2
+    while bit < members:
+        total = total + swap((total * SHRINK).astype(jnp.float16), groups, members, 0, bit + 1).astype(f32) * (1.0 / SHRINK)
+        bit *= 2
     new_duals, new_velocity = call(
         finish_kernel, [(whole, f32)] * 2, marks, total, duals, velocity, name="finish"
     )

time: 32.2 us -> 30.5 us (0.947)
  waiting for transfers between devices: 9.82 us -> 8.61 us
  Pallas kernels: 5.7 us -> 4.7 us
  starting transfers between devices: 15.8 us -> 16.2 us
    ppermute x14 -> x11, waiting for transfers between devices: 9.82 us -> 8.61 us  [swap(): return lax.ppermute(array, ('grp', 'feat'), pairs)]
    pallas_call x6, Pallas kernels: 5.7 us -> 4.7 us  [call(): pl.pallas_call(kernel, out_shape=[jax.ShapeDtypeStruct(shape, dtype) for...]
    ppermute x14 -> x11, starting transfers between devices: 15.8 us -> 16.2 us  [swap(): return lax.ppermute(array, ('grp', 'feat'), pairs)]
  transfers between devices with their start and end apart: 14 -> 11, of which waited for: 8 -> 6; matrix products, arithmetic and copies ran while one was open for 0% -> 0% of each run, Pallas kernels for 8% -> 8%
where the time goes in v3:
time: 30.5 us; the launch traced here: 30.3 us
  starting transfers between devices  16.2 us (53%)
  waiting for transfers between devices  8.61 us (28%)
  Pallas kernels  4.7 us (15%)
  between operations  0.72 us (2%)
    ppermute x11, starting transfers between devices, swap(): return lax.ppermute(array, ('grp', 'feat'), pairs)  16.2 us
    ppermute x11, waiting for transfers between devices, swap(): return lax.ppermute(array, ('grp', 'feat'), pairs)  8.61 us
    pallas_call x6, Pallas kernels, call(): pl.pallas_call(kernel, out_shape=[jax.ShapeDtypeStruct(shape, dtype) for...  4.7 us
  transfers between devices with their start and end apart: 11, of which 6 were waited for; matrix products, arithmetic and copies ran while one was open for 0% of the time, Pallas kernels for 8%

profile of v3, /device:TPU:0, one launch (start us, length us, event | category | flops | bytes accessed | tf_op | source)
XLA Modules:
  0.0 30.3 jit_solution(4981001388938182152)
XLA Ops:
  0.6 0.5 %collective-permute-start = (bf16[32,256]{1,0:T(8,128)(2,1)}, bf16[32,256]{1,0:T(8,128)(2,1)S(1)}, u32[]{:S(2)}, u32[]{:S(2)}) collective-permute-start(bf16[32,256]{1,0:T(8,128)(2,1)} %bitcast.14), channel_id=1, source_target_pairs={{0,1},{1,0},{2,3},{3,2},{4,5},{5,4},{6,7},{7,6},{8,9},{9,8},{10,11... | collective-permute-start | bytes 49160 | tf_op jit(solution)/shard_map/ppermute | solution.py:242
  1.2 1.3 %prepare.1 = (bf16[128,2048]{1,0:T(8,128)(2,1)S(1)}, bf16[64,2048]{1,0:T(8,128)(2,1)S(1)}, f32[64,128]{1,0:T(8,128)S(1)}, f32[64,128]{1,0:T(8,128)S(1)}, f32[32,...) custom-call(s32[2]{0:T(128)} %bitcast.18, ...), custom_call_target="tpu_custom_call" | custom-call | flops 100000000 | bytes 615432 | tf_op jit(solution)/shard_map/prepare/pallas_call | solution.py:224
  2.4 0.0 collective-permute-done.other_ref
  2.5 2.7 %collective-permute-start.1 = (bf16[96,256]{1,0:T(8,128)(2,1)S(1)}, bf16[96,256]{1,0:T(8,128)(2,1)S(1)}, u32[]{:S(2)}, u32[]{:S(2)}) collective-permute-start(bf16[96,256]{1,0:T(8,128)(2,1)S(1)} %get-tuple-element.26.rest_2_.rest_0_), channel_id=1, source_target_pairs={{0,9},{1,8},{2,11},{3,10},{4,13},{5,12},{6,15},{7,14},{8,1},{9,0},... | collective-permute-start | bytes 147464 | tf_op jit(solution)/shard_map/ppermute | solution.py:242
  5.2 1.3 %collective-permute-start.2 = (bf16[64,128]{1,0:T(8,128)(2,1)S(1)}, bf16[64,128]{1,0:T(8,128)(2,1)S(1)}, u32[]{:S(2)}, u32[]{:S(2)}) collective-permute-start(bf16[64,128]{1,0:T(8,128)(2,1)S(1)} %get-tuple-element.25), channel_id=1, source_target_pairs={{0,3},{1,2},{2,1},{3,0},{4,7},{5,6},{6,5},{7,4},{8,11},{9,10},{10,... | collective-permute-start | bytes 49160 | tf_op jit(solution)/shard_map/ppermute | solution.py:242
  6.4 1.9 %collective-permute-done.2 = bf16[64,128]{1,0:T(8,128)(2,1)S(1)} collective-permute-done((bf16[64,128]{1,0:T(8,128)(2,1)S(1)}, bf16[64,128]{1,0:T(8,128)(2,1)S(1)}, u32[]{:S(2)}, u32[]{:S(2)}) %collective-permute-start.2) | collective-permute-done | bytes 16416 | tf_op jit(solution)/shard_map/ppermute | solution.py:242
  8.3 0.0 collective-permute-done.1.rest_3_.rest_1_
  8.3 1.3 %collective-permute-start.4 = (bf16[96,512]{1,0:T(8,128)(2,1)S(1)}, bf16[96,512]{1,0:T(8,128)(2,1)S(1)}, u32[]{:S(2)}, u32[]{:S(2)}) collective-permute-start(bf16[96,512]{1,0:T(8,128)(2,1)S(1)} %pad_maximum_fusion), channel_id=1, source_target_pairs={{0,17},{1,16},{2,19},{3,18},{4,21},{5,20},{6,23},{7,22},{8,25},{9,... | collective-permute-start | bytes 294920 | tf_op jit(solution)/shard_map/ppermute | solution.py:242
  9.7 2.7 %collective-permute-start.3 = (bf16[64,128]{1,0:T(8,128)(2,1)S(1)}, bf16[64,128]{1,0:T(8,128)(2,1)S(1)}, u32[]{:S(2)}, u32[]{:S(2)}) collective-permute-start(bf16[64,128]{1,0:T(8,128)(2,1)S(1)} %add.12.rest_0_), channel_id=1, source_target_pairs={{0,5},{1,4},{2,7},{3,6},{4,1},{5,0},{6,3},{7,2},{8,13},{9,12},{10,... | collective-permute-start | bytes 49160 | tf_op jit(solution)/shard_map/ppermute | solution.py:242
  12.3 1.4 %collective-permute-done.3.rest_1_ = bf16[64,128]{1,0:T(8,128)(2,1)S(1)} collective-permute-done((bf16[64,128]{1,0:T(8,128)(2,1)S(1)}, bf16[64,128]{1,0:T(8,128)(2,1)S(1)}, u32[]{:S(2)}, u32[]{:S(2)}) %collective-permute-start.3) | collective-permute-done | bytes 16416 | tf_op jit(solution)/shard_map/ppermute | solution.py:242
  13.8 0.0 collective-permute-done.4.rest_4_.rest_2_
  13.8 1.1 %first.1 = (f32[64,128]{1,0:T(8,128)S(1)}, bf16[96,128]{1,0:T(8,128)(2,1)S(1)}, bf16[64,128]{1,0:T(8,128)(2,1)S(1)}) custom-call(bf16[128,2048]{1,0:T(8,128)(2,1)S(1)} %get-tuple-element.20.angle_ref, bf16[64,2048]{1,0:T(8,128)(2,1)S(1)} %get-tuple-element.21.weight_ref, f32[64,128]{1,0:T(8,128)S(1)} %get-tuple-element.22.base_ref, ...), custom_call_target="tpu_custom_call" | custom-call | flops 1000000000 | bytes 1048576 | tf_op jit(solution)/shard_map/first/pallas_call | solution.py:224
  14.9 0.7 %collective-permute-start.7 = (bf16[96,128]{1,0:T(8,128)(2,1)S(1)}, bf16[96,128]{1,0:T(8,128)(2,1)S(1)}, u32[]{:S(2)}, u32[]{:S(2)}) collective-permute-start(bf16[96,128]{1,0:T(8,128)(2,1)S(1)} %get-tuple-element.32.rest_0_), channel_id=1, source_target_pairs={{0,25},{1,24},{2,27},{3,26},{4,29},{5,28},{6,31},{7,30},{8,17},{9,... | collective-permute-start | bytes 73736 | tf_op jit(solution)/shard_map/ppermute | solution.py:242
  15.6 1.2 %collective-permute-start.6 = (bf16[96,128]{1,0:T(8,128)(2,1)S(1)}, bf16[96,128]{1,0:T(8,128)(2,1)S(1)}, u32[]{:S(2)}, u32[]{:S(2)}) collective-permute-start(bf16[96,128]{1,0:T(8,128)(2,1)S(1)} %get-tuple-element.32.rest_0_), channel_id=1, source_target_pairs={{0,17},{1,16},{2,19},{3,18},{4,21},{5,20},{6,23},{7,22},{8,25},{9,... | collective-permute-start | bytes 73736 | tf_op jit(solution)/shard_map/ppermute | solution.py:242
  16.8 1.4 %collective-permute-start.5 = (bf16[96,128]{1,0:T(8,128)(2,1)S(1)}, bf16[96,128]{1,0:T(8,128)(2,1)S(1)}, u32[]{:S(2)}, u32[]{:S(2)}) collective-permute-start(bf16[96,128]{1,0:T(8,128)(2,1)S(1)} %get-tuple-element.32.rest_0_), channel_id=1, source_target_pairs={{0,9},{1,8},{2,11},{3,10},{4,13},{5,12},{6,15},{7,14},{8,1},{9,0},... | collective-permute-start | bytes 73736 | tf_op jit(solution)/shard_map/ppermute | solution.py:242
  18.2 1.1 %second.1.second_ref = f32[64,128]{1,0:T(8,128)S(1)} custom-call(bf16[128,2048]{1,0:T(8,128)(2,1)S(1)} %get-tuple-element.20.angle_ref, bf16[64,2048]{1,0:T(8,128)(2,1)S(1)} %get-tuple-element.21.weight_ref, f32[64,128]{1,0:T(8,128)S(1)} %get-tuple-element.31.later_ref, bf16[64,128]{1,0:T(8,128)(2,1)S(1)} %get-tuple-element.29.batch_ref, ...), custom_call_target="tpu_custom_call" | custom-call | flops 1000000000 | bytes 1032192 | tf_op jit(solution)/shard_map/second/pallas_call | solution.py:224
  19.3 0.0 collective-permute-done.7.rest_3_
  19.3 0.0 collective-permute-done.6.rest_2_
  19.3 0.7 %collective-permute-done.5.rest_1_ = bf16[96,128]{1,0:T(8,128)(2,1)S(1)} collective-permute-done((bf16[96,128]{1,0:T(8,128)(2,1)S(1)}, bf16[96,128]{1,0:T(8,128)(2,1)S(1)}, u32[]{:S(2)}, u32[]{:S(2)}) %collective-permute-start.5) | collective-permute-done | bytes 24608 | tf_op jit(solution)/shard_map/ppermute | solution.py:242
  20.0 0.5 %correct.1 = f32[128,128]{1,0:T(8,128)S(1)} custom-call(bf16[64,128]{1,0:T(8,128)(2,1)S(1)} %get-tuple-element.29.batch_ref, f32[64,128]{1,0:T(8,128)S(1)} %get-tuple-element.30.first_ref, f32[64,128]{1,0:T(8,128)S(1)} %second.1.second_ref, bf16[96,128]{1,0:T(8,128)(2,1)S(1)} %get-tuple-element.32.rest_0_, ...), custom_call_target="tpu_custom_call" | custom-call | flops 100000000 | bytes 180224 | tf_op jit(solution)/shard_map/correct/pallas_call | solution.py:224
  20.6 0.4 %collective-permute-start.8 = (f32[128,128]{1,0:T(8,128)S(1)}, f32[128,128]{1,0:T(8,128)S(1)}, u32[]{:S(2)}, u32[]{:S(2)}) collective-permute-start(f32[128,128]{1,0:T(8,128)S(1)} %correct.1), channel_id=1, source_target_pairs={{0,1},{1,0},{2,3},{3,2},{4,5},{5,4},{6,7},{7,6},{8,9},{9,8},{10,11... | collective-permute-start | bytes 196616 | tf_op jit(solution)/shard_map/ppermute | solution.py:242
  20.9 1.0 %collective-permute-done.8 = f32[128,128]{1,0:T(8,128)S(1)} collective-permute-done((f32[128,128]{1,0:T(8,128)S(1)}, f32[128,128]{1,0:T(8,128)S(1)}, u32[]{:S(2)}, u32[]{:S(2)}) %collective-permute-start.8) | collective-permute-done | bytes 65568 | tf_op jit(solution)/shard_map/ppermute | solution.py:242
  21.9 1.5 %collective-permute-start.9 = (f16[128,128]{1,0:T(8,128)(2,1)S(1)}, f16[128,128]{1,0:T(8,128)(2,1)S(1)}, u32[]{:S(2)}, u32[]{:S(2)}) collective-permute-start(f16[128,128]{1,0:T(8,128)(2,1)S(1)} %get-tuple-element.36), channel_id=1, source_target_pairs={{0,3},{1,2},{2,1},{3,0},{4,7},{5,6},{6,5},{7,4},{8,11},{9,10},{10,... | collective-permute-start | bytes 98312 | tf_op jit(solution)/shard_map/ppermute | solution.py:242
  23.5 1.9 %collective-permute-done.9 = f16[128,128]{1,0:T(8,128)(2,1)S(1)} collective-permute-done((f16[128,128]{1,0:T(8,128)(2,1)S(1)}, f16[128,128]{1,0:T(8,128)(2,1)S(1)}, u32[]{:S(2)}, u32[]{:S(2)}) %collective-permute-start.9) | collective-permute-done | bytes 32800 | tf_op jit(solution)/shard_map/ppermute | solution.py:242
  25.3 2.6 %collective-permute-start.10 = (f16[128,128]{1,0:T(8,128)(2,1)S(1)}, f16[128,128]{1,0:T(8,128)(2,1)S(1)}, u32[]{:S(2)}, u32[]{:S(2)}) collective-permute-start(f16[128,128]{1,0:T(8,128)(2,1)S(1)} %multiply_convert_fusion), channel_id=1, source_target_pairs={{0,5},{1,4},{2,7},{3,6},{4,1},{5,0},{6,3},{7,2},{8,13},{9,12},{10,... | collective-permute-start | bytes 98312 | tf_op jit(solution)/shard_map/ppermute | solution.py:242
  27.9 1.7 %collective-permute-done.10 = f16[128,128]{1,0:T(8,128)(2,1)S(1)} collective-permute-done((f16[128,128]{1,0:T(8,128)(2,1)S(1)}, f16[128,128]{1,0:T(8,128)(2,1)S(1)}, u32[]{:S(2)}, u32[]{:S(2)}) %collective-permute-start.10) | collective-permute-done | bytes 32800 | tf_op jit(solution)/shard_map/ppermute | solution.py:242
  29.7 0.7 %finish.1 = (f32[64,256]{1,0:T(8,128)}, f32[64,256]{1,0:T(8,128)}) custom-call(f32[32,256]{1,0:T(8,128)S(1)} %get-tuple-element.19.marks_ref, f32[128,128]{1,0:T(8,128)S(1)} %multiply_add_fusion.total_ref, f32[64,256]{1,0:T(8,128)S(1)} %get-tuple-element.24.duals_ref, f32[64,256]{1,0:T(8,128)S(1)} %get-tuple-element.33.velocity_ref), custom_call_target="tpu_custom_call" | custom-call | bytes 229376 | tf_op jit(solution)/shard_map/finish/pallas_call | solution.py:224
  (6 shorter events, 0.1 us)
Async XLA Ops:
  0.6 1.8 %collective-permute-start = (bf16[32,256]{1,0:T(8,128)(2,1)}, bf16[32,256]{1,0:T(8,128)(2,1)S(1)}, u32[]{:S(2)}, u32[]{:S(2)}) collective-permute-start(bf16[32,256]{1,0:T(8,128)(2,1)} %bitcast.14), channel_id=1, source_target_pairs={{0,1},{1,0},{2,3},{3,2},{4,5},{5,4},{6,7},{7,6},{8,9},{9,8},{10,11... | collective-permute-start | bytes 49160 | tf_op jit(solution)/shard_map/ppermute | solution.py:242
  2.5 5.8 %collective-permute-start.1 = (bf16[96,256]{1,0:T(8,128)(2,1)S(1)}, bf16[96,256]{1,0:T(8,128)(2,1)S(1)}, u32[]{:S(2)}, u32[]{:S(2)}) collective-permute-start(bf16[96,256]{1,0:T(8,128)(2,1)S(1)} %get-tuple-element.26.rest_2_.rest_0_), channel_id=1, source_target_pairs={{0,9},{1,8},{2,11},{3,10},{4,13},{5,12},{6,15},{7,14},{8,1},{9,0},... | collective-permute-start | bytes 147464 | tf_op jit(solution)/shard_map/ppermute | solution.py:242
  5.2 3.2 %collective-permute-start.2 = (bf16[64,128]{1,0:T(8,128)(2,1)S(1)}, bf16[64,128]{1,0:T(8,128)(2,1)S(1)}, u32[]{:S(2)}, u32[]{:S(2)}) collective-permute-start(bf16[64,128]{1,0:T(8,128)(2,1)S(1)} %get-tuple-element.25), channel_id=1, source_target_pairs={{0,3},{1,2},{2,1},{3,0},{4,7},{5,6},{6,5},{7,4},{8,11},{9,10},{10,... | collective-permute-start | bytes 49160 | tf_op jit(solution)/shard_map/ppermute | solution.py:242
  8.3 5.5 %collective-permute-start.4 = (bf16[96,512]{1,0:T(8,128)(2,1)S(1)}, bf16[96,512]{1,0:T(8,128)(2,1)S(1)}, u32[]{:S(2)}, u32[]{:S(2)}) collective-permute-start(bf16[96,512]{1,0:T(8,128)(2,1)S(1)} %pad_maximum_fusion), channel_id=1, source_target_pairs={{0,17},{1,16},{2,19},{3,18},{4,21},{5,20},{6,23},{7,22},{8,25},{9,... | collective-permute-start | bytes 294920 | tf_op jit(solution)/shard_map/ppermute | solution.py:242
  9.7 4.1 %collective-permute-start.3 = (bf16[64,128]{1,0:T(8,128)(2,1)S(1)}, bf16[64,128]{1,0:T(8,128)(2,1)S(1)}, u32[]{:S(2)}, u32[]{:S(2)}) collective-permute-start(bf16[64,128]{1,0:T(8,128)(2,1)S(1)} %add.12.rest_0_), channel_id=1, source_target_pairs={{0,5},{1,4},{2,7},{3,6},{4,1},{5,0},{6,3},{7,2},{8,13},{9,12},{10,... | collective-permute-start | bytes 49160 | tf_op jit(solution)/shard_map/ppermute | solution.py:242
  14.9 4.4 %collective-permute-start.7 = (bf16[96,128]{1,0:T(8,128)(2,1)S(1)}, bf16[96,128]{1,0:T(8,128)(2,1)S(1)}, u32[]{:S(2)}, u32[]{:S(2)}) collective-permute-start(bf16[96,128]{1,0:T(8,128)(2,1)S(1)} %get-tuple-element.32.rest_0_), channel_id=1, source_target_pairs={{0,25},{1,24},{2,27},{3,26},{4,29},{5,28},{6,31},{7,30},{8,17},{9,... | collective-permute-start | bytes 73736 | tf_op jit(solution)/shard_map/ppermute | solution.py:242
  15.6 3.7 %collective-permute-start.6 = (bf16[96,128]{1,0:T(8,128)(2,1)S(1)}, bf16[96,128]{1,0:T(8,128)(2,1)S(1)}, u32[]{:S(2)}, u32[]{:S(2)}) collective-permute-start(bf16[96,128]{1,0:T(8,128)(2,1)S(1)} %get-tuple-element.32.rest_0_), channel_id=1, source_target_pairs={{0,17},{1,16},{2,19},{3,18},{4,21},{5,20},{6,23},{7,22},{8,25},{9,... | collective-permute-start | bytes 73736 | tf_op jit(solution)/shard_map/ppermute | solution.py:242
  16.8 3.3 %collective-permute-start.5 = (bf16[96,128]{1,0:T(8,128)(2,1)S(1)}, bf16[96,128]{1,0:T(8,128)(2,1)S(1)}, u32[]{:S(2)}, u32[]{:S(2)}) collective-permute-start(bf16[96,128]{1,0:T(8,128)(2,1)S(1)} %get-tuple-element.32.rest_0_), channel_id=1, source_target_pairs={{0,9},{1,8},{2,11},{3,10},{4,13},{5,12},{6,15},{7,14},{8,1},{9,0},... | collective-permute-start | bytes 73736 | tf_op jit(solution)/shard_map/ppermute | solution.py:242
  20.6 1.3 %collective-permute-start.8 = (f32[128,128]{1,0:T(8,128)S(1)}, f32[128,128]{1,0:T(8,128)S(1)}, u32[]{:S(2)}, u32[]{:S(2)}) collective-permute-start(f32[128,128]{1,0:T(8,128)S(1)} %correct.1), channel_id=1, source_target_pairs={{0,1},{1,0},{2,3},{3,2},{4,5},{5,4},{6,7},{7,6},{8,9},{9,8},{10,11... | collective-permute-start | bytes 196616 | tf_op jit(solution)/shard_map/ppermute | solution.py:242
  21.9 3.4 %collective-permute-start.9 = (f16[128,128]{1,0:T(8,128)(2,1)S(1)}, f16[128,128]{1,0:T(8,128)(2,1)S(1)}, u32[]{:S(2)}, u32[]{:S(2)}) collective-permute-start(f16[128,128]{1,0:T(8,128)(2,1)S(1)} %get-tuple-element.36), channel_id=1, source_target_pairs={{0,3},{1,2},{2,1},{3,0},{4,7},{5,6},{6,5},{7,4},{8,11},{9,10},{10,... | collective-permute-start | bytes 98312 | tf_op jit(solution)/shard_map/ppermute | solution.py:242
  25.3 4.3 %collective-permute-start.10 = (f16[128,128]{1,0:T(8,128)(2,1)S(1)}, f16[128,128]{1,0:T(8,128)(2,1)S(1)}, u32[]{:S(2)}, u32[]{:S(2)}) collective-permute-start(f16[128,128]{1,0:T(8,128)(2,1)S(1)} %multiply_convert_fusion), channel_id=1, source_target_pairs={{0,5},{1,4},{2,7},{3,6},{4,1},{5,0},{6,3},{7,2},{8,13},{9,12},{10,... | collective-permute-start | bytes 98312 | tf_op jit(solution)/shard_map/ppermute | solution.py:242

commit v4 on v3

--- a/solution.py
+++ b/solution.py
@@ -94,6 +94,9 @@
     return total
 
 
+PLACE, PACK, PREPARE = 2 * 10**9, 10**9, 10**9
+
+
 def place_of(tiles_ref, step, tiles_per, core=0):
     tile = tiles_ref[step]
     mine = lax.div(tile, tiles_per) == lax.bitwise_xor(lax.axis_index("feat"), core)
@@ -108,32 +111,44 @@
         copy.wait()
 
 
-def pack_kernel(marks_ref, points_ref, other_ref, duals_ref, batch_ref, static_ref):
-    depth, count = points_ref.shape
+def place_kernel(tiles_hbm, points_hbm, duals_hbm, marks_ref, static_ref, tiles_ref, points_ref, duals_ref, sems):
+    fetch([(tiles_hbm, tiles_ref), (points_hbm, points_ref), (duals_hbm, duals_ref)], sems)
+    count = points_ref.shape[1]
     values = duals_ref.shape[0]
+    columns = lax.broadcasted_iota(jnp.int32, (8, count), 1)
+    for core in range(2):
+        for step in range(2):
+            mine, where = place_of(tiles_ref, step, count // TILE, core)
+            inside = (columns >= where.start) & (columns < where.start + TILE)
+            row = 8 * (step + 2 * core)
+            marks_ref[row : row + 8, :] = jnp.where(mine & inside, 1.0, 0.0)
+    static_ref[:values, :] = duals_ref[...].astype(bf16)
+    static_ref[values:, :] = points_ref[...]
+
+
+def pack_kernel(marks_ref, static_ref, other_ref, batch_ref):
+    depth, count = other_ref.shape
+    values = static_ref.shape[0] - depth
     for step in range(2):
         rows = None
-        for core, from_ref in enumerate((points_ref, other_ref)):
+        for core, points in enumerate((static_ref[values:, :], other_ref[...])):
             row = 8 * (step + 2 * core)
-            kept = jnp.where(marks_ref[row : row + 1, :] > 0.0, from_ref[...].astype(f32), 0.0)
+            kept = jnp.where(marks_ref[row : row + 1, :] > 0.0, points.astype(f32), 0.0)
             for start in range(0, count, TILE):
                 piece = kept[:, start : start + TILE]
                 rows = piece if rows is None else rows + piece
         batch_ref[depth * step : depth * (step + 1), :] = rows.astype(bf16)
-    static_ref[:values, :] = duals_ref[...].astype(bf16)
-    static_ref[values:, :] = points_ref[...]
 
 
 def prepare_kernel(
-    tiles_hbm, freq_hbm, phase_hbm, weight_hbm, observed_hbm, noise_hbm, velocity_hbm, duals_hbm, points_hbm,
-    angle_ref, weight_ref, base_ref, later_ref, marks_ref, velocity_ref, duals_ref, points_ref,
-    tiles_ref, freq_ref, phase_ref, observed_ref, noise_ref, sems,
+    freq_hbm, phase_hbm, weight_hbm, observed_hbm, noise_hbm, velocity_hbm, duals_hbm, marks_ref,
+    angle_ref, weight_ref, base_ref, velocity_ref, duals_ref,
+    freq_ref, phase_ref, observed_ref, noise_ref, sems,
 ):
     fetch(
         [
-            (freq_hbm, freq_ref), (phase_hbm, phase_ref), (weight_hbm, weight_ref), (tiles_hbm, tiles_ref),
+            (freq_hbm, freq_ref), (phase_hbm, phase_ref), (weight_hbm, weight_ref),
             (observed_hbm, observed_ref), (noise_hbm, noise_ref), (velocity_hbm, velocity_ref), (duals_hbm, duals_ref),
-            (points_hbm, points_ref),
         ],
         sems,
     )
@@ -148,50 +163,57 @@
         tail = jnp.where(ids == k, part.astype(f32), tail)
     angle_ref[3 * depth :, :] = tail.astype(bf16)
 
-    count = velocity_ref.shape[1]
-    columns = lax.broadcasted_iota(jnp.int32, (8, count), 1)
-    for step, share_ref in enumerate((base_ref, later_ref)):
-        mine, where = place_of(tiles_ref, step, count // TILE)
-        share = step_size * (observed_ref[0:1, where] - noise_ref[:, where])
-        if step == 0:
-            share = share + momentum * velocity_ref[:, where]
-        share_ref[...] = jnp.where(mine, share, 0.0)
-        inside = (columns >= where.start) & (columns < where.start + TILE)
-        marks_ref[8 * step : 8 * (step + 1), :] = jnp.where(mine & inside, 1.0, 0.0)
-        mine, _ = place_of(tiles_ref, step, count // TILE, 1)
-        marks_ref[8 * (step + 2) : 8 * (step + 3), :] = jnp.where(mine & inside, 1.0, 0.0)
-
-
-def share_of(scales, upright, rows, angle_ref, weight_ref, base_ref, blocks):
-    inv_root, prior_scale = scales
-    kernel_part = kernel_sum(rows, blocks, rows.shape[1])
-    prior_part = prior_sum(upright, angle_ref, weight_ref)
-    return base_ref[...] - (step_size * inv_root) * kernel_part - (step_size * prior_scale) * prior_part
-
-
-def first_kernel(scales, parts, angle_ref, weight_ref, base_ref, *rest):
-    terms, blocks, (share_ref, send_ref, batch_ref) = rest[:parts], rest[parts:-3], rest[-3:]
+    values, count = velocity_ref.shape
+    data = step_size * (observed_ref[...] - noise_ref[...])
+    for step in range(2):
+        here = data + momentum * velocity_ref[...] if step == 0 else data
+        here = jnp.where(marks_ref[8 * step : 8 * step + 1, :] > 0.0, here, 0.0)
+        share = here[:, :TILE]
+        for start in range(TILE, count, TILE):
+            share = share + here[:, start : start + TILE]
+        base_ref[values * step : values * (step + 1), :] = share
+
+
+def stand_kernel(*refs):
+    terms, (batch_ref, upright_ref, rows_ref) = refs[:-3], refs[-3:]
     batch = terms[0][...]
     for term_ref in terms[1:]:
         batch = batch + term_ref[...]
     batch_ref[...] = batch
     depth = batch.shape[0] // 2
-    upright, rows = rows_of(batch[:depth])
-    share = share_of(scales, upright, rows, angle_ref, weight_ref, base_ref, blocks)
+    for step in range(2):
+        upright, rows = rows_of(batch[depth * step : depth * (step + 1)])
+        upright_ref[TILE * step : TILE * (step + 1), :] = upright
+        rows_ref[TILE * step : TILE * (step + 1), :] = rows
+
+
+def share_of(scales, step, upright_ref, rows_ref, angle_ref, weight_ref, base_ref, blocks):
+    inv_root, prior_scale = scales
+    cut = slice(TILE * step, TILE * (step + 1))
+    rows = rows_ref[cut, :]
+    kernel_part = kernel_sum(rows, blocks, rows.shape[1])
+    prior_part = prior_sum(upright_ref[cut, :], angle_ref, weight_ref)
+    values = prior_part.shape[0]
+    base = base_ref[values * step : values * (step + 1), :]
+    return base - (step_size * inv_root) * kernel_part - (step_size * prior_scale) * prior_part
+
+
+def first_kernel(scales, angle_ref, weight_ref, base_ref, batch_ref, upright_ref, rows_ref, *rest):
+    blocks, (share_ref, send_ref) = rest[:-2], rest[-2:]
+    share = share_of(scales, 0, upright_ref, rows_ref, angle_ref, weight_ref, base_ref, blocks)
     share_ref[...] = share
     send_ref[: share.shape[0], :] = share.astype(bf16)
-    send_ref[share.shape[0] :, :] = batch[:depth]
-
-
-def second_kernel(scales, angle_ref, weight_ref, later_ref, batch_ref, *rest):
+    send_ref[share.shape[0] :, :] = batch_ref[: batch_ref.shape[0] // 2, :]
+
+
+def second_kernel(scales, angle_ref, weight_ref, base_ref, upright_ref, rows_ref, *rest):
     blocks, share_ref = rest[:-1], rest[-1]
-    upright, rows = rows_of(batch_ref[batch_ref.shape[0] // 2 :, :])
-    share_ref[...] = share_of(scales, upright, rows, angle_ref, weight_ref, later_ref, blocks)
-
-
-def correct_kernel(scales, batch_ref, first_ref, second_ref, *rest):
+    share_ref[...] = share_of(scales, 1, upright_ref, rows_ref, angle_ref, weight_ref, base_ref, blocks)
+
+
+def correct_kernel(scales, rows_ref, first_ref, second_ref, *rest):
     blocks, total_ref = rest[:-1], rest[-1]
-    _, rows = rows_of(batch_ref[batch_ref.shape[0] // 2 :, :])
+    rows = rows_ref[TILE:, :]
     moved = kernel_sum(rows, blocks, rows.shape[1])
     values = first_ref.shape[0]
     total_ref[:values, :] = first_ref[...]
@@ -212,19 +234,15 @@
     new_duals_ref[...] = jnp.where(second, duals + moved, duals)
 
 
-def call(kernel, outs, *args, flops=0, name=None, from_hbm=False):
-    small, large = pltpu.SMEM, pltpu.VMEM
-    scratch = []
+def call(kernel, outs, *args, flops=0, name=None, from_hbm=(), scratch_for=()):
+    args = [pltpu.with_memory_space_constraint(a, pltpu.HBM) if k in from_hbm else a for k, a in enumerate(args)]
+    scratch = [(pltpu.SMEM if args[k].dtype == jnp.int32 else pltpu.VMEM)(args[k].shape, args[k].dtype) for k in scratch_for]
     if from_hbm:
-        small = large = pltpu.HBM
-        args = [pltpu.with_memory_space_constraint(a, pltpu.HBM) for a in args]
-        scratch = [
-            (pltpu.SMEM if a.dtype == jnp.int32 else pltpu.VMEM)(a.shape, a.dtype) for k, a in enumerate(args) if k not in from_hbm
-        ] + [pltpu.SemaphoreType.DMA((len(args),))]
+        scratch.append(pltpu.SemaphoreType.DMA((len(from_hbm),)))
     return pl.pallas_call(
         kernel,
         out_shape=[jax.ShapeDtypeStruct(shape, dtype) for shape, dtype in outs],
-        in_specs=[pl.BlockSpec(memory_space=small if a.dtype == jnp.int32 else large) for a in args],
+        in_specs=[pl.BlockSpec(memory_space=pltpu.HBM if k in from_hbm else pltpu.VMEM) for k in range(len(args))],
         out_specs=[pl.BlockSpec(memory_space=pltpu.VMEM)] * len(outs),
         scratch_shapes=scratch,
         compiler_params=pltpu.CompilerParams(vmem_limit_bytes=24 * 1024 * 1024),
@@ -266,44 +284,45 @@
 
     whole = (samples, count)
     other_points = other_core(points)
-    angles, weights, base, later, marks, velocity, duals, points = call(
+    marks, static = call(
+        place_kernel, [((32, count), f32), ((samples + depth, count), bf16)], tiles, points, duals,
+        name="place", from_hbm=(0, 1, 2), scratch_for=(0, 1, 2), flops=PLACE,
+    )
+    fixed = [static, swap(static, groups, members, 1, 1)]
+    (batch,) = call(pack_kernel, [((2 * depth, TILE), bf16)], marks, static, other_points, name="pack", flops=PACK)
+    angles, weights, base, velocity, duals = call(
         prepare_kernel,
-        [((ANGLE_ROWS, features), bf16), ((samples, features), bf16), (part, f32), (part, f32),
-         ((32, count), f32), (whole, f32), (whole, f32), ((depth, count), bf16)],
-        tiles, frequencies, phases, weights, observed, noise, velocity, duals, points,
-        name="prepare", from_hbm=(3, 6, 7, 8), flops=10**8,
-    )
-    batch, static = call(
-        pack_kernel, [((2 * depth, TILE), bf16), ((samples + depth, count), bf16)], marks, points, other_points, duals,
-        name="pack",
-    )
-    batch, fixed = [batch], [static]
-    chip_bit, group_bit = 2, 1
+        [((ANGLE_ROWS, features), bf16), ((samples, features), bf16), ((2 * samples, TILE), f32), (whole, f32), (whole, f32)],
+        frequencies, phases, weights, observed, noise, velocity, duals, marks,
+        name="prepare", from_hbm=(0, 1, 2, 3, 4, 5, 6), scratch_for=(0, 1, 3, 4), flops=PREPARE,
+    )
+    batch = [batch]
+    chip_bit, group_bit = 2, 2
     while chip_bit < members or group_bit < groups:
         if group_bit < groups:
-            wide = jnp.concatenate(fixed, axis=1) if len(fixed) > 1 else static
-            fixed.append(swap(wide, groups, members, group_bit, 1))
+            fixed.append(swap(jnp.concatenate(fixed, axis=1), groups, members, group_bit, 1))
         if chip_bit < members:
             whole_batch = sum(batch[1:], batch[0])
-            batch = [whole_batch, swap(whole_batch, groups, members, 0, chip_bit + 1)]
+            batch = [whole_batch, swap(whole_batch, groups, members, 0, members // chip_bit + 1)]
         if 2 * group_bit < groups and 2 * chip_bit < members:
             fixed[-1], batch[1] = lax.optimization_barrier((fixed[-1], batch[1]))
         chip_bit, group_bit = 2 * chip_bit, 2 * group_bit
-
-    share, send, batch = call(
-        functools.partial(first_kernel, scales, len(batch)),
-        [(part, f32), ((samples + depth, TILE), bf16), ((2 * depth, TILE), bf16)],
-        angles, weights, base, *batch, *fixed,
-        flops=10**9, name="first",
+    batch, upright, rows = call(
+        stand_kernel, [((2 * depth, TILE), bf16), ((2 * TILE, ANGLE_ROWS), bf16), ((2 * TILE, depth), f32)], *batch,
+        name="stand",
+    )
+    share, send = call(
+        functools.partial(first_kernel, scales), [(part, f32), ((samples + depth, TILE), bf16)],
+        angles, weights, base, batch, upright, rows, *fixed, flops=10**9, name="first",
     )
     moves = [send] + other_groups(send)
     (later,) = call(
-        functools.partial(second_kernel, scales), [(part, f32)], angles, weights, later, batch, *fixed,
+        functools.partial(second_kernel, scales), [(part, f32)], angles, weights, base, upright, rows, *fixed,
         flops=10**9, name="second",
     )
     (total,) = call(
         functools.partial(correct_kernel, scales), [((2 * samples, TILE), f32)],
-        batch, share, later, *moves, flops=10**8, name="correct",
+        rows, share, later, *moves, flops=10**8, name="correct",
     )
     total = total + other_core(total)
     bit = 2

time: 30.5 us -> 29.2 us (0.957)
  waiting for transfers between devices: 8.61 us -> 7.16 us
  Pallas kernels: 4.7 us -> 5.48 us
  starting transfers between devices: 16.2 us -> 15.6 us
    ppermute x11, waiting for transfers between devices: 8.61 us -> 7.16 us  [swap(): return lax.ppermute(array, ('grp', 'feat'), pairs)]
    pallas_call x6 -> x8, Pallas kernels: 4.7 us -> 5.48 us  [call(): pl.pallas_call(kernel, out_shape=[jax.ShapeDtypeStruct(shape, dtype) for...]
    ppermute x11, starting transfers between devices: 16.2 us -> 15.6 us  [swap(): return lax.ppermute(array, ('grp', 'feat'), pairs)]
  transfers between devices with their start and end apart: 11 -> 11, of which waited for: 6 -> 8; matrix products, arithmetic and copies ran while one was open for 0% -> 0% of each run, Pallas kernels for 8% -> 11%
where the time goes in v4:
time: 29.2 us; the launch traced here: 29 us
  starting transfers between devices  15.6 us (53%)
  waiting for transfers between devices  7.16 us (25%)
  Pallas kernels  5.48 us (19%)
  between operations  0.72 us (2%)
    ppermute x11, starting transfers between devices, swap(): return lax.ppermute(array, ('grp', 'feat'), pairs)  15.6 us
    ppermute x11, waiting for transfers between devices, swap(): return lax.ppermute(array, ('grp', 'feat'), pairs)  7.16 us
    pallas_call x8, Pallas kernels, call(): pl.pallas_call(kernel, out_shape=[jax.ShapeDtypeStruct(shape, dtype) for...  5.48 us
  transfers between devices with their start and end apart: 11, of which 8 were waited for; matrix products, arithmetic and copies ran while one was open for 0% of the time, Pallas kernels for 11%

profile of v4, /device:TPU:0, one launch (start us, length us, event | category | flops | bytes accessed | tf_op | source)
XLA Modules:
  0.0 29.0 jit_solution(261496197280593159)
XLA Ops:
  0.6 0.5 %collective-permute-start = (bf16[32,256]{1,0:T(8,128)(2,1)}, bf16[32,256]{1,0:T(8,128)(2,1)S(1)}, u32[]{:S(2)}, u32[]{:S(2)}) collective-permute-start(bf16[32,256]{1,0:T(8,128)(2,1)} %bitcast.17), channel_id=1, source_target_pairs={{0,1},{1,0},{2,3},{3,2},{4,5},{5,4},{6,7},{7,6},{8,9},{9,8},{10,11... | collective-permute-start | bytes 49160 | tf_op jit(solution)/shard_map/ppermute | solution.py:260
  1.1 0.9 %place.1 = (f32[32,256]{1,0:T(8,128)S(1)}, bf16[96,256]{1,0:T(8,128)(2,1)S(1)}) custom-call(s32[2]{0:T(128)} %bitcast.21, bf16[32,256]{1,0:T(8,128)(2,1)} %bitcast.18, f32[64,256]{1,0:T(8,128)} %bitcast.11), custom_call_target="tpu_custom_call" | custom-call | flops 2000000000 | bytes 81928 | tf_op jit(solution)/shard_map/place/pallas_call | solution.py:242
  2.1 2.7 %collective-permute-start.3 = (bf16[96,256]{1,0:T(8,128)(2,1)S(1)}, bf16[96,256]{1,0:T(8,128)(2,1)S(1)}, u32[]{:S(2)}, u32[]{:S(2)}) collective-permute-start(bf16[96,256]{1,0:T(8,128)(2,1)S(1)} %get-tuple-element.17.static_ref.rest_0_), channel_id=1, source_target_pairs={{0,9},{1,8},{2,11},{3,10},{4,13},{5,12},{6,15},{7,14},{8,1},{9,0},... | collective-permute-start | bytes 147464 | tf_op jit(solution)/shard_map/ppermute | solution.py:260
  4.7 0.0 collective-permute-done.other_ref
  4.7 2.3 %collective-permute-start.1 = (bf16[64,128]{1,0:T(8,128)(2,1)S(1)}, bf16[64,128]{1,0:T(8,128)(2,1)S(1)}, u32[]{:S(2)}, u32[]{:S(2)}) collective-permute-start(bf16[64,128]{1,0:T(8,128)(2,1)S(1)} %pack.1), channel_id=1, source_target_pairs={{0,5},{1,4},{2,7},{3,6},{4,1},{5,0},{6,3},{7,2},{8,13},{9,12},{10,... | collective-permute-start | bytes 49160 | tf_op jit(solution)/shard_map/ppermute | solution.py:260
  7.0 0.0 collective-permute-done.3.rest_1_
  7.0 1.7 %collective-permute-start.4 = (bf16[96,512]{1,0:T(8,128)(2,1)S(1)}, bf16[96,512]{1,0:T(8,128)(2,1)S(1)}, u32[]{:S(2)}, u32[]{:S(2)}) collective-permute-start(bf16[96,512]{1,0:T(8,128)(2,1)S(1)} %pad_maximum_fusion), channel_id=1, source_target_pairs={{0,17},{1,16},{2,19},{3,18},{4,21},{5,20},{6,23},{7,22},{8,25},{9,... | collective-permute-start | bytes 294920 | tf_op jit(solution)/shard_map/ppermute | solution.py:260
  8.7 0.2 collective-permute-done.1
  8.9 1.4 %collective-permute-start.2 = (bf16[64,128]{1,0:T(8,128)(2,1)S(1)}, bf16[64,128]{1,0:T(8,128)(2,1)S(1)}, u32[]{:S(2)}, u32[]{:S(2)}) collective-permute-start(bf16[64,128]{1,0:T(8,128)(2,1)S(1)} %add.12.refs_0_), channel_id=1, source_target_pairs={{0,3},{1,2},{2,1},{3,0},{4,7},{5,6},{6,5},{7,4},{8,11},{9,10},{10,... | collective-permute-start | bytes 49160 | tf_op jit(solution)/shard_map/ppermute | solution.py:260
  10.2 1.3 %prepare.1 = (bf16[128,2048]{1,0:T(8,128)(2,1)S(1)}, bf16[64,2048]{1,0:T(8,128)(2,1)S(1)}, f32[128,128]{1,0:T(8,128)S(1)}, f32[64,256]{1,0:T(8,128)S(1)}, f32[64,256]{1,0:T(8,128)S(1)}) custom-call(bf16[32,2048]{1,0:T(8,128)(2,1)} %freq_hbm.1, f32[1,2048]{1,0:T(1,128)} %bitcast.19, bf16[64,2048]{1,0:T(8,128)(2,1)} %bitcast.10, f32[1,256]{1,0:T(1,128)} %bitcast.20, ...), custom_call_target="tpu_custom_call" | custom-call | flops 1000000000 | bytes 631808 | tf_op jit(solution)/shard_map/prepare/pallas_call | solution.py:242
  11.5 0.6 %collective-permute-done.2.refs_1_ = bf16[64,128]{1,0:T(8,128)(2,1)S(1)} collective-permute-done((bf16[64,128]{1,0:T(8,128)(2,1)S(1)}, bf16[64,128]{1,0:T(8,128)(2,1)S(1)}, u32[]{:S(2)}, u32[]{:S(2)}) %collective-permute-start.2) | collective-permute-done | bytes 16416 | tf_op jit(solution)/shard_map/ppermute | solution.py:260
  12.1 0.1 stand.1
  12.2 0.0 collective-permute-done.4.rest_2_
  12.2 1.0 %first.1 = (f32[64,128]{1,0:T(8,128)S(1)}, bf16[96,128]{1,0:T(8,128)(2,1)S(1)}) custom-call(bf16[128,2048]{1,0:T(8,128)(2,1)S(1)} %get-tuple-element.19.angle_ref, bf16[64,2048]{1,0:T(8,128)(2,1)S(1)} %get-tuple-element.20.weight_ref, f32[128,128]{1,0:T(8,128)S(1)} %get-tuple-element.21.base_ref, bf16[64,128]{1,0:T(8,128)(2,1)S(1)} %get-tuple-element.22.batch_ref, ...), custom_call_target="tpu_custom_call" | custom-call | flops 1000000000 | bytes 1163264 | tf_op jit(solution)/shard_map/first/pallas_call | solution.py:242
  13.3 1.5 %collective-permute-start.7 = (bf16[96,128]{1,0:T(8,128)(2,1)S(1)}, bf16[96,128]{1,0:T(8,128)(2,1)S(1)}, u32[]{:S(2)}, u32[]{:S(2)}) collective-permute-start(bf16[96,128]{1,0:T(8,128)(2,1)S(1)} %get-tuple-element.25.rest_0_), channel_id=1, source_target_pairs={{0,25},{1,24},{2,27},{3,26},{4,29},{5,28},{6,31},{7,30},{8,17},{9,... | collective-permute-start | bytes 73736 | tf_op jit(solution)/shard_map/ppermute | solution.py:260
  14.8 0.7 %collective-permute-start.6 = (bf16[96,128]{1,0:T(8,128)(2,1)S(1)}, bf16[96,128]{1,0:T(8,128)(2,1)S(1)}, u32[]{:S(2)}, u32[]{:S(2)}) collective-permute-start(bf16[96,128]{1,0:T(8,128)(2,1)S(1)} %get-tuple-element.25.rest_0_), channel_id=1, source_target_pairs={{0,17},{1,16},{2,19},{3,18},{4,21},{5,20},{6,23},{7,22},{8,25},{9,... | collective-permute-start | bytes 73736 | tf_op jit(solution)/shard_map/ppermute | solution.py:260
  15.5 0.8 %collective-permute-start.5 = (bf16[96,128]{1,0:T(8,128)(2,1)S(1)}, bf16[96,128]{1,0:T(8,128)(2,1)S(1)}, u32[]{:S(2)}, u32[]{:S(2)}) collective-permute-start(bf16[96,128]{1,0:T(8,128)(2,1)S(1)} %get-tuple-element.25.rest_0_), channel_id=1, source_target_pairs={{0,9},{1,8},{2,11},{3,10},{4,13},{5,12},{6,15},{7,14},{8,1},{9,0},... | collective-permute-start | bytes 73736 | tf_op jit(solution)/shard_map/ppermute | solution.py:260
  16.3 1.0 %second.1.second_ref = f32[64,128]{1,0:T(8,128)S(1)} custom-call(bf16[128,2048]{1,0:T(8,128)(2,1)S(1)} %get-tuple-element.19.angle_ref, bf16[64,2048]{1,0:T(8,128)(2,1)S(1)} %get-tuple-element.20.weight_ref, f32[128,128]{1,0:T(8,128)S(1)} %get-tuple-element.21.base_ref, bf16[256,128]{1,0:T(8,128)(2,1)S(1)} %get-tuple-element.23.upright_ref, ...), custom_call_target="tpu_custom_call" | custom-call | flops 1000000000 | bytes 1146880 | tf_op jit(solution)/shard_map/second/pallas_call | solution.py:242
  17.3 0.2 collective-permute-done.7.rest_3_
  17.5 0.6 %collective-permute-done.6.rest_2_ = bf16[96,128]{1,0:T(8,128)(2,1)S(1)} collective-permute-done((bf16[96,128]{1,0:T(8,128)(2,1)S(1)}, bf16[96,128]{1,0:T(8,128)(2,1)S(1)}, u32[]{:S(2)}, u32[]{:S(2)}) %collective-permute-start.6) | collective-permute-done | bytes 24608 | tf_op jit(solution)/shard_map/ppermute | solution.py:260
  18.0 0.7 %collective-permute-done.5.rest_1_ = bf16[96,128]{1,0:T(8,128)(2,1)S(1)} collective-permute-done((bf16[96,128]{1,0:T(8,128)(2,1)S(1)}, bf16[96,128]{1,0:T(8,128)(2,1)S(1)}, u32[]{:S(2)}, u32[]{:S(2)}) %collective-permute-start.5) | collective-permute-done | bytes 24608 | tf_op jit(solution)/shard_map/ppermute | solution.py:260
  18.7 0.5 %correct.1 = f32[128,128]{1,0:T(8,128)S(1)} custom-call(f32[256,32]{1,0:T(8,128)S(1)} %get-tuple-element.18.rows_ref, f32[64,128]{1,0:T(8,128)S(1)} %get-tuple-element.24.first_ref, f32[64,128]{1,0:T(8,128)S(1)} %second.1.second_ref, bf16[96,128]{1,0:T(8,128)(2,1)S(1)} %get-tuple-element.25.rest_0_, bf16[96,128]{1,0:T(8,128)(2,1)S(1)} %collective-permute-done.5.rest_1_, ...), custom_call_target="tpu_custom_call" | custom-call | flops 100000000 | bytes 196608 | tf_op jit(solution)/shard_map/correct/pallas_call | solution.py:242
  19.2 0.2 collective-permute-start.8
  19.4 1.1 %collective-permute-done.8 = f32[128,128]{1,0:T(8,128)S(1)} collective-permute-done((f32[128,128]{1,0:T(8,128)S(1)}, f32[128,128]{1,0:T(8,128)S(1)}, u32[]{:S(2)}, u32[]{:S(2)}) %collective-permute-start.8) | collective-permute-done | bytes 65568 | tf_op jit(solution)/shard_map/ppermute | solution.py:260
  20.5 1.4 %collective-permute-start.9 = (f16[128,128]{1,0:T(8,128)(2,1)S(1)}, f16[128,128]{1,0:T(8,128)(2,1)S(1)}, u32[]{:S(2)}, u32[]{:S(2)}) collective-permute-start(f16[128,128]{1,0:T(8,128)(2,1)S(1)} %get-tuple-element.30), channel_id=1, source_target_pairs={{0,3},{1,2},{2,1},{3,0},{4,7},{5,6},{6,5},{7,4},{8,11},{9,10},{10,... | collective-permute-start | bytes 98312 | tf_op jit(solution)/shard_map/ppermute | solution.py:260
  21.9 2.0 %collective-permute-done.9 = f16[128,128]{1,0:T(8,128)(2,1)S(1)} collective-permute-done((f16[128,128]{1,0:T(8,128)(2,1)S(1)}, f16[128,128]{1,0:T(8,128)(2,1)S(1)}, u32[]{:S(2)}, u32[]{:S(2)}) %collective-permute-start.9) | collective-permute-done | bytes 32800 | tf_op jit(solution)/shard_map/ppermute | solution.py:260
  24.0 2.5 %collective-permute-start.10 = (f16[128,128]{1,0:T(8,128)(2,1)S(1)}, f16[128,128]{1,0:T(8,128)(2,1)S(1)}, u32[]{:S(2)}, u32[]{:S(2)}) collective-permute-start(f16[128,128]{1,0:T(8,128)(2,1)S(1)} %multiply_convert_fusion), channel_id=1, source_target_pairs={{0,5},{1,4},{2,7},{3,6},{4,1},{5,0},{6,3},{7,2},{8,13},{9,12},{10,... | collective-permute-start | bytes 98312 | tf_op jit(solution)/shard_map/ppermute | solution.py:260
  26.4 1.9 %collective-permute-done.10 = f16[128,128]{1,0:T(8,128)(2,1)S(1)} collective-permute-done((f16[128,128]{1,0:T(8,128)(2,1)S(1)}, f16[128,128]{1,0:T(8,128)(2,1)S(1)}, u32[]{:S(2)}, u32[]{:S(2)}) %collective-permute-start.10) | collective-permute-done | bytes 32800 | tf_op jit(solution)/shard_map/ppermute | solution.py:260
  28.3 0.7 %finish.1 = (f32[64,256]{1,0:T(8,128)}, f32[64,256]{1,0:T(8,128)}) custom-call(f32[32,256]{1,0:T(8,128)S(1)} %get-tuple-element.16.marks_ref, f32[128,128]{1,0:T(8,128)S(1)} %multiply_add_fusion.total_ref, f32[64,256]{1,0:T(8,128)S(1)} %get-tuple-element.26.duals_ref, f32[64,256]{1,0:T(8,128)S(1)} %get-tuple-element.27.velocity_ref), custom_call_target="tpu_custom_call" | custom-call | bytes 229376 | tf_op jit(solution)/shard_map/finish/pallas_call | solution.py:242
  (6 shorter events, 0.1 us)
Async XLA Ops:
  0.6 4.1 %collective-permute-start = (bf16[32,256]{1,0:T(8,128)(2,1)}, bf16[32,256]{1,0:T(8,128)(2,1)S(1)}, u32[]{:S(2)}, u32[]{:S(2)}) collective-permute-start(bf16[32,256]{1,0:T(8,128)(2,1)} %bitcast.17), channel_id=1, source_target_pairs={{0,1},{1,0},{2,3},{3,2},{4,5},{5,4},{6,7},{7,6},{8,9},{9,8},{10,11... | collective-permute-start | bytes 49160 | tf_op jit(solution)/shard_map/ppermute | solution.py:260
  2.1 5.0 %collective-permute-start.3 = (bf16[96,256]{1,0:T(8,128)(2,1)S(1)}, bf16[96,256]{1,0:T(8,128)(2,1)S(1)}, u32[]{:S(2)}, u32[]{:S(2)}) collective-permute-start(bf16[96,256]{1,0:T(8,128)(2,1)S(1)} %get-tuple-element.17.static_ref.rest_0_), channel_id=1, source_target_pairs={{0,9},{1,8},{2,11},{3,10},{4,13},{5,12},{6,15},{7,14},{8,1},{9,0},... | collective-permute-start | bytes 147464 | tf_op jit(solution)/shard_map/ppermute | solution.py:260
  4.7 4.1 %collective-permute-start.1 = (bf16[64,128]{1,0:T(8,128)(2,1)S(1)}, bf16[64,128]{1,0:T(8,128)(2,1)S(1)}, u32[]{:S(2)}, u32[]{:S(2)}) collective-permute-start(bf16[64,128]{1,0:T(8,128)(2,1)S(1)} %pack.1), channel_id=1, source_target_pairs={{0,5},{1,4},{2,7},{3,6},{4,1},{5,0},{6,3},{7,2},{8,13},{9,12},{10,... | collective-permute-start | bytes 49160 | tf_op jit(solution)/shard_map/ppermute | solution.py:260
  7.0 5.2 %collective-permute-start.4 = (bf16[96,512]{1,0:T(8,128)(2,1)S(1)}, bf16[96,512]{1,0:T(8,128)(2,1)S(1)}, u32[]{:S(2)}, u32[]{:S(2)}) collective-permute-start(bf16[96,512]{1,0:T(8,128)(2,1)S(1)} %pad_maximum_fusion), channel_id=1, source_target_pairs={{0,17},{1,16},{2,19},{3,18},{4,21},{5,20},{6,23},{7,22},{8,25},{9,... | collective-permute-start | bytes 294920 | tf_op jit(solution)/shard_map/ppermute | solution.py:260
  8.9 3.2 %collective-permute-start.2 = (bf16[64,128]{1,0:T(8,128)(2,1)S(1)}, bf16[64,128]{1,0:T(8,128)(2,1)S(1)}, u32[]{:S(2)}, u32[]{:S(2)}) collective-permute-start(bf16[64,128]{1,0:T(8,128)(2,1)S(1)} %add.12.refs_0_), channel_id=1, source_target_pairs={{0,3},{1,2},{2,1},{3,0},{4,7},{5,6},{6,5},{7,4},{8,11},{9,10},{10,... | collective-permute-start | bytes 49160 | tf_op jit(solution)/shard_map/ppermute | solution.py:260
  13.3 4.2 %collective-permute-start.7 = (bf16[96,128]{1,0:T(8,128)(2,1)S(1)}, bf16[96,128]{1,0:T(8,128)(2,1)S(1)}, u32[]{:S(2)}, u32[]{:S(2)}) collective-permute-start(bf16[96,128]{1,0:T(8,128)(2,1)S(1)} %get-tuple-element.25.rest_0_), channel_id=1, source_target_pairs={{0,25},{1,24},{2,27},{3,26},{4,29},{5,28},{6,31},{7,30},{8,17},{9,... | collective-permute-start | bytes 73736 | tf_op jit(solution)/shard_map/ppermute | solution.py:260
  14.8 3.3 %collective-permute-start.6 = (bf16[96,128]{1,0:T(8,128)(2,1)S(1)}, bf16[96,128]{1,0:T(8,128)(2,1)S(1)}, u32[]{:S(2)}, u32[]{:S(2)}) collective-permute-start(bf16[96,128]{1,0:T(8,128)(2,1)S(1)} %get-tuple-element.25.rest_0_), channel_id=1, source_target_pairs={{0,17},{1,16},{2,19},{3,18},{4,21},{5,20},{6,23},{7,22},{8,25},{9,... | collective-permute-start | bytes 73736 | tf_op jit(solution)/shard_map/ppermute | solution.py:260
  15.5 3.3 %collective-permute-start.5 = (bf16[96,128]{1,0:T(8,128)(2,1)S(1)}, bf16[96,128]{1,0:T(8,128)(2,1)S(1)}, u32[]{:S(2)}, u32[]{:S(2)}) collective-permute-start(bf16[96,128]{1,0:T(8,128)(2,1)S(1)} %get-tuple-element.25.rest_0_), channel_id=1, source_target_pairs={{0,9},{1,8},{2,11},{3,10},{4,13},{5,12},{6,15},{7,14},{8,1},{9,0},... | collective-permute-start | bytes 73736 | tf_op jit(solution)/shard_map/ppermute | solution.py:260
  19.2 1.3 %collective-permute-start.8 = (f32[128,128]{1,0:T(8,128)S(1)}, f32[128,128]{1,0:T(8,128)S(1)}, u32[]{:S(2)}, u32[]{:S(2)}) collective-permute-start(f32[128,128]{1,0:T(8,128)S(1)} %correct.1), channel_id=1, source_target_pairs={{0,1},{1,0},{2,3},{3,2},{4,5},{5,4},{6,7},{7,6},{8,9},{9,8},{10,11... | collective-permute-start | bytes 196616 | tf_op jit(solution)/shard_map/ppermute | solution.py:260
  20.5 3.4 %collective-permute-start.9 = (f16[128,128]{1,0:T(8,128)(2,1)S(1)}, f16[128,128]{1,0:T(8,128)(2,1)S(1)}, u32[]{:S(2)}, u32[]{:S(2)}) collective-permute-start(f16[128,128]{1,0:T(8,128)(2,1)S(1)} %get-tuple-element.30), channel_id=1, source_target_pairs={{0,3},{1,2},{2,1},{3,0},{4,7},{5,6},{6,5},{7,4},{8,11},{9,10},{10,... | collective-permute-start | bytes 98312 | tf_op jit(solution)/shard_map/ppermute | solution.py:260
  24.0 4.3 %collective-permute-start.10 = (f16[128,128]{1,0:T(8,128)(2,1)S(1)}, f16[128,128]{1,0:T(8,128)(2,1)S(1)}, u32[]{:S(2)}, u32[]{:S(2)}) collective-permute-start(f16[128,128]{1,0:T(8,128)(2,1)S(1)} %multiply_convert_fusion), channel_id=1, source_target_pairs={{0,5},{1,4},{2,7},{3,6},{4,1},{5,0},{6,3},{7,2},{8,13},{9,12},{10,... | collective-permute-start | bytes 98312 | tf_op jit(solution)/shard_map/ppermute | solution.py:260

commit v5 on v4

--- a/solution.py
+++ b/solution.py
@@ -94,7 +94,7 @@
     return total
 
 
-PLACE, PACK, PREPARE = 2 * 10**9, 10**9, 10**9
+PLACE, PACK, PREPARE, JOIN = 2 * 10**9, 10**9, 10**9, 3 * 10**9
 
 
 def place_of(tiles_ref, step, tiles_per, core=0):
@@ -211,13 +211,15 @@
     share_ref[...] = share_of(scales, 1, upright_ref, rows_ref, angle_ref, weight_ref, base_ref, blocks)
 
 
-def correct_kernel(scales, rows_ref, first_ref, second_ref, *rest):
-    blocks, total_ref = rest[:-1], rest[-1]
+def correct_kernel(scales, rows_ref, second_ref, *rest):
+    blocks, new_ref = rest[:-1], rest[-1]
     rows = rows_ref[TILE:, :]
-    moved = kernel_sum(rows, blocks, rows.shape[1])
-    values = first_ref.shape[0]
-    total_ref[:values, :] = first_ref[...]
-    total_ref[values:, :] = second_ref[...] - (step_size * scales[0]) * moved
+    new_ref[...] = second_ref[...] - (step_size * scales[0]) * kernel_sum(rows, blocks, rows.shape[1])
+
+
+def join_kernel(scales, rows_ref, block_ref, new_ref):
+    rows = rows_ref[TILE:, :]
+    new_ref[...] = (-step_size * scales[0]) * kernel_sum(rows, (block_ref,), rows.shape[1])
 
 
 def finish_kernel(marks_ref, total_ref, duals_ref, velocity_ref, new_duals_ref, new_velocity_ref):
@@ -247,7 +249,9 @@
         scratch_shapes=scratch,
         compiler_params=pltpu.CompilerParams(vmem_limit_bytes=24 * 1024 * 1024),
         cost_estimate=pl.CostEstimate(
-            flops=flops, bytes_accessed=sum(a.size * a.dtype.itemsize for a in args), transcendentals=0
+            flops=flops,
+            bytes_accessed=0 if flops == 0 else sum(a.size * a.dtype.itemsize for a in args),
+            transcendentals=0,
         ),
         name=name,
     )(*args)
@@ -315,16 +319,24 @@
         functools.partial(first_kernel, scales), [(part, f32), ((samples + depth, TILE), bf16)],
         angles, weights, base, batch, upright, rows, *fixed, flops=10**9, name="first",
     )
-    moves = [send] + other_groups(send)
+    summed = other_core(share)
+    moves = [send] + other_groups(send)[:-1]
+    share = share + summed
+    last = jnp.concatenate([share.astype(bf16), batch[:depth]], axis=0)
+    last, upright = lax.optimization_barrier((last, upright))
+    last = swap(last, groups, members, groups - 1, 1)
     (later,) = call(
         functools.partial(second_kernel, scales), [(part, f32)], angles, weights, base, upright, rows, *fixed,
-        flops=10**9, name="second",
-    )
-    (total,) = call(
-        functools.partial(correct_kernel, scales), [((2 * samples, TILE), f32)],
-        rows, share, later, *moves, flops=10**8, name="correct",
-    )
-    total = total + other_core(total)
+        flops=0, name="second",
+    )
+    (later,) = call(
+        functools.partial(correct_kernel, scales), [(part, f32)], rows, later, *moves, flops=0, name="correct"
+    )
+    other = other_core((later * SHRINK).astype(jnp.float16)).astype(f32) * (1.0 / SHRINK)
+    (joined,) = call(
+        functools.partial(join_kernel, scales), [(part, f32)], rows, last, flops=JOIN, name="join"
+    )
+    total = jnp.concatenate([share, later + other + joined], axis=0)
     bit = 2
     while bit < members:
         total = total + swap((total * SHRINK).astype(jnp.float16), groups, members, 0, bit + 1).astype(f32) * (1.0 / SHRINK)

time: 29.2 us -> 28.7 us (0.983)
  waiting for transfers between devices: 7.16 us -> 5.85 us
  starting transfers between devices: 15.6 us -> 16 us
    ppermute x11 -> x12, waiting for transfers between devices: 7.16 us -> 5.85 us  [swap(): return lax.ppermute(array, ('grp', 'feat'), pairs)]
    ppermute x11 -> x12, starting transfers between devices: 15.6 us -> 16 us  [swap(): return lax.ppermute(array, ('grp', 'feat'), pairs)]
    pallas_call x8 -> x9, Pallas kernels: 5.48 us -> 5.72 us  [call(): pl.pallas_call(kernel, out_shape=[jax.ShapeDtypeStruct(shape, dtype) for...]
  transfers between devices with their start and end apart: 11 -> 12, of which waited for: 8 -> 5; matrix products, arithmetic and copies ran while one was open for 0% -> 0% of each run, Pallas kernels for 11% -> 14%
where the time goes in v5:
time: 28.7 us; the launch traced here: 28.5 us
  starting transfers between devices  16 us (56%)
  waiting for transfers between devices  5.85 us (20%)
  Pallas kernels  5.72 us (20%)
  between operations  0.77 us (3%)
    ppermute x12, starting transfers between devices, swap(): return lax.ppermute(array, ('grp', 'feat'), pairs)  16 us
    ppermute x12, waiting for transfers between devices, swap(): return lax.ppermute(array, ('grp', 'feat'), pairs)  5.85 us
    pallas_call x9, Pallas kernels, call(): pl.pallas_call(kernel, out_shape=[jax.ShapeDtypeStruct(shape, dtype) for...  5.72 us
  transfers between devices with their start and end apart: 12, of which 5 were waited for; matrix products, arithmetic and copies ran while one was open for 0% of the time, Pallas kernels for 14%

profile of v5, /device:TPU:0, one launch (start us, length us, event | category | flops | bytes accessed | tf_op | source)
XLA Modules:
  0.0 28.5 jit_solution(10540148798924859477)
XLA Ops:
  0.6 0.5 %collective-permute-start = (bf16[32,256]{1,0:T(8,128)(2,1)}, bf16[32,256]{1,0:T(8,128)(2,1)S(1)}, u32[]{:S(2)}, u32[]{:S(2)}) collective-permute-start(bf16[32,256]{1,0:T(8,128)(2,1)} %bitcast.17), channel_id=1, source_target_pairs={{0,1},{1,0},{2,3},{3,2},{4,5},{5,4},{6,7},{7,6},{8,9},{9,8},{10,11... | collective-permute-start | bytes 49160 | tf_op jit(solution)/shard_map/ppermute | solution.py:264
  1.1 0.9 %place.1 = (f32[32,256]{1,0:T(8,128)S(1)}, bf16[96,256]{1,0:T(8,128)(2,1)S(1)}) custom-call(s32[2]{0:T(128)} %bitcast.21, bf16[32,256]{1,0:T(8,128)(2,1)} %bitcast.18, f32[64,256]{1,0:T(8,128)} %bitcast.11), custom_call_target="tpu_custom_call" | custom-call | flops 2000000000 | bytes 81928 | tf_op jit(solution)/shard_map/place/pallas_call | solution.py:244
  2.1 2.7 %collective-permute-start.3 = (bf16[96,256]{1,0:T(8,128)(2,1)S(1)}, bf16[96,256]{1,0:T(8,128)(2,1)S(1)}, u32[]{:S(2)}, u32[]{:S(2)}) collective-permute-start(bf16[96,256]{1,0:T(8,128)(2,1)S(1)} %get-tuple-element.22.static_ref.rest_0_), channel_id=1, source_target_pairs={{0,9},{1,8},{2,11},{3,10},{4,13},{5,12},{6,15},{7,14},{8,1},{9,0},... | collective-permute-start | bytes 147464 | tf_op jit(solution)/shard_map/ppermute | solution.py:264
  4.7 0.0 collective-permute-done.other_ref
  4.7 2.3 %collective-permute-start.1 = (bf16[64,128]{1,0:T(8,128)(2,1)S(1)}, bf16[64,128]{1,0:T(8,128)(2,1)S(1)}, u32[]{:S(2)}, u32[]{:S(2)}) collective-permute-start(bf16[64,128]{1,0:T(8,128)(2,1)S(1)} %pack.1), channel_id=1, source_target_pairs={{0,5},{1,4},{2,7},{3,6},{4,1},{5,0},{6,3},{7,2},{8,13},{9,12},{10,... | collective-permute-start | bytes 49160 | tf_op jit(solution)/shard_map/ppermute | solution.py:264
  7.0 0.0 collective-permute-done.3.rest_1_
  7.0 1.7 %collective-permute-start.4 = (bf16[96,512]{1,0:T(8,128)(2,1)S(1)}, bf16[96,512]{1,0:T(8,128)(2,1)S(1)}, u32[]{:S(2)}, u32[]{:S(2)}) collective-permute-start(bf16[96,512]{1,0:T(8,128)(2,1)S(1)} %pad_maximum_fusion), channel_id=1, source_target_pairs={{0,17},{1,16},{2,19},{3,18},{4,21},{5,20},{6,23},{7,22},{8,25},{9,... | collective-permute-start | bytes 294920 | tf_op jit(solution)/shard_map/ppermute | solution.py:264
  8.7 0.2 collective-permute-done.1
  8.9 1.4 %collective-permute-start.2 = (bf16[64,128]{1,0:T(8,128)(2,1)S(1)}, bf16[64,128]{1,0:T(8,128)(2,1)S(1)}, u32[]{:S(2)}, u32[]{:S(2)}) collective-permute-start(bf16[64,128]{1,0:T(8,128)(2,1)S(1)} %add.18.refs_0_), channel_id=1, source_target_pairs={{0,3},{1,2},{2,1},{3,0},{4,7},{5,6},{6,5},{7,4},{8,11},{9,10},{10,... | collective-permute-start | bytes 49160 | tf_op jit(solution)/shard_map/ppermute | solution.py:264
  10.2 1.3 %prepare.1 = (bf16[128,2048]{1,0:T(8,128)(2,1)S(1)}, bf16[64,2048]{1,0:T(8,128)(2,1)S(1)}, f32[128,128]{1,0:T(8,128)S(1)}, f32[64,256]{1,0:T(8,128)S(1)}, f32[64,256]{1,0:T(8,128)S(1)}) custom-call(bf16[32,2048]{1,0:T(8,128)(2,1)} %freq_hbm.1, f32[1,2048]{1,0:T(1,128)} %bitcast.19, bf16[64,2048]{1,0:T(8,128)(2,1)} %bitcast.10, f32[1,256]{1,0:T(1,128)} %bitcast.20, ...), custom_call_target="tpu_custom_call" | custom-call | flops 1000000000 | bytes 631808 | tf_op jit(solution)/shard_map/prepare/pallas_call | solution.py:244
  11.5 0.6 %collective-permute-done.2.refs_1_ = bf16[64,128]{1,0:T(8,128)(2,1)S(1)} collective-permute-done((bf16[64,128]{1,0:T(8,128)(2,1)S(1)}, bf16[64,128]{1,0:T(8,128)(2,1)S(1)}, u32[]{:S(2)}, u32[]{:S(2)}) %collective-permute-start.2) | collective-permute-done | bytes 16416 | tf_op jit(solution)/shard_map/ppermute | solution.py:264
  12.1 0.1 stand.1
  12.2 0.0 collective-permute-done.4.rest_2_
  12.2 1.0 %first.1 = (f32[64,128]{1,0:T(8,128)S(1)}, bf16[96,128]{1,0:T(8,128)(2,1)S(1)}) custom-call(bf16[128,2048]{1,0:T(8,128)(2,1)S(1)} %get-tuple-element.19.angle_ref, bf16[64,2048]{1,0:T(8,128)(2,1)S(1)} %get-tuple-element.20.weight_ref, f32[128,128]{1,0:T(8,128)S(1)} %get-tuple-element.21.base_ref, bf16[64,128]{1,0:T(8,128)(2,1)S(1)} %get-tuple-element.23.batch_ref, ...), custom_call_target="tpu_custom_call" | custom-call | flops 1000000000 | bytes 1163264 | tf_op jit(solution)/shard_map/first/pallas_call | solution.py:244
  13.3 0.2 collective-permute-start.5
  13.4 1.0 %collective-permute-start.6 = (bf16[96,128]{1,0:T(8,128)(2,1)S(1)}, bf16[96,128]{1,0:T(8,128)(2,1)S(1)}, u32[]{:S(2)}, u32[]{:S(2)}) collective-permute-start(bf16[96,128]{1,0:T(8,128)(2,1)S(1)} %get-tuple-element.28.rest_0_), channel_id=1, source_target_pairs={{0,9},{1,8},{2,11},{3,10},{4,13},{5,12},{6,15},{7,14},{8,1},{9,0},... | collective-permute-start | bytes 73736 | tf_op jit(solution)/shard_map/ppermute | solution.py:264
  14.4 1.1 %collective-permute-start.7 = (bf16[96,128]{1,0:T(8,128)(2,1)S(1)}, bf16[96,128]{1,0:T(8,128)(2,1)S(1)}, u32[]{:S(2)}, u32[]{:S(2)}) collective-permute-start(bf16[96,128]{1,0:T(8,128)(2,1)S(1)} %get-tuple-element.28.rest_0_), channel_id=1, source_target_pairs={{0,17},{1,16},{2,19},{3,18},{4,21},{5,20},{6,23},{7,22},{8,25},{9,... | collective-permute-start | bytes 73736 | tf_op jit(solution)/shard_map/ppermute | solution.py:264
  15.5 0.0 collective-permute-done.5
  15.5 1.3 %collective-permute-start.9 = (bf16[96,128]{1,0:T(8,128)(2,1)S(1)}, bf16[96,128]{1,0:T(8,128)(2,1)S(1)}, u32[]{:S(2)}, u32[]{:S(2)}) collective-permute-start(bf16[96,128]{1,0:T(8,128)(2,1)S(1)} %pad_maximum_fusion.2), channel_id=1, source_target_pairs={{0,25},{1,24},{2,27},{3,26},{4,29},{5,28},{6,31},{7,30},{8,17},{9,... | collective-permute-start | bytes 73736 | tf_op jit(solution)/shard_map/ppermute | solution.py:264
  16.7 1.0 %second.1.second_ref = f32[64,128]{1,0:T(8,128)S(1)} custom-call(bf16[128,2048]{1,0:T(8,128)(2,1)S(1)} %get-tuple-element.19.angle_ref, bf16[64,2048]{1,0:T(8,128)(2,1)S(1)} %get-tuple-element.20.weight_ref, f32[128,128]{1,0:T(8,128)S(1)} %get-tuple-element.21.base_ref, bf16[256,128]{1,0:T(8,128)(2,1)S(1)} %get-tuple-element.27.upright_ref, ...), custom_call_target="tpu_custom_call" | custom-call | tf_op jit(solution)/shard_map/second/pallas_call | solution.py:244
  17.8 0.0 collective-permute-done.6.rest_1_
  17.8 0.0 collective-permute-done.7.rest_2_
  17.8 0.5 %correct.1 = f32[64,128]{1,0:T(8,128)S(1)} custom-call(f32[256,32]{1,0:T(8,128)S(1)} %get-tuple-element.25.rows_ref, f32[64,128]{1,0:T(8,128)S(1)} %second.1.second_ref, bf16[96,128]{1,0:T(8,128)(2,1)S(1)} %get-tuple-element.28.rest_0_, bf16[96,128]{1,0:T(8,128)(2,1)S(1)} %collective-permute-done.6.rest_1_, bf16[96,128]{1,0:T(8,128)(2,1)S(1)} %collective-permute-done.7.rest_2_), custom_call_target="tpu_custom_call" | custom-call | tf_op jit(solution)/shard_map/correct/pallas_call | solution.py:244
  18.3 0.2 collective-permute-start.8
  18.5 1.2 %collective-permute-done.9.block_ref = bf16[96,128]{1,0:T(8,128)(2,1)S(1)} collective-permute-done((bf16[96,128]{1,0:T(8,128)(2,1)S(1)}, bf16[96,128]{1,0:T(8,128)(2,1)S(1)}, u32[]{:S(2)}, u32[]{:S(2)}) %collective-permute-start.9) | collective-permute-done | bytes 24608 | tf_op jit(solution)/shard_map/ppermute | solution.py:264
  19.7 0.3 join.1
  20.0 0.0 collective-permute-done.8
  20.0 1.4 %collective-permute-start.10 = (f16[128,128]{1,0:T(8,128)(2,1)S(1)}, f16[128,128]{1,0:T(8,128)(2,1)S(1)}, u32[]{:S(2)}, u32[]{:S(2)}) collective-permute-start(f16[128,128]{1,0:T(8,128)(2,1)S(1)} %multiply_convert_fusion.1), channel_id=1, source_target_pairs={{0,3},{1,2},{2,1},{3,0},{4,7},{5,6},{6,5},{7,4},{8,11},{9,10},{10,... | collective-permute-start | bytes 98312 | tf_op jit(solution)/shard_map/ppermute | solution.py:264
  21.4 2.0 %collective-permute-done.10 = f16[128,128]{1,0:T(8,128)(2,1)S(1)} collective-permute-done((f16[128,128]{1,0:T(8,128)(2,1)S(1)}, f16[128,128]{1,0:T(8,128)(2,1)S(1)}, u32[]{:S(2)}, u32[]{:S(2)}) %collective-permute-start.10) | collective-permute-done | bytes 32800 | tf_op jit(solution)/shard_map/ppermute | solution.py:264
  23.5 2.4 %collective-permute-start.11 = (f16[128,128]{1,0:T(8,128)(2,1)S(1)}, f16[128,128]{1,0:T(8,128)(2,1)S(1)}, u32[]{:S(2)}, u32[]{:S(2)}) collective-permute-start(f16[128,128]{1,0:T(8,128)(2,1)S(1)} %multiply_convert_fusion), channel_id=1, source_target_pairs={{0,5},{1,4},{2,7},{3,6},{4,1},{5,0},{6,3},{7,2},{8,13},{9,12},{10,... | collective-permute-start | bytes 98312 | tf_op jit(solution)/shard_map/ppermute | solution.py:264
  25.9 1.9 %collective-permute-done.11 = f16[128,128]{1,0:T(8,128)(2,1)S(1)} collective-permute-done((f16[128,128]{1,0:T(8,128)(2,1)S(1)}, f16[128,128]{1,0:T(8,128)(2,1)S(1)}, u32[]{:S(2)}, u32[]{:S(2)}) %collective-permute-start.11) | collective-permute-done | bytes 32800 | tf_op jit(solution)/shard_map/ppermute | solution.py:264
  27.8 0.7 %finish.1 = (f32[64,256]{1,0:T(8,128)}, f32[64,256]{1,0:T(8,128)}) custom-call(f32[32,256]{1,0:T(8,128)S(1)} %get-tuple-element.18.marks_ref, f32[128,128]{1,0:T(8,128)S(1)} %multiply_add_fusion.total_ref, f32[64,256]{1,0:T(8,128)S(1)} %get-tuple-element.30.duals_ref, f32[64,256]{1,0:T(8,128)S(1)} %get-tuple-element.31.velocity_ref), custom_call_target="tpu_custom_call" | custom-call | tf_op jit(solution)/shard_map/finish/pallas_call | solution.py:244
  (11 shorter events, 0.1 us)
Async XLA Ops:
  0.6 4.1 %collective-permute-start = (bf16[32,256]{1,0:T(8,128)(2,1)}, bf16[32,256]{1,0:T(8,128)(2,1)S(1)}, u32[]{:S(2)}, u32[]{:S(2)}) collective-permute-start(bf16[32,256]{1,0:T(8,128)(2,1)} %bitcast.17), channel_id=1, source_target_pairs={{0,1},{1,0},{2,3},{3,2},{4,5},{5,4},{6,7},{7,6},{8,9},{9,8},{10,11... | collective-permute-start | bytes 49160 | tf_op jit(solution)/shard_map/ppermute | solution.py:264
  2.1 5.0 %collective-permute-start.3 = (bf16[96,256]{1,0:T(8,128)(2,1)S(1)}, bf16[96,256]{1,0:T(8,128)(2,1)S(1)}, u32[]{:S(2)}, u32[]{:S(2)}) collective-permute-start(bf16[96,256]{1,0:T(8,128)(2,1)S(1)} %get-tuple-element.22.static_ref.rest_0_), channel_id=1, source_target_pairs={{0,9},{1,8},{2,11},{3,10},{4,13},{5,12},{6,15},{7,14},{8,1},{9,0},... | collective-permute-start | bytes 147464 | tf_op jit(solution)/shard_map/ppermute | solution.py:264
  4.7 4.1 %collective-permute-start.1 = (bf16[64,128]{1,0:T(8,128)(2,1)S(1)}, bf16[64,128]{1,0:T(8,128)(2,1)S(1)}, u32[]{:S(2)}, u32[]{:S(2)}) collective-permute-start(bf16[64,128]{1,0:T(8,128)(2,1)S(1)} %pack.1), channel_id=1, source_target_pairs={{0,5},{1,4},{2,7},{3,6},{4,1},{5,0},{6,3},{7,2},{8,13},{9,12},{10,... | collective-permute-start | bytes 49160 | tf_op jit(solution)/shard_map/ppermute | solution.py:264
  7.0 5.2 %collective-permute-start.4 = (bf16[96,512]{1,0:T(8,128)(2,1)S(1)}, bf16[96,512]{1,0:T(8,128)(2,1)S(1)}, u32[]{:S(2)}, u32[]{:S(2)}) collective-permute-start(bf16[96,512]{1,0:T(8,128)(2,1)S(1)} %pad_maximum_fusion), channel_id=1, source_target_pairs={{0,17},{1,16},{2,19},{3,18},{4,21},{5,20},{6,23},{7,22},{8,25},{9,... | collective-permute-start | bytes 294920 | tf_op jit(solution)/shard_map/ppermute | solution.py:264
  8.9 3.2 %collective-permute-start.2 = (bf16[64,128]{1,0:T(8,128)(2,1)S(1)}, bf16[64,128]{1,0:T(8,128)(2,1)S(1)}, u32[]{:S(2)}, u32[]{:S(2)}) collective-permute-start(bf16[64,128]{1,0:T(8,128)(2,1)S(1)} %add.18.refs_0_), channel_id=1, source_target_pairs={{0,3},{1,2},{2,1},{3,0},{4,7},{5,6},{6,5},{7,4},{8,11},{9,10},{10,... | collective-permute-start | bytes 49160 | tf_op jit(solution)/shard_map/ppermute | solution.py:264
  13.3 2.2 %collective-permute-start.5 = (f32[64,128]{1,0:T(8,128)S(1)}, f32[64,128]{1,0:T(8,128)S(1)}, u32[]{:S(2)}, u32[]{:S(2)}) collective-permute-start(f32[64,128]{1,0:T(8,128)S(1)} %get-tuple-element.26), channel_id=1, source_target_pairs={{0,1},{1,0},{2,3},{3,2},{4,5},{5,4},{6,7},{7,6},{8,9},{9,8},{10,11... | collective-permute-start | bytes 98312 | tf_op jit(solution)/shard_map/ppermute | solution.py:264
  13.4 4.3 %collective-permute-start.6 = (bf16[96,128]{1,0:T(8,128)(2,1)S(1)}, bf16[96,128]{1,0:T(8,128)(2,1)S(1)}, u32[]{:S(2)}, u32[]{:S(2)}) collective-permute-start(bf16[96,128]{1,0:T(8,128)(2,1)S(1)} %get-tuple-element.28.rest_0_), channel_id=1, source_target_pairs={{0,9},{1,8},{2,11},{3,10},{4,13},{5,12},{6,15},{7,14},{8,1},{9,0},... | collective-permute-start | bytes 73736 | tf_op jit(solution)/shard_map/ppermute | solution.py:264
  14.4 3.4 %collective-permute-start.7 = (bf16[96,128]{1,0:T(8,128)(2,1)S(1)}, bf16[96,128]{1,0:T(8,128)(2,1)S(1)}, u32[]{:S(2)}, u32[]{:S(2)}) collective-permute-start(bf16[96,128]{1,0:T(8,128)(2,1)S(1)} %get-tuple-element.28.rest_0_), channel_id=1, source_target_pairs={{0,17},{1,16},{2,19},{3,18},{4,21},{5,20},{6,23},{7,22},{8,25},{9,... | collective-permute-start | bytes 73736 | tf_op jit(solution)/shard_map/ppermute | solution.py:264
  15.5 4.2 %collective-permute-start.9 = (bf16[96,128]{1,0:T(8,128)(2,1)S(1)}, bf16[96,128]{1,0:T(8,128)(2,1)S(1)}, u32[]{:S(2)}, u32[]{:S(2)}) collective-permute-start(bf16[96,128]{1,0:T(8,128)(2,1)S(1)} %pad_maximum_fusion.2), channel_id=1, source_target_pairs={{0,25},{1,24},{2,27},{3,26},{4,29},{5,28},{6,31},{7,30},{8,17},{9,... | collective-permute-start | bytes 73736 | tf_op jit(solution)/shard_map/ppermute | solution.py:264
  18.3 1.7 %collective-permute-start.8 = (f16[64,128]{1,0:T(8,128)(2,1)S(1)}, f16[64,128]{1,0:T(8,128)(2,1)S(1)}, u32[]{:S(2)}, u32[]{:S(2)}) collective-permute-start(f16[64,128]{1,0:T(8,128)(2,1)S(1)} %multiply_convert_fusion.2), channel_id=1, source_target_pairs={{0,1},{1,0},{2,3},{3,2},{4,5},{5,4},{6,7},{7,6},{8,9},{9,8},{10,11... | collective-permute-start | bytes 49160 | tf_op jit(solution)/shard_map/ppermute | solution.py:264
  20.0 3.4 %collective-permute-start.10 = (f16[128,128]{1,0:T(8,128)(2,1)S(1)}, f16[128,128]{1,0:T(8,128)(2,1)S(1)}, u32[]{:S(2)}, u32[]{:S(2)}) collective-permute-start(f16[128,128]{1,0:T(8,128)(2,1)S(1)} %multiply_convert_fusion.1), channel_id=1, source_target_pairs={{0,3},{1,2},{2,1},{3,0},{4,7},{5,6},{6,5},{7,4},{8,11},{9,10},{10,... | collective-permute-start | bytes 98312 | tf_op jit(solution)/shard_map/ppermute | solution.py:264
  23.5 4.3 %collective-permute-start.11 = (f16[128,128]{1,0:T(8,128)(2,1)S(1)}, f16[128,128]{1,0:T(8,128)(2,1)S(1)}, u32[]{:S(2)}, u32[]{:S(2)}) collective-permute-start(f16[128,128]{1,0:T(8,128)(2,1)S(1)} %multiply_convert_fusion), channel_id=1, source_target_pairs={{0,5},{1,4},{2,7},{3,6},{4,1},{5,0},{6,3},{7,2},{8,13},{9,12},{10,... | collective-permute-start | bytes 98312 | tf_op jit(solution)/shard_map/ppermute | solution.py:264

commit v6 on v5

--- a/solution.py
+++ b/solution.py
@@ -11,6 +11,7 @@
 
 TILE = 128
 CHUNK = 256
+COLUMNS = 512
 
 amplitude = 4.0
 signal = 2.0
@@ -21,6 +22,7 @@
 bf16 = jnp.bfloat16
 
 SHRINK = 0.25
+
 
 def cos_terms():
     nodes = np.cos(np.pi * (np.arange(64) + 0.5) / 64)
@@ -71,7 +73,7 @@
     for block_ref in blocks:
         values = block_ref.shape[0] - depth
         size = block_ref.shape[1]
-        step = min(size, CHUNK)
+        step = min(size, COLUMNS)
         for start in range(0, size, step):
             cut = slice(start, start + step)
             points = block_ref[values:, cut]
@@ -97,12 +99,6 @@
 PLACE, PACK, PREPARE, JOIN = 2 * 10**9, 10**9, 10**9, 3 * 10**9
 
 
-def place_of(tiles_ref, step, tiles_per, core=0):
-    tile = tiles_ref[step]
-    mine = lax.div(tile, tiles_per) == lax.bitwise_xor(lax.axis_index("feat"), core)
-    return mine, pl.ds(pl.multiple_of(lax.rem(tile, tiles_per) * TILE, TILE), TILE)
-
-
 def fetch(pairs, sems):
     copies = [pltpu.make_async_copy(src, dst, sems.at[k]) for k, (src, dst) in enumerate(pairs)]
     for copy in copies:
@@ -117,11 +113,11 @@
     values = duals_ref.shape[0]
     columns = lax.broadcasted_iota(jnp.int32, (8, count), 1)
     for core in range(2):
+        member = lax.bitwise_xor(lax.axis_index("feat"), core)
         for step in range(2):
-            mine, where = place_of(tiles_ref, step, count // TILE, core)
-            inside = (columns >= where.start) & (columns < where.start + TILE)
+            place = columns + (member * count - tiles_ref[step] * TILE)
             row = 8 * (step + 2 * core)
-            marks_ref[row : row + 8, :] = jnp.where(mine & inside, 1.0, 0.0)
+            marks_ref[row : row + 8, :] = jnp.where((place >= 0) & (place < TILE), 1.0, 0.0)
     static_ref[:values, :] = duals_ref[...].astype(bf16)
     static_ref[values:, :] = points_ref[...]
 
@@ -264,6 +260,15 @@
     return lax.ppermute(array, ("grp", "feat"), pairs)
 
 
+def two_ways(array, groups, members, rounds, turn):
+    pairs = []
+    for member in range(members):
+        even = bin(member).count("1") % 2 == 0
+        bit = 2 << (turn if even else rounds - 1 - turn)
+        pairs += [(g * members + member, g * members + (member ^ (bit + 1))) for g in range(groups)]
+    return lax.ppermute(array, ("grp", "feat"), pairs)
+
+
 def local(points, dual_weights, velocity, observed, noise_draws, frequencies, phases, prior_weights, batch_tiles):
     groups = lax.axis_size("grp")
     members = lax.axis_size("feat")
@@ -280,9 +285,6 @@
     def other_core(array):
         return swap(array, groups, members, 0, 1)
 
-    def other_chips(array):
-        return [swap(array, groups, members, 0, 2 * k + 1) for k in range(1, members // 2)]
-
     def other_groups(array):
         return [swap(array, groups, members, k, 1) for k in range(1, groups)]
 
@@ -304,7 +306,8 @@
     chip_bit, group_bit = 2, 2
     while chip_bit < members or group_bit < groups:
         if group_bit < groups:
-            fixed.append(swap(jnp.concatenate(fixed, axis=1), groups, members, group_bit, 1))
+            near = jnp.concatenate(fixed, axis=1)
+            fixed = [near, swap(near, groups, members, group_bit, 1)]
         if chip_bit < members:
             whole_batch = sum(batch[1:], batch[0])
             batch = [whole_batch, swap(whole_batch, groups, members, 0, members // chip_bit + 1)]
@@ -337,10 +340,10 @@
         functools.partial(join_kernel, scales), [(part, f32)], rows, last, flops=JOIN, name="join"
     )
     total = jnp.concatenate([share, later + other + joined], axis=0)
-    bit = 2
-    while bit < members:
-        total = total + swap((total * SHRINK).astype(jnp.float16), groups, members, 0, bit + 1).astype(f32) * (1.0 / SHRINK)
-        bit *= 2
+    rounds = members.bit_length() - 2
+    for turn in range(rounds):
+        small = two_ways((total * SHRINK).astype(jnp.float16), groups, members, rounds, turn)
+        total = total + small.astype(f32) * (1.0 / SHRINK)
     new_duals, new_velocity = call(
         finish_kernel, [(whole, f32)] * 2, marks, total, duals, velocity, name="finish"
     )

time: 28.7 us -> 28.5 us (level)
    ppermute x0 -> x2, starting transfers between devices: none -> 4 us  [two_ways(): return lax.ppermute(array, ('grp', 'feat'), pairs)]
    ppermute x12 -> x10, starting transfers between devices: 16 us -> 12.1 us  [swap(): return lax.ppermute(array, ('grp', 'feat'), pairs)]
    ppermute x12 -> x10, waiting for transfers between devices: 5.85 us -> 2 us  [swap(): return lax.ppermute(array, ('grp', 'feat'), pairs)]
    ppermute x0 -> x2, waiting for transfers between devices: none -> 3.71 us  [two_ways(): return lax.ppermute(array, ('grp', 'feat'), pairs)]
where the time goes in v6:
time: 28.5 us; the launch traced here: 28.3 us
  starting transfers between devices  16.1 us (56%)
  waiting for transfers between devices  5.71 us (20%)
  Pallas kernels  5.62 us (20%)
  between operations  0.77 us (3%)
    ppermute x10, starting transfers between devices, swap(): return lax.ppermute(array, ('grp', 'feat'), pairs)  12.1 us
    pallas_call x9, Pallas kernels, call(): pl.pallas_call(kernel, out_shape=[jax.ShapeDtypeStruct(shape, dtype) for...  5.62 us
    ppermute x2, starting transfers between devices, two_ways(): return lax.ppermute(array, ('grp', 'feat'), pairs)  4 us
    ppermute x2, waiting for transfers between devices, two_ways(): return lax.ppermute(array, ('grp', 'feat'), pairs)  3.71 us
    ppermute x10, waiting for transfers between devices, swap(): return lax.ppermute(array, ('grp', 'feat'), pairs)  2 us
  transfers between devices with their start and end apart: 12, of which 5 were waited for; matrix products, arithmetic and copies ran while one was open for 0% of the time, Pallas kernels for 14%

profile of v6, /device:TPU:0, one launch (start us, length us, event | category | flops | bytes accessed | tf_op | source)
XLA Modules:
  0.0 28.3 jit_solution(8665803713309157730)
XLA Ops:
  0.6 0.5 %collective-permute-start = (bf16[32,256]{1,0:T(8,128)(2,1)}, bf16[32,256]{1,0:T(8,128)(2,1)S(1)}, u32[]{:S(2)}, u32[]{:S(2)}) collective-permute-start(bf16[32,256]{1,0:T(8,128)(2,1)} %bitcast.17), channel_id=1, source_target_pairs={{0,1},{1,0},{2,3},{3,2},{4,5},{5,4},{6,7},{7,6},{8,9},{9,8},{10,11... | collective-permute-start | bytes 49160 | tf_op jit(solution)/shard_map/ppermute | solution.py:260
  1.1 0.9 %place.1 = (f32[32,256]{1,0:T(8,128)S(1)}, bf16[96,256]{1,0:T(8,128)(2,1)S(1)}) custom-call(s32[2]{0:T(128)} %bitcast.21, bf16[32,256]{1,0:T(8,128)(2,1)} %bitcast.18, f32[64,256]{1,0:T(8,128)} %bitcast.11), custom_call_target="tpu_custom_call" | custom-call | flops 2000000000 | bytes 81928 | tf_op jit(solution)/shard_map/place/pallas_call | solution.py:240
  2.1 2.7 %collective-permute-start.3 = (bf16[96,256]{1,0:T(8,128)(2,1)S(1)}, bf16[96,256]{1,0:T(8,128)(2,1)S(1)}, u32[]{:S(2)}, u32[]{:S(2)}) collective-permute-start(bf16[96,256]{1,0:T(8,128)(2,1)S(1)} %get-tuple-element.22.static_ref), channel_id=1, source_target_pairs={{0,9},{1,8},{2,11},{3,10},{4,13},{5,12},{6,15},{7,14},{8,1},{9,0},... | collective-permute-start | bytes 147464 | tf_op jit(solution)/shard_map/ppermute | solution.py:260
  4.7 0.0 collective-permute-done.other_ref
  4.7 2.3 %collective-permute-start.1 = (bf16[64,128]{1,0:T(8,128)(2,1)S(1)}, bf16[64,128]{1,0:T(8,128)(2,1)S(1)}, u32[]{:S(2)}, u32[]{:S(2)}) collective-permute-start(bf16[64,128]{1,0:T(8,128)(2,1)S(1)} %pack.1), channel_id=1, source_target_pairs={{0,5},{1,4},{2,7},{3,6},{4,1},{5,0},{6,3},{7,2},{8,13},{9,12},{10,... | collective-permute-start | bytes 49160 | tf_op jit(solution)/shard_map/ppermute | solution.py:260
  7.0 0.0 collective-permute-done.3
  7.0 1.7 %collective-permute-start.4 = (bf16[96,512]{1,0:T(8,128)(2,1)S(1)}, bf16[96,512]{1,0:T(8,128)(2,1)S(1)}, u32[]{:S(2)}, u32[]{:S(2)}) collective-permute-start(bf16[96,512]{1,0:T(8,128)(2,1)S(1)} %constant_dynamic-update-slice_fusion.rest_0_), channel_id=1, source_target_pairs={{0,17},{1,16},{2,19},{3,18},{4,21},{5,20},{6,23},{7,22},{8,25},{9,... | collective-permute-start | bytes 294920 | tf_op jit(solution)/shard_map/ppermute | solution.py:260
  8.7 0.2 collective-permute-done.1
  8.9 1.4 %collective-permute-start.2 = (bf16[64,128]{1,0:T(8,128)(2,1)S(1)}, bf16[64,128]{1,0:T(8,128)(2,1)S(1)}, u32[]{:S(2)}, u32[]{:S(2)}) collective-permute-start(bf16[64,128]{1,0:T(8,128)(2,1)S(1)} %add.18.refs_0_), channel_id=1, source_target_pairs={{0,3},{1,2},{2,1},{3,0},{4,7},{5,6},{6,5},{7,4},{8,11},{9,10},{10,... | collective-permute-start | bytes 49160 | tf_op jit(solution)/shard_map/ppermute | solution.py:260
  10.2 1.3 %prepare.1 = (bf16[128,2048]{1,0:T(8,128)(2,1)S(1)}, bf16[64,2048]{1,0:T(8,128)(2,1)S(1)}, f32[128,128]{1,0:T(8,128)S(1)}, f32[64,256]{1,0:T(8,128)S(1)}, f32[64,256]{1,0:T(8,128)S(1)}) custom-call(bf16[32,2048]{1,0:T(8,128)(2,1)} %freq_hbm.1, f32[1,2048]{1,0:T(1,128)} %bitcast.19, bf16[64,2048]{1,0:T(8,128)(2,1)} %bitcast.10, f32[1,256]{1,0:T(1,128)} %bitcast.20, ...), custom_call_target="tpu_custom_call" | custom-call | flops 1000000000 | bytes 631808 | tf_op jit(solution)/shard_map/prepare/pallas_call | solution.py:240
  11.5 0.6 %collective-permute-done.2.refs_1_ = bf16[64,128]{1,0:T(8,128)(2,1)S(1)} collective-permute-done((bf16[64,128]{1,0:T(8,128)(2,1)S(1)}, bf16[64,128]{1,0:T(8,128)(2,1)S(1)}, u32[]{:S(2)}, u32[]{:S(2)}) %collective-permute-start.2) | collective-permute-done | bytes 16416 | tf_op jit(solution)/shard_map/ppermute | solution.py:260
  12.1 0.1 stand.1
  12.2 0.0 collective-permute-done.4.rest_1_
  12.2 1.0 %first.1 = (f32[64,128]{1,0:T(8,128)S(1)}, bf16[96,128]{1,0:T(8,128)(2,1)S(1)}) custom-call(bf16[128,2048]{1,0:T(8,128)(2,1)S(1)} %get-tuple-element.19.angle_ref, bf16[64,2048]{1,0:T(8,128)(2,1)S(1)} %get-tuple-element.20.weight_ref, f32[128,128]{1,0:T(8,128)S(1)} %get-tuple-element.21.base_ref, bf16[64,128]{1,0:T(8,128)(2,1)S(1)} %get-tuple-element.23.batch_ref, ...), custom_call_target="tpu_custom_call" | custom-call | flops 1000000000 | bytes 1163264 | tf_op jit(solution)/shard_map/first/pallas_call | solution.py:240
  13.2 0.2 collective-permute-start.5
  13.4 0.9 %collective-permute-start.6 = (bf16[96,128]{1,0:T(8,128)(2,1)S(1)}, bf16[96,128]{1,0:T(8,128)(2,1)S(1)}, u32[]{:S(2)}, u32[]{:S(2)}) collective-permute-start(bf16[96,128]{1,0:T(8,128)(2,1)S(1)} %get-tuple-element.28.rest_0_), channel_id=1, source_target_pairs={{0,9},{1,8},{2,11},{3,10},{4,13},{5,12},{6,15},{7,14},{8,1},{9,0},... | collective-permute-start | bytes 73736 | tf_op jit(solution)/shard_map/ppermute | solution.py:260
  14.3 1.0 %collective-permute-start.7 = (bf16[96,128]{1,0:T(8,128)(2,1)S(1)}, bf16[96,128]{1,0:T(8,128)(2,1)S(1)}, u32[]{:S(2)}, u32[]{:S(2)}) collective-permute-start(bf16[96,128]{1,0:T(8,128)(2,1)S(1)} %get-tuple-element.28.rest_0_), channel_id=1, source_target_pairs={{0,17},{1,16},{2,19},{3,18},{4,21},{5,20},{6,23},{7,22},{8,25},{9,... | collective-permute-start | bytes 73736 | tf_op jit(solution)/shard_map/ppermute | solution.py:260
  15.3 0.0 collective-permute-done.5
  15.4 1.4 %collective-permute-start.9 = (bf16[96,128]{1,0:T(8,128)(2,1)S(1)}, bf16[96,128]{1,0:T(8,128)(2,1)S(1)}, u32[]{:S(2)}, u32[]{:S(2)}) collective-permute-start(bf16[96,128]{1,0:T(8,128)(2,1)S(1)} %pad_maximum_fusion.1), channel_id=1, source_target_pairs={{0,25},{1,24},{2,27},{3,26},{4,29},{5,28},{6,31},{7,30},{8,17},{9,... | collective-permute-start | bytes 73736 | tf_op jit(solution)/shard_map/ppermute | solution.py:260
  16.7 1.0 %second.1.second_ref = f32[64,128]{1,0:T(8,128)S(1)} custom-call(bf16[128,2048]{1,0:T(8,128)(2,1)S(1)} %get-tuple-element.19.angle_ref, bf16[64,2048]{1,0:T(8,128)(2,1)S(1)} %get-tuple-element.20.weight_ref, f32[128,128]{1,0:T(8,128)S(1)} %get-tuple-element.21.base_ref, bf16[256,128]{1,0:T(8,128)(2,1)S(1)} %get-tuple-element.27.upright_ref, ...), custom_call_target="tpu_custom_call" | custom-call | tf_op jit(solution)/shard_map/second/pallas_call | solution.py:240
  17.7 0.0 collective-permute-done.6.rest_1_
  17.7 0.0 collective-permute-done.7.rest_2_
  17.7 0.5 %correct.1 = f32[64,128]{1,0:T(8,128)S(1)} custom-call(f32[256,32]{1,0:T(8,128)S(1)} %get-tuple-element.25.rows_ref, f32[64,128]{1,0:T(8,128)S(1)} %second.1.second_ref, bf16[96,128]{1,0:T(8,128)(2,1)S(1)} %get-tuple-element.28.rest_0_, bf16[96,128]{1,0:T(8,128)(2,1)S(1)} %collective-permute-done.6.rest_1_, bf16[96,128]{1,0:T(8,128)(2,1)S(1)} %collective-permute-done.7.rest_2_), custom_call_target="tpu_custom_call" | custom-call | tf_op jit(solution)/shard_map/correct/pallas_call | solution.py:240
  18.2 0.1 collective-permute-start.8
  18.4 1.2 %collective-permute-done.9.block_ref = bf16[96,128]{1,0:T(8,128)(2,1)S(1)} collective-permute-done((bf16[96,128]{1,0:T(8,128)(2,1)S(1)}, bf16[96,128]{1,0:T(8,128)(2,1)S(1)}, u32[]{:S(2)}, u32[]{:S(2)}) %collective-permute-start.9) | collective-permute-done | bytes 24608 | tf_op jit(solution)/shard_map/ppermute | solution.py:260
  19.6 0.3 join.1
  19.8 0.0 collective-permute-done.8
  19.9 1.5 %collective-permute-start.10 = (f16[128,128]{1,0:T(8,128)(2,1)S(1)}, f16[128,128]{1,0:T(8,128)(2,1)S(1)}, u32[]{:S(2)}, u32[]{:S(2)}) collective-permute-start(f16[128,128]{1,0:T(8,128)(2,1)S(1)} %multiply_convert_fusion.1), channel_id=1, source_target_pairs={{0,3},{8,11},{16,19},{24,27},{1,4},{9,12},{17,20},{25,28},{2,7},{1... | collective-permute-start | bytes 98312 | tf_op jit(solution)/shard_map/ppermute | solution.py:269
  21.4 1.9 %collective-permute-done.10 = f16[128,128]{1,0:T(8,128)(2,1)S(1)} collective-permute-done((f16[128,128]{1,0:T(8,128)(2,1)S(1)}, f16[128,128]{1,0:T(8,128)(2,1)S(1)}, u32[]{:S(2)}, u32[]{:S(2)}) %collective-permute-start.10) | collective-permute-done | bytes 32800 | tf_op jit(solution)/shard_map/ppermute | solution.py:269
  23.3 2.5 %collective-permute-start.11 = (f16[128,128]{1,0:T(8,128)(2,1)S(1)}, f16[128,128]{1,0:T(8,128)(2,1)S(1)}, u32[]{:S(2)}, u32[]{:S(2)}) collective-permute-start(f16[128,128]{1,0:T(8,128)(2,1)S(1)} %multiply_convert_fusion), channel_id=1, source_target_pairs={{0,5},{8,13},{16,21},{24,29},{1,2},{9,10},{17,18},{25,26},{2,1},{1... | collective-permute-start | bytes 98312 | tf_op jit(solution)/shard_map/ppermute | solution.py:269
  25.9 1.8 %collective-permute-done.11 = f16[128,128]{1,0:T(8,128)(2,1)S(1)} collective-permute-done((f16[128,128]{1,0:T(8,128)(2,1)S(1)}, f16[128,128]{1,0:T(8,128)(2,1)S(1)}, u32[]{:S(2)}, u32[]{:S(2)}) %collective-permute-start.11) | collective-permute-done | bytes 32800 | tf_op jit(solution)/shard_map/ppermute | solution.py:269
  27.7 0.7 %finish.1 = (f32[64,256]{1,0:T(8,128)}, f32[64,256]{1,0:T(8,128)}) custom-call(f32[32,256]{1,0:T(8,128)S(1)} %get-tuple-element.18.marks_ref, f32[128,128]{1,0:T(8,128)S(1)} %multiply_add_fusion.total_ref, f32[64,256]{1,0:T(8,128)S(1)} %get-tuple-element.30.duals_ref, f32[64,256]{1,0:T(8,128)S(1)} %get-tuple-element.31.velocity_ref), custom_call_target="tpu_custom_call" | custom-call | tf_op jit(solution)/shard_map/finish/pallas_call | solution.py:240
  (12 shorter events, 0.1 us)
Async XLA Ops:
  0.6 4.1 %collective-permute-start = (bf16[32,256]{1,0:T(8,128)(2,1)}, bf16[32,256]{1,0:T(8,128)(2,1)S(1)}, u32[]{:S(2)}, u32[]{:S(2)}) collective-permute-start(bf16[32,256]{1,0:T(8,128)(2,1)} %bitcast.17), channel_id=1, source_target_pairs={{0,1},{1,0},{2,3},{3,2},{4,5},{5,4},{6,7},{7,6},{8,9},{9,8},{10,11... | collective-permute-start | bytes 49160 | tf_op jit(solution)/shard_map/ppermute | solution.py:260
  2.1 5.0 %collective-permute-start.3 = (bf16[96,256]{1,0:T(8,128)(2,1)S(1)}, bf16[96,256]{1,0:T(8,128)(2,1)S(1)}, u32[]{:S(2)}, u32[]{:S(2)}) collective-permute-start(bf16[96,256]{1,0:T(8,128)(2,1)S(1)} %get-tuple-element.22.static_ref), channel_id=1, source_target_pairs={{0,9},{1,8},{2,11},{3,10},{4,13},{5,12},{6,15},{7,14},{8,1},{9,0},... | collective-permute-start | bytes 147464 | tf_op jit(solution)/shard_map/ppermute | solution.py:260
  4.7 4.1 %collective-permute-start.1 = (bf16[64,128]{1,0:T(8,128)(2,1)S(1)}, bf16[64,128]{1,0:T(8,128)(2,1)S(1)}, u32[]{:S(2)}, u32[]{:S(2)}) collective-permute-start(bf16[64,128]{1,0:T(8,128)(2,1)S(1)} %pack.1), channel_id=1, source_target_pairs={{0,5},{1,4},{2,7},{3,6},{4,1},{5,0},{6,3},{7,2},{8,13},{9,12},{10,... | collective-permute-start | bytes 49160 | tf_op jit(solution)/shard_map/ppermute | solution.py:260
  7.0 5.2 %collective-permute-start.4 = (bf16[96,512]{1,0:T(8,128)(2,1)S(1)}, bf16[96,512]{1,0:T(8,128)(2,1)S(1)}, u32[]{:S(2)}, u32[]{:S(2)}) collective-permute-start(bf16[96,512]{1,0:T(8,128)(2,1)S(1)} %constant_dynamic-update-slice_fusion.rest_0_), channel_id=1, source_target_pairs={{0,17},{1,16},{2,19},{3,18},{4,21},{5,20},{6,23},{7,22},{8,25},{9,... | collective-permute-start | bytes 294920 | tf_op jit(solution)/shard_map/ppermute | solution.py:260
  8.9 3.2 %collective-permute-start.2 = (bf16[64,128]{1,0:T(8,128)(2,1)S(1)}, bf16[64,128]{1,0:T(8,128)(2,1)S(1)}, u32[]{:S(2)}, u32[]{:S(2)}) collective-permute-start(bf16[64,128]{1,0:T(8,128)(2,1)S(1)} %add.18.refs_0_), channel_id=1, source_target_pairs={{0,3},{1,2},{2,1},{3,0},{4,7},{5,6},{6,5},{7,4},{8,11},{9,10},{10,... | collective-permute-start | bytes 49160 | tf_op jit(solution)/shard_map/ppermute | solution.py:260
  13.2 2.1 %collective-permute-start.5 = (f32[64,128]{1,0:T(8,128)S(1)}, f32[64,128]{1,0:T(8,128)S(1)}, u32[]{:S(2)}, u32[]{:S(2)}) collective-permute-start(f32[64,128]{1,0:T(8,128)S(1)} %get-tuple-element.26), channel_id=1, source_target_pairs={{0,1},{1,0},{2,3},{3,2},{4,5},{5,4},{6,7},{7,6},{8,9},{9,8},{10,11... | collective-permute-start | bytes 98312 | tf_op jit(solution)/shard_map/ppermute | solution.py:260
  13.4 4.3 %collective-permute-start.6 = (bf16[96,128]{1,0:T(8,128)(2,1)S(1)}, bf16[96,128]{1,0:T(8,128)(2,1)S(1)}, u32[]{:S(2)}, u32[]{:S(2)}) collective-permute-start(bf16[96,128]{1,0:T(8,128)(2,1)S(1)} %get-tuple-element.28.rest_0_), channel_id=1, source_target_pairs={{0,9},{1,8},{2,11},{3,10},{4,13},{5,12},{6,15},{7,14},{8,1},{9,0},... | collective-permute-start | bytes 73736 | tf_op jit(solution)/shard_map/ppermute | solution.py:260
  14.3 3.4 %collective-permute-start.7 = (bf16[96,128]{1,0:T(8,128)(2,1)S(1)}, bf16[96,128]{1,0:T(8,128)(2,1)S(1)}, u32[]{:S(2)}, u32[]{:S(2)}) collective-permute-start(bf16[96,128]{1,0:T(8,128)(2,1)S(1)} %get-tuple-element.28.rest_0_), channel_id=1, source_target_pairs={{0,17},{1,16},{2,19},{3,18},{4,21},{5,20},{6,23},{7,22},{8,25},{9,... | collective-permute-start | bytes 73736 | tf_op jit(solution)/shard_map/ppermute | solution.py:260
  15.4 4.2 %collective-permute-start.9 = (bf16[96,128]{1,0:T(8,128)(2,1)S(1)}, bf16[96,128]{1,0:T(8,128)(2,1)S(1)}, u32[]{:S(2)}, u32[]{:S(2)}) collective-permute-start(bf16[96,128]{1,0:T(8,128)(2,1)S(1)} %pad_maximum_fusion.1), channel_id=1, source_target_pairs={{0,25},{1,24},{2,27},{3,26},{4,29},{5,28},{6,31},{7,30},{8,17},{9,... | collective-permute-start | bytes 73736 | tf_op jit(solution)/shard_map/ppermute | solution.py:260
  18.2 1.6 %collective-permute-start.8 = (f16[64,128]{1,0:T(8,128)(2,1)S(1)}, f16[64,128]{1,0:T(8,128)(2,1)S(1)}, u32[]{:S(2)}, u32[]{:S(2)}) collective-permute-start(f16[64,128]{1,0:T(8,128)(2,1)S(1)} %multiply_convert_fusion.2), channel_id=1, source_target_pairs={{0,1},{1,0},{2,3},{3,2},{4,5},{5,4},{6,7},{7,6},{8,9},{9,8},{10,11... | collective-permute-start | bytes 49160 | tf_op jit(solution)/shard_map/ppermute | solution.py:260
  19.9 3.4 %collective-permute-start.10 = (f16[128,128]{1,0:T(8,128)(2,1)S(1)}, f16[128,128]{1,0:T(8,128)(2,1)S(1)}, u32[]{:S(2)}, u32[]{:S(2)}) collective-permute-start(f16[128,128]{1,0:T(8,128)(2,1)S(1)} %multiply_convert_fusion.1), channel_id=1, source_target_pairs={{0,3},{8,11},{16,19},{24,27},{1,4},{9,12},{17,20},{25,28},{2,7},{1... | collective-permute-start | bytes 98312 | tf_op jit(solution)/shard_map/ppermute | solution.py:269
  23.3 4.3 %collective-permute-start.11 = (f16[128,128]{1,0:T(8,128)(2,1)S(1)}, f16[128,128]{1,0:T(8,128)(2,1)S(1)}, u32[]{:S(2)}, u32[]{:S(2)}) collective-permute-start(f16[128,128]{1,0:T(8,128)(2,1)S(1)} %multiply_convert_fusion), channel_id=1, source_target_pairs={{0,5},{8,13},{16,21},{24,29},{1,2},{9,10},{17,18},{25,26},{2,1},{1... | collective-permute-start | bytes 98312 | tf_op jit(solution)/shard_map/ppermute | solution.py:269

commit v7 on v6

--- a/solution.py
+++ b/solution.py
@@ -10,7 +10,7 @@
 from jax.sharding import PartitionSpec as P
 
 TILE = 128
-CHUNK = 256
+CHUNK = 512
 COLUMNS = 512
 
 amplitude = 4.0
@@ -213,9 +213,10 @@
     new_ref[...] = second_ref[...] - (step_size * scales[0]) * kernel_sum(rows, blocks, rows.shape[1])
 
 
-def join_kernel(scales, rows_ref, block_ref, new_ref):
+def join_kernel(scales, rows_ref, *rest):
     rows = rows_ref[TILE:, :]
-    new_ref[...] = (-step_size * scales[0]) * kernel_sum(rows, (block_ref,), rows.shape[1])
+    blocks, new_ref = rest[:-1], rest[-1]
+    new_ref[...] = (-step_size * scales[0]) * kernel_sum(rows, blocks, rows.shape[1])
 
 
 def finish_kernel(marks_ref, total_ref, duals_ref, velocity_ref, new_duals_ref, new_velocity_ref):
@@ -285,9 +286,6 @@
     def other_core(array):
         return swap(array, groups, members, 0, 1)
 
-    def other_groups(array):
-        return [swap(array, groups, members, k, 1) for k in range(1, groups)]
-
     whole = (samples, count)
     other_points = other_core(points)
     marks, static = call(
@@ -323,11 +321,12 @@
         angles, weights, base, batch, upright, rows, *fixed, flops=10**9, name="first",
     )
     summed = other_core(share)
-    moves = [send] + other_groups(send)[:-1]
+    summed_first = [k for k in (groups - 1, groups - 2) if k > 0]
+    moves = [send] + [swap(send, groups, members, k, 1) for k in range(1, groups) if k not in summed_first]
     share = share + summed
     last = jnp.concatenate([share.astype(bf16), batch[:depth]], axis=0)
     last, upright = lax.optimization_barrier((last, upright))
-    last = swap(last, groups, members, groups - 1, 1)
+    last = [swap(last, groups, members, k, 1) for k in summed_first]
     (later,) = call(
         functools.partial(second_kernel, scales), [(part, f32)], angles, weights, base, upright, rows, *fixed,
         flops=0, name="second",
@@ -337,7 +336,7 @@
     )
     other = other_core((later * SHRINK).astype(jnp.float16)).astype(f32) * (1.0 / SHRINK)
     (joined,) = call(
-        functools.partial(join_kernel, scales), [(part, f32)], rows, last, flops=JOIN, name="join"
+        functools.partial(join_kernel, scales), [(part, f32)], rows, *last, flops=JOIN, name="join"
     )
     total = jnp.concatenate([share, later + other + joined], axis=0)
     rounds = members.bit_length() - 2

time: 28.5 us -> 28.4 us (level)
    ppermute x2, starting transfers between devices: 4 us -> 4.29 us  [two_ways(): return lax.ppermute(array, ('grp', 'feat'), pairs)]
    ppermute x2, waiting for transfers between devices: 3.71 us -> 3.42 us  [two_ways(): return lax.ppermute(array, ('grp', 'feat'), pairs)]
  transfers between devices with their start and end apart: 12 -> 12, of which waited for: 5 -> 7; matrix products, arithmetic and copies ran while one was open for 0% -> 0% of each run, Pallas kernels for 14% -> 14%
where the time goes in v7:
time: 28.4 us; the launch traced here: 28.2 us
  starting transfers between devices  16.3 us (57%)
  waiting for transfers between devices  5.67 us (20%)
  Pallas kernels  5.46 us (19%)
  between operations  0.78 us (3%)
    ppermute x10, starting transfers between devices, swap(): return lax.ppermute(array, ('grp', 'feat'), pairs)  12 us
    pallas_call x9, Pallas kernels, call(): pl.pallas_call(kernel, out_shape=[jax.ShapeDtypeStruct(shape, dtype) for...  5.46 us
    ppermute x2, starting transfers between devices, two_ways(): return lax.ppermute(array, ('grp', 'feat'), pairs)  4.29 us
    ppermute x2, waiting for transfers between devices, two_ways(): return lax.ppermute(array, ('grp', 'feat'), pairs)  3.42 us
    ppermute x10, waiting for transfers between devices, swap(): return lax.ppermute(array, ('grp', 'feat'), pairs)  2.25 us
  transfers between devices with their start and end apart: 12, of which 7 were waited for; matrix products, arithmetic and copies ran while one was open for 0% of the time, Pallas kernels for 14%

profile of v7, /device:TPU:0, one launch (start us, length us, event | category | flops | bytes accessed | tf_op | source)
XLA Modules:
  0.0 28.2 jit_solution(2774785498763756726)
XLA Ops:
  0.6 0.5 %collective-permute-start = (bf16[32,256]{1,0:T(8,128)(2,1)}, bf16[32,256]{1,0:T(8,128)(2,1)S(1)}, u32[]{:S(2)}, u32[]{:S(2)}) collective-permute-start(bf16[32,256]{1,0:T(8,128)(2,1)} %bitcast.17), channel_id=1, source_target_pairs={{0,1},{1,0},{2,3},{3,2},{4,5},{5,4},{6,7},{7,6},{8,9},{9,8},{10,11... | collective-permute-start | bytes 49160 | tf_op jit(solution)/shard_map/ppermute | solution.py:261
  1.1 0.9 %place.1 = (f32[32,256]{1,0:T(8,128)S(1)}, bf16[96,256]{1,0:T(8,128)(2,1)S(1)}) custom-call(s32[2]{0:T(128)} %bitcast.21, bf16[32,256]{1,0:T(8,128)(2,1)} %bitcast.18, f32[64,256]{1,0:T(8,128)} %bitcast.11), custom_call_target="tpu_custom_call" | custom-call | flops 2000000000 | bytes 81928 | tf_op jit(solution)/shard_map/place/pallas_call | solution.py:241
  2.1 2.7 %collective-permute-start.3 = (bf16[96,256]{1,0:T(8,128)(2,1)S(1)}, bf16[96,256]{1,0:T(8,128)(2,1)S(1)}, u32[]{:S(2)}, u32[]{:S(2)}) collective-permute-start(bf16[96,256]{1,0:T(8,128)(2,1)S(1)} %get-tuple-element.22.static_ref), channel_id=1, source_target_pairs={{0,9},{1,8},{2,11},{3,10},{4,13},{5,12},{6,15},{7,14},{8,1},{9,0},... | collective-permute-start | bytes 147464 | tf_op jit(solution)/shard_map/ppermute | solution.py:261
  4.7 0.0 collective-permute-done.other_ref
  4.7 2.3 %collective-permute-start.1 = (bf16[64,128]{1,0:T(8,128)(2,1)S(1)}, bf16[64,128]{1,0:T(8,128)(2,1)S(1)}, u32[]{:S(2)}, u32[]{:S(2)}) collective-permute-start(bf16[64,128]{1,0:T(8,128)(2,1)S(1)} %pack.1), channel_id=1, source_target_pairs={{0,5},{1,4},{2,7},{3,6},{4,1},{5,0},{6,3},{7,2},{8,13},{9,12},{10,... | collective-permute-start | bytes 49160 | tf_op jit(solution)/shard_map/ppermute | solution.py:261
  7.0 0.0 collective-permute-done.3
  7.0 1.7 %collective-permute-start.4 = (bf16[96,512]{1,0:T(8,128)(2,1)S(1)}, bf16[96,512]{1,0:T(8,128)(2,1)S(1)}, u32[]{:S(2)}, u32[]{:S(2)}) collective-permute-start(bf16[96,512]{1,0:T(8,128)(2,1)S(1)} %constant_dynamic-update-slice_fusion.rest_0_), channel_id=1, source_target_pairs={{0,17},{1,16},{2,19},{3,18},{4,21},{5,20},{6,23},{7,22},{8,25},{9,... | collective-permute-start | bytes 294920 | tf_op jit(solution)/shard_map/ppermute | solution.py:261
  8.7 0.2 collective-permute-done.1
  8.9 1.4 %collective-permute-start.2 = (bf16[64,128]{1,0:T(8,128)(2,1)S(1)}, bf16[64,128]{1,0:T(8,128)(2,1)S(1)}, u32[]{:S(2)}, u32[]{:S(2)}) collective-permute-start(bf16[64,128]{1,0:T(8,128)(2,1)S(1)} %add.18.refs_0_), channel_id=1, source_target_pairs={{0,3},{1,2},{2,1},{3,0},{4,7},{5,6},{6,5},{7,4},{8,11},{9,10},{10,... | collective-permute-start | bytes 49160 | tf_op jit(solution)/shard_map/ppermute | solution.py:261
  10.2 1.3 %prepare.1 = (bf16[128,2048]{1,0:T(8,128)(2,1)S(1)}, bf16[64,2048]{1,0:T(8,128)(2,1)S(1)}, f32[128,128]{1,0:T(8,128)S(1)}, f32[64,256]{1,0:T(8,128)S(1)}, f32[64,256]{1,0:T(8,128)S(1)}) custom-call(bf16[32,2048]{1,0:T(8,128)(2,1)} %freq_hbm.1, f32[1,2048]{1,0:T(1,128)} %bitcast.19, bf16[64,2048]{1,0:T(8,128)(2,1)} %bitcast.10, f32[1,256]{1,0:T(1,128)} %bitcast.20, ...), custom_call_target="tpu_custom_call" | custom-call | flops 1000000000 | bytes 631808 | tf_op jit(solution)/shard_map/prepare/pallas_call | solution.py:241
  11.5 0.6 %collective-permute-done.2.refs_1_ = bf16[64,128]{1,0:T(8,128)(2,1)S(1)} collective-permute-done((bf16[64,128]{1,0:T(8,128)(2,1)S(1)}, bf16[64,128]{1,0:T(8,128)(2,1)S(1)}, u32[]{:S(2)}, u32[]{:S(2)}) %collective-permute-start.2) | collective-permute-done | bytes 16416 | tf_op jit(solution)/shard_map/ppermute | solution.py:261
  12.1 0.1 stand.1
  12.2 0.0 collective-permute-done.4.rest_1_
  12.2 1.0 %first.1 = (f32[64,128]{1,0:T(8,128)S(1)}, bf16[96,128]{1,0:T(8,128)(2,1)S(1)}) custom-call(bf16[128,2048]{1,0:T(8,128)(2,1)S(1)} %get-tuple-element.19.angle_ref, bf16[64,2048]{1,0:T(8,128)(2,1)S(1)} %get-tuple-element.20.weight_ref, f32[128,128]{1,0:T(8,128)S(1)} %get-tuple-element.21.base_ref, bf16[64,128]{1,0:T(8,128)(2,1)S(1)} %get-tuple-element.23.batch_ref, ...), custom_call_target="tpu_custom_call" | custom-call | flops 1000000000 | bytes 1163264 | tf_op jit(solution)/shard_map/first/pallas_call | solution.py:241
  13.2 0.2 collective-permute-start.5
  13.4 0.9 %collective-permute-start.6 = (bf16[96,128]{1,0:T(8,128)(2,1)S(1)}, bf16[96,128]{1,0:T(8,128)(2,1)S(1)}, u32[]{:S(2)}, u32[]{:S(2)}) collective-permute-start(bf16[96,128]{1,0:T(8,128)(2,1)S(1)} %get-tuple-element.28.rest_0_), channel_id=1, source_target_pairs={{0,9},{1,8},{2,11},{3,10},{4,13},{5,12},{6,15},{7,14},{8,1},{9,0},... | collective-permute-start | bytes 73736 | tf_op jit(solution)/shard_map/ppermute | solution.py:261
  14.3 0.2 collective-permute-done.5
  14.5 1.7 %collective-permute-start.8 = (bf16[96,128]{1,0:T(8,128)(2,1)S(1)}, bf16[96,128]{1,0:T(8,128)(2,1)S(1)}, u32[]{:S(2)}, u32[]{:S(2)}) collective-permute-start(bf16[96,128]{1,0:T(8,128)(2,1)S(1)} %pad_maximum_fusion.1), channel_id=1, source_target_pairs={{0,25},{1,24},{2,27},{3,26},{4,29},{5,28},{6,31},{7,30},{8,17},{9,... | collective-permute-start | bytes 73736 | tf_op jit(solution)/shard_map/ppermute | solution.py:261
  16.2 0.5 %collective-permute-start.9 = (bf16[96,128]{1,0:T(8,128)(2,1)S(1)}, bf16[96,128]{1,0:T(8,128)(2,1)S(1)}, u32[]{:S(2)}, u32[]{:S(2)}) collective-permute-start(bf16[96,128]{1,0:T(8,128)(2,1)S(1)} %pad_maximum_fusion.1), channel_id=1, source_target_pairs={{0,17},{1,16},{2,19},{3,18},{4,21},{5,20},{6,23},{7,22},{8,25},{9,... | collective-permute-start | bytes 73736 | tf_op jit(solution)/shard_map/ppermute | solution.py:261
  16.7 1.0 %second.1.second_ref = f32[64,128]{1,0:T(8,128)S(1)} custom-call(bf16[128,2048]{1,0:T(8,128)(2,1)S(1)} %get-tuple-element.19.angle_ref, bf16[64,2048]{1,0:T(8,128)(2,1)S(1)} %get-tuple-element.20.weight_ref, f32[128,128]{1,0:T(8,128)S(1)} %get-tuple-element.21.base_ref, bf16[256,128]{1,0:T(8,128)(2,1)S(1)} %get-tuple-element.27.upright_ref, ...), custom_call_target="tpu_custom_call" | custom-call | tf_op jit(solution)/shard_map/second/pallas_call | solution.py:241
  17.7 0.0 collective-permute-done.6.rest_1_
  17.7 0.3 %correct.1 = f32[64,128]{1,0:T(8,128)S(1)} custom-call(f32[256,32]{1,0:T(8,128)S(1)} %get-tuple-element.25.rows_ref, f32[64,128]{1,0:T(8,128)S(1)} %second.1.second_ref, bf16[96,128]{1,0:T(8,128)(2,1)S(1)} %get-tuple-element.28.rest_0_, bf16[96,128]{1,0:T(8,128)(2,1)S(1)} %collective-permute-done.6.rest_1_), custom_call_target="tpu_custom_call" | custom-call | tf_op jit(solution)/shard_map/correct/pallas_call | solution.py:241
  18.0 0.1 collective-permute-start.7
  18.2 0.5 %collective-permute-done.8.rest_0_ = bf16[96,128]{1,0:T(8,128)(2,1)S(1)} collective-permute-done((bf16[96,128]{1,0:T(8,128)(2,1)S(1)}, bf16[96,128]{1,0:T(8,128)(2,1)S(1)}, u32[]{:S(2)}, u32[]{:S(2)}) %collective-permute-start.8) | collective-permute-done | bytes 24608 | tf_op jit(solution)/shard_map/ppermute | solution.py:261
  18.7 0.8 %collective-permute-done.9.rest_1_ = bf16[96,128]{1,0:T(8,128)(2,1)S(1)} collective-permute-done((bf16[96,128]{1,0:T(8,128)(2,1)S(1)}, bf16[96,128]{1,0:T(8,128)(2,1)S(1)}, u32[]{:S(2)}, u32[]{:S(2)}) %collective-permute-start.9) | collective-permute-done | bytes 24608 | tf_op jit(solution)/shard_map/ppermute | solution.py:261
  19.5 0.3 join.1
  19.8 0.0 collective-permute-done.7
  19.8 1.6 %collective-permute-start.10 = (f16[128,128]{1,0:T(8,128)(2,1)S(1)}, f16[128,128]{1,0:T(8,128)(2,1)S(1)}, u32[]{:S(2)}, u32[]{:S(2)}) collective-permute-start(f16[128,128]{1,0:T(8,128)(2,1)S(1)} %multiply_convert_fusion.1), channel_id=1, source_target_pairs={{0,3},{8,11},{16,19},{24,27},{1,4},{9,12},{17,20},{25,28},{2,7},{1... | collective-permute-start | bytes 98312 | tf_op jit(solution)/shard_map/ppermute | solution.py:270
  21.5 1.8 %collective-permute-done.10 = f16[128,128]{1,0:T(8,128)(2,1)S(1)} collective-permute-done((f16[128,128]{1,0:T(8,128)(2,1)S(1)}, f16[128,128]{1,0:T(8,128)(2,1)S(1)}, u32[]{:S(2)}, u32[]{:S(2)}) %collective-permute-start.10) | collective-permute-done | bytes 32800 | tf_op jit(solution)/shard_map/ppermute | solution.py:270
  23.3 2.6 %collective-permute-start.11 = (f16[128,128]{1,0:T(8,128)(2,1)S(1)}, f16[128,128]{1,0:T(8,128)(2,1)S(1)}, u32[]{:S(2)}, u32[]{:S(2)}) collective-permute-start(f16[128,128]{1,0:T(8,128)(2,1)S(1)} %multiply_convert_fusion), channel_id=1, source_target_pairs={{0,5},{8,13},{16,21},{24,29},{1,2},{9,10},{17,18},{25,26},{2,1},{1... | collective-permute-start | bytes 98312 | tf_op jit(solution)/shard_map/ppermute | solution.py:270
  25.9 1.7 %collective-permute-done.11 = f16[128,128]{1,0:T(8,128)(2,1)S(1)} collective-permute-done((f16[128,128]{1,0:T(8,128)(2,1)S(1)}, f16[128,128]{1,0:T(8,128)(2,1)S(1)}, u32[]{:S(2)}, u32[]{:S(2)}) %collective-permute-start.11) | collective-permute-done | bytes 32800 | tf_op jit(solution)/shard_map/ppermute | solution.py:270
  27.6 0.7 %finish.1 = (f32[64,256]{1,0:T(8,128)}, f32[64,256]{1,0:T(8,128)}) custom-call(f32[32,256]{1,0:T(8,128)S(1)} %get-tuple-element.18.marks_ref, f32[128,128]{1,0:T(8,128)S(1)} %multiply_add_fusion.total_ref, f32[64,256]{1,0:T(8,128)S(1)} %get-tuple-element.30.duals_ref, f32[64,256]{1,0:T(8,128)S(1)} %get-tuple-element.31.velocity_ref), custom_call_target="tpu_custom_call" | custom-call | tf_op jit(solution)/shard_map/finish/pallas_call | solution.py:241
  (12 shorter events, 0.1 us)
Async XLA Ops:
  0.6 4.1 %collective-permute-start = (bf16[32,256]{1,0:T(8,128)(2,1)}, bf16[32,256]{1,0:T(8,128)(2,1)S(1)}, u32[]{:S(2)}, u32[]{:S(2)}) collective-permute-start(bf16[32,256]{1,0:T(8,128)(2,1)} %bitcast.17), channel_id=1, source_target_pairs={{0,1},{1,0},{2,3},{3,2},{4,5},{5,4},{6,7},{7,6},{8,9},{9,8},{10,11... | collective-permute-start | bytes 49160 | tf_op jit(solution)/shard_map/ppermute | solution.py:261
  2.1 5.0 %collective-permute-start.3 = (bf16[96,256]{1,0:T(8,128)(2,1)S(1)}, bf16[96,256]{1,0:T(8,128)(2,1)S(1)}, u32[]{:S(2)}, u32[]{:S(2)}) collective-permute-start(bf16[96,256]{1,0:T(8,128)(2,1)S(1)} %get-tuple-element.22.static_ref), channel_id=1, source_target_pairs={{0,9},{1,8},{2,11},{3,10},{4,13},{5,12},{6,15},{7,14},{8,1},{9,0},... | collective-permute-start | bytes 147464 | tf_op jit(solution)/shard_map/ppermute | solution.py:261
  4.7 4.1 %collective-permute-start.1 = (bf16[64,128]{1,0:T(8,128)(2,1)S(1)}, bf16[64,128]{1,0:T(8,128)(2,1)S(1)}, u32[]{:S(2)}, u32[]{:S(2)}) collective-permute-start(bf16[64,128]{1,0:T(8,128)(2,1)S(1)} %pack.1), channel_id=1, source_target_pairs={{0,5},{1,4},{2,7},{3,6},{4,1},{5,0},{6,3},{7,2},{8,13},{9,12},{10,... | collective-permute-start | bytes 49160 | tf_op jit(solution)/shard_map/ppermute | solution.py:261
  7.0 5.2 %collective-permute-start.4 = (bf16[96,512]{1,0:T(8,128)(2,1)S(1)}, bf16[96,512]{1,0:T(8,128)(2,1)S(1)}, u32[]{:S(2)}, u32[]{:S(2)}) collective-permute-start(bf16[96,512]{1,0:T(8,128)(2,1)S(1)} %constant_dynamic-update-slice_fusion.rest_0_), channel_id=1, source_target_pairs={{0,17},{1,16},{2,19},{3,18},{4,21},{5,20},{6,23},{7,22},{8,25},{9,... | collective-permute-start | bytes 294920 | tf_op jit(solution)/shard_map/ppermute | solution.py:261
  8.9 3.2 %collective-permute-start.2 = (bf16[64,128]{1,0:T(8,128)(2,1)S(1)}, bf16[64,128]{1,0:T(8,128)(2,1)S(1)}, u32[]{:S(2)}, u32[]{:S(2)}) collective-permute-start(bf16[64,128]{1,0:T(8,128)(2,1)S(1)} %add.18.refs_0_), channel_id=1, source_target_pairs={{0,3},{1,2},{2,1},{3,0},{4,7},{5,6},{6,5},{7,4},{8,11},{9,10},{10,... | collective-permute-start | bytes 49160 | tf_op jit(solution)/shard_map/ppermute | solution.py:261
  13.2 1.3 %collective-permute-start.5 = (f32[64,128]{1,0:T(8,128)S(1)}, f32[64,128]{1,0:T(8,128)S(1)}, u32[]{:S(2)}, u32[]{:S(2)}) collective-permute-start(f32[64,128]{1,0:T(8,128)S(1)} %get-tuple-element.26), channel_id=1, source_target_pairs={{0,1},{1,0},{2,3},{3,2},{4,5},{5,4},{6,7},{7,6},{8,9},{9,8},{10,11... | collective-permute-start | bytes 98312 | tf_op jit(solution)/shard_map/ppermute | solution.py:261
  13.4 4.3 %collective-permute-start.6 = (bf16[96,128]{1,0:T(8,128)(2,1)S(1)}, bf16[96,128]{1,0:T(8,128)(2,1)S(1)}, u32[]{:S(2)}, u32[]{:S(2)}) collective-permute-start(bf16[96,128]{1,0:T(8,128)(2,1)S(1)} %get-tuple-element.28.rest_0_), channel_id=1, source_target_pairs={{0,9},{1,8},{2,11},{3,10},{4,13},{5,12},{6,15},{7,14},{8,1},{9,0},... | collective-permute-start | bytes 73736 | tf_op jit(solution)/shard_map/ppermute | solution.py:261
  14.5 4.2 %collective-permute-start.8 = (bf16[96,128]{1,0:T(8,128)(2,1)S(1)}, bf16[96,128]{1,0:T(8,128)(2,1)S(1)}, u32[]{:S(2)}, u32[]{:S(2)}) collective-permute-start(bf16[96,128]{1,0:T(8,128)(2,1)S(1)} %pad_maximum_fusion.1), channel_id=1, source_target_pairs={{0,25},{1,24},{2,27},{3,26},{4,29},{5,28},{6,31},{7,30},{8,17},{9,... | collective-permute-start | bytes 73736 | tf_op jit(solution)/shard_map/ppermute | solution.py:261
  16.2 3.3 %collective-permute-start.9 = (bf16[96,128]{1,0:T(8,128)(2,1)S(1)}, bf16[96,128]{1,0:T(8,128)(2,1)S(1)}, u32[]{:S(2)}, u32[]{:S(2)}) collective-permute-start(bf16[96,128]{1,0:T(8,128)(2,1)S(1)} %pad_maximum_fusion.1), channel_id=1, source_target_pairs={{0,17},{1,16},{2,19},{3,18},{4,21},{5,20},{6,23},{7,22},{8,25},{9,... | collective-permute-start | bytes 73736 | tf_op jit(solution)/shard_map/ppermute | solution.py:261
  18.0 1.7 %collective-permute-start.7 = (f16[64,128]{1,0:T(8,128)(2,1)S(1)}, f16[64,128]{1,0:T(8,128)(2,1)S(1)}, u32[]{:S(2)}, u32[]{:S(2)}) collective-permute-start(f16[64,128]{1,0:T(8,128)(2,1)S(1)} %multiply_convert_fusion.2), channel_id=1, source_target_pairs={{0,1},{1,0},{2,3},{3,2},{4,5},{5,4},{6,7},{7,6},{8,9},{9,8},{10,11... | collective-permute-start | bytes 49160 | tf_op jit(solution)/shard_map/ppermute | solution.py:261
  19.8 3.4 %collective-permute-start.10 = (f16[128,128]{1,0:T(8,128)(2,1)S(1)}, f16[128,128]{1,0:T(8,128)(2,1)S(1)}, u32[]{:S(2)}, u32[]{:S(2)}) collective-permute-start(f16[128,128]{1,0:T(8,128)(2,1)S(1)} %multiply_convert_fusion.1), channel_id=1, source_target_pairs={{0,3},{8,11},{16,19},{24,27},{1,4},{9,12},{17,20},{25,28},{2,7},{1... | collective-permute-start | bytes 98312 | tf_op jit(solution)/shard_map/ppermute | solution.py:270
  23.3 4.3 %collective-permute-start.11 = (f16[128,128]{1,0:T(8,128)(2,1)S(1)}, f16[128,128]{1,0:T(8,128)(2,1)S(1)}, u32[]{:S(2)}, u32[]{:S(2)}) collective-permute-start(f16[128,128]{1,0:T(8,128)(2,1)S(1)} %multiply_convert_fusion), channel_id=1, source_target_pairs={{0,5},{8,13},{16,21},{24,29},{1,2},{9,10},{17,18},{25,26},{2,1},{1... | collective-permute-start | bytes 98312 | tf_op jit(solution)/shard_map/ppermute | solution.py:270

commit v8 on v7

--- a/solution.py
+++ b/solution.py
@@ -170,51 +170,44 @@
         base_ref[values * step : values * (step + 1), :] = share
 
 
-def stand_kernel(*refs):
-    terms, (batch_ref, upright_ref, rows_ref) = refs[:-3], refs[-3:]
+def share_of(scales, step, upright, rows, angle_ref, weight_ref, base_ref, blocks):
+    inv_root, prior_scale = scales
+    kernel_part = kernel_sum(rows, blocks, rows.shape[1])
+    prior_part = prior_sum(upright, angle_ref, weight_ref)
+    values = prior_part.shape[0]
+    base = base_ref[values * step : values * (step + 1), :]
+    return base - (step_size * inv_root) * kernel_part - (step_size * prior_scale) * prior_part
+
+
+def first_kernel(scales, parts, angle_ref, weight_ref, base_ref, *rest):
+    terms, blocks, (share_ref, send_ref, batch_ref) = rest[:parts], rest[parts:-3], rest[-3:]
     batch = terms[0][...]
     for term_ref in terms[1:]:
         batch = batch + term_ref[...]
     batch_ref[...] = batch
-    depth = batch.shape[0] // 2
-    for step in range(2):
-        upright, rows = rows_of(batch[depth * step : depth * (step + 1)])
-        upright_ref[TILE * step : TILE * (step + 1), :] = upright
-        rows_ref[TILE * step : TILE * (step + 1), :] = rows
-
-
-def share_of(scales, step, upright_ref, rows_ref, angle_ref, weight_ref, base_ref, blocks):
-    inv_root, prior_scale = scales
-    cut = slice(TILE * step, TILE * (step + 1))
-    rows = rows_ref[cut, :]
-    kernel_part = kernel_sum(rows, blocks, rows.shape[1])
-    prior_part = prior_sum(upright_ref[cut, :], angle_ref, weight_ref)
-    values = prior_part.shape[0]
-    base = base_ref[values * step : values * (step + 1), :]
-    return base - (step_size * inv_root) * kernel_part - (step_size * prior_scale) * prior_part
-
-
-def first_kernel(scales, angle_ref, weight_ref, base_ref, batch_ref, upright_ref, rows_ref, *rest):
-    blocks, (share_ref, send_ref) = rest[:-2], rest[-2:]
-    share = share_of(scales, 0, upright_ref, rows_ref, angle_ref, weight_ref, base_ref, blocks)
+    turned = batch[: batch.shape[0] // 2]
+    upright, rows = rows_of(turned)
+    share = share_of(scales, 0, upright, rows, angle_ref, weight_ref, base_ref, blocks)
     share_ref[...] = share
     send_ref[: share.shape[0], :] = share.astype(bf16)
-    send_ref[share.shape[0] :, :] = batch_ref[: batch_ref.shape[0] // 2, :]
-
-
-def second_kernel(scales, angle_ref, weight_ref, base_ref, upright_ref, rows_ref, *rest):
-    blocks, share_ref = rest[:-1], rest[-1]
-    share_ref[...] = share_of(scales, 1, upright_ref, rows_ref, angle_ref, weight_ref, base_ref, blocks)
+    send_ref[share.shape[0] :, :] = turned
+
+
+def second_kernel(scales, angle_ref, weight_ref, base_ref, batch_ref, *rest):
+    blocks, (share_ref, rows_ref) = rest[:-2], rest[-2:]
+    upright, rows = rows_of(batch_ref[batch_ref.shape[0] // 2 :, :])
+    rows_ref[...] = rows
+    share_ref[...] = share_of(scales, 1, upright, rows, angle_ref, weight_ref, base_ref, blocks)
 
 
 def correct_kernel(scales, rows_ref, second_ref, *rest):
     blocks, new_ref = rest[:-1], rest[-1]
-    rows = rows_ref[TILE:, :]
+    rows = rows_ref[...]
     new_ref[...] = second_ref[...] - (step_size * scales[0]) * kernel_sum(rows, blocks, rows.shape[1])
 
 
 def join_kernel(scales, rows_ref, *rest):
-    rows = rows_ref[TILE:, :]
+    rows = rows_ref[...]
     blocks, new_ref = rest[:-1], rest[-1]
     new_ref[...] = (-step_size * scales[0]) * kernel_sum(rows, blocks, rows.shape[1])
 
@@ -312,24 +305,21 @@
         if 2 * group_bit < groups and 2 * chip_bit < members:
             fixed[-1], batch[1] = lax.optimization_barrier((fixed[-1], batch[1]))
         chip_bit, group_bit = 2 * chip_bit, 2 * group_bit
-    batch, upright, rows = call(
-        stand_kernel, [((2 * depth, TILE), bf16), ((2 * TILE, ANGLE_ROWS), bf16), ((2 * TILE, depth), f32)], *batch,
-        name="stand",
-    )
-    share, send = call(
-        functools.partial(first_kernel, scales), [(part, f32), ((samples + depth, TILE), bf16)],
-        angles, weights, base, batch, upright, rows, *fixed, flops=10**9, name="first",
+    share, send, batch = call(
+        functools.partial(first_kernel, scales, len(batch)),
+        [(part, f32), ((samples + depth, TILE), bf16), ((2 * depth, TILE), bf16)],
+        angles, weights, base, *batch, *fixed, flops=10**9, name="first",
     )
     summed = other_core(share)
     summed_first = [k for k in (groups - 1, groups - 2) if k > 0]
     moves = [send] + [swap(send, groups, members, k, 1) for k in range(1, groups) if k not in summed_first]
     share = share + summed
     last = jnp.concatenate([share.astype(bf16), batch[:depth]], axis=0)
-    last, upright = lax.optimization_barrier((last, upright))
+    last, batch = lax.optimization_barrier((last, batch))
     last = [swap(last, groups, members, k, 1) for k in summed_first]
-    (later,) = call(
-        functools.partial(second_kernel, scales), [(part, f32)], angles, weights, base, upright, rows, *fixed,
-        flops=0, name="second",
+    later, rows = call(
+        functools.partial(second_kernel, scales), [(part, f32), ((TILE, depth), f32)],
+        angles, weights, base, batch, *fixed, flops=0, name="second",
     )
     (later,) = call(
         functools.partial(correct_kernel, scales), [(part, f32)], rows, later, *moves, flops=0, name="correct"

time: 28.4 us -> 28.3 us (level)
    pallas_call x9 -> x8, Pallas kernels: 5.46 us -> 5.47 us  [call(): pl.pallas_call(kernel, out_shape=[jax.ShapeDtypeStruct(shape, dtype) for...]
  transfers between devices with their start and end apart: 12 -> 12, of which waited for: 7 -> 7; matrix products, arithmetic and copies ran while one was open for 0% -> 0% of each run, Pallas kernels for 14% -> 13%
where the time goes in v8:
time: 28.3 us; the launch traced here: 28.1 us
  starting transfers between devices  16.3 us (58%)
  waiting for transfers between devices  5.54 us (20%)
  Pallas kernels  5.47 us (19%)
  between operations  0.76 us (3%)
    ppermute x10, starting transfers between devices, swap(): return lax.ppermute(array, ('grp', 'feat'), pairs)  11.9 us
    pallas_call x8, Pallas kernels, call(): pl.pallas_call(kernel, out_shape=[jax.ShapeDtypeStruct(shape, dtype) for...  5.47 us
    ppermute x2, starting transfers between devices, two_ways(): return lax.ppermute(array, ('grp', 'feat'), pairs)  4.35 us
    ppermute x2, waiting for transfers between devices, two_ways(): return lax.ppermute(array, ('grp', 'feat'), pairs)  3.36 us
    ppermute x10, waiting for transfers between devices, swap(): return lax.ppermute(array, ('grp', 'feat'), pairs)  2.18 us
  transfers between devices with their start and end apart: 12, of which 7 were waited for; matrix products, arithmetic and copies ran while one was open for 0% of the time, Pallas kernels for 13%

profile of v8, /device:TPU:0, one launch (start us, length us, event | category | flops | bytes accessed | tf_op | source)
XLA Modules:
  0.0 28.1 jit_solution(16205649282288357340)
XLA Ops:
  0.6 0.5 %collective-permute-start = (bf16[32,256]{1,0:T(8,128)(2,1)}, bf16[32,256]{1,0:T(8,128)(2,1)S(1)}, u32[]{:S(2)}, u32[]{:S(2)}) collective-permute-start(bf16[32,256]{1,0:T(8,128)(2,1)} %bitcast.17), channel_id=1, source_target_pairs={{0,1},{1,0},{2,3},{3,2},{4,5},{5,4},{6,7},{7,6},{8,9},{9,8},{10,11... | collective-permute-start | bytes 49160 | tf_op jit(solution)/shard_map/ppermute | solution.py:254
  1.1 0.9 %place.1 = (f32[32,256]{1,0:T(8,128)S(1)}, bf16[96,256]{1,0:T(8,128)(2,1)S(1)}) custom-call(s32[2]{0:T(128)} %bitcast.21, bf16[32,256]{1,0:T(8,128)(2,1)} %bitcast.18, f32[64,256]{1,0:T(8,128)} %bitcast.11), custom_call_target="tpu_custom_call" | custom-call | flops 2000000000 | bytes 81928 | tf_op jit(solution)/shard_map/place/pallas_call | solution.py:234
  2.1 2.7 %collective-permute-start.3 = (bf16[96,256]{1,0:T(8,128)(2,1)S(1)}, bf16[96,256]{1,0:T(8,128)(2,1)S(1)}, u32[]{:S(2)}, u32[]{:S(2)}) collective-permute-start(bf16[96,256]{1,0:T(8,128)(2,1)S(1)} %get-tuple-element.22.static_ref), channel_id=1, source_target_pairs={{0,9},{1,8},{2,11},{3,10},{4,13},{5,12},{6,15},{7,14},{8,1},{9,0},... | collective-permute-start | bytes 147464 | tf_op jit(solution)/shard_map/ppermute | solution.py:254
  4.7 0.0 collective-permute-done.other_ref
  4.7 2.3 %collective-permute-start.1 = (bf16[64,128]{1,0:T(8,128)(2,1)S(1)}, bf16[64,128]{1,0:T(8,128)(2,1)S(1)}, u32[]{:S(2)}, u32[]{:S(2)}) collective-permute-start(bf16[64,128]{1,0:T(8,128)(2,1)S(1)} %pack.1), channel_id=1, source_target_pairs={{0,5},{1,4},{2,7},{3,6},{4,1},{5,0},{6,3},{7,2},{8,13},{9,12},{10,... | collective-permute-start | bytes 49160 | tf_op jit(solution)/shard_map/ppermute | solution.py:254
  7.0 0.0 collective-permute-done.3
  7.0 1.7 %collective-permute-start.4 = (bf16[96,512]{1,0:T(8,128)(2,1)S(1)}, bf16[96,512]{1,0:T(8,128)(2,1)S(1)}, u32[]{:S(2)}, u32[]{:S(2)}) collective-permute-start(bf16[96,512]{1,0:T(8,128)(2,1)S(1)} %constant_dynamic-update-slice_fusion.rest_2_.rest_0_), channel_id=1, source_target_pairs={{0,17},{1,16},{2,19},{3,18},{4,21},{5,20},{6,23},{7,22},{8,25},{9,... | collective-permute-start | bytes 294920 | tf_op jit(solution)/shard_map/ppermute | solution.py:254
  8.7 0.2 collective-permute-done.1
  8.9 1.4 %collective-permute-start.2 = (bf16[64,128]{1,0:T(8,128)(2,1)S(1)}, bf16[64,128]{1,0:T(8,128)(2,1)S(1)}, u32[]{:S(2)}, u32[]{:S(2)}) collective-permute-start(bf16[64,128]{1,0:T(8,128)(2,1)S(1)} %add.18.rest_0_), channel_id=1, source_target_pairs={{0,3},{1,2},{2,1},{3,0},{4,7},{5,6},{6,5},{7,4},{8,11},{9,10},{10,... | collective-permute-start | bytes 49160 | tf_op jit(solution)/shard_map/ppermute | solution.py:254
  10.2 1.3 %prepare.1 = (bf16[128,2048]{1,0:T(8,128)(2,1)S(1)}, bf16[64,2048]{1,0:T(8,128)(2,1)S(1)}, f32[128,128]{1,0:T(8,128)S(1)}, f32[64,256]{1,0:T(8,128)S(1)}, f32[64,256]{1,0:T(8,128)S(1)}) custom-call(bf16[32,2048]{1,0:T(8,128)(2,1)} %freq_hbm.1, f32[1,2048]{1,0:T(1,128)} %bitcast.19, bf16[64,2048]{1,0:T(8,128)(2,1)} %bitcast.10, f32[1,256]{1,0:T(1,128)} %bitcast.20, ...), custom_call_target="tpu_custom_call" | custom-call | flops 1000000000 | bytes 631808 | tf_op jit(solution)/shard_map/prepare/pallas_call | solution.py:234
  11.5 0.6 %collective-permute-done.2.rest_1_ = bf16[64,128]{1,0:T(8,128)(2,1)S(1)} collective-permute-done((bf16[64,128]{1,0:T(8,128)(2,1)S(1)}, bf16[64,128]{1,0:T(8,128)(2,1)S(1)}, u32[]{:S(2)}, u32[]{:S(2)}) %collective-permute-start.2) | collective-permute-done | bytes 16416 | tf_op jit(solution)/shard_map/ppermute | solution.py:254
  12.1 0.0 collective-permute-done.4.rest_3_.rest_1_
  12.1 1.0 %first.1 = (f32[64,128]{1,0:T(8,128)S(1)}, bf16[96,128]{1,0:T(8,128)(2,1)S(1)}, bf16[64,128]{1,0:T(8,128)(2,1)S(1)}) custom-call(bf16[128,2048]{1,0:T(8,128)(2,1)S(1)} %get-tuple-element.19.angle_ref, bf16[64,2048]{1,0:T(8,128)(2,1)S(1)} %get-tuple-element.20.weight_ref, f32[128,128]{1,0:T(8,128)S(1)} %get-tuple-element.21.base_ref, ...), custom_call_target="tpu_custom_call" | custom-call | flops 1000000000 | bytes 1081344 | tf_op jit(solution)/shard_map/first/pallas_call | solution.py:234
  13.2 0.2 collective-permute-start.5
  13.3 0.9 %collective-permute-start.6 = (bf16[96,128]{1,0:T(8,128)(2,1)S(1)}, bf16[96,128]{1,0:T(8,128)(2,1)S(1)}, u32[]{:S(2)}, u32[]{:S(2)}) collective-permute-start(bf16[96,128]{1,0:T(8,128)(2,1)S(1)} %get-tuple-element.28.rest_0_), channel_id=1, source_target_pairs={{0,9},{1,8},{2,11},{3,10},{4,13},{5,12},{6,15},{7,14},{8,1},{9,0},... | collective-permute-start | bytes 73736 | tf_op jit(solution)/shard_map/ppermute | solution.py:254
  14.2 0.2 collective-permute-done.5
  14.4 1.7 %collective-permute-start.8 = (bf16[96,128]{1,0:T(8,128)(2,1)S(1)}, bf16[96,128]{1,0:T(8,128)(2,1)S(1)}, u32[]{:S(2)}, u32[]{:S(2)}) collective-permute-start(bf16[96,128]{1,0:T(8,128)(2,1)S(1)} %pad_maximum_fusion.1), channel_id=1, source_target_pairs={{0,25},{1,24},{2,27},{3,26},{4,29},{5,28},{6,31},{7,30},{8,17},{9,... | collective-permute-start | bytes 73736 | tf_op jit(solution)/shard_map/ppermute | solution.py:254
  16.1 0.6 %collective-permute-start.9 = (bf16[96,128]{1,0:T(8,128)(2,1)S(1)}, bf16[96,128]{1,0:T(8,128)(2,1)S(1)}, u32[]{:S(2)}, u32[]{:S(2)}) collective-permute-start(bf16[96,128]{1,0:T(8,128)(2,1)S(1)} %pad_maximum_fusion.1), channel_id=1, source_target_pairs={{0,17},{1,16},{2,19},{3,18},{4,21},{5,20},{6,23},{7,22},{8,25},{9,... | collective-permute-start | bytes 73736 | tf_op jit(solution)/shard_map/ppermute | solution.py:254
  16.7 1.0 %second.1 = (f32[64,128]{1,0:T(8,128)S(1)}, f32[128,32]{1,0:T(8,128)S(1)}) custom-call(bf16[128,2048]{1,0:T(8,128)(2,1)S(1)} %get-tuple-element.19.angle_ref, bf16[64,2048]{1,0:T(8,128)(2,1)S(1)} %get-tuple-element.20.weight_ref, f32[128,128]{1,0:T(8,128)S(1)} %get-tuple-element.21.base_ref, bf16[64,128]{1,0:T(8,128)(2,1)S(1)} %get-tuple-element.25.batch_ref, ...), custom_call_target="tpu_custom_call" | custom-call | tf_op jit(solution)/shard_map/second/pallas_call | solution.py:234
  17.7 0.0 collective-permute-done.6.rest_1_
  17.7 0.3 %correct.1 = f32[64,128]{1,0:T(8,128)S(1)} custom-call(f32[128,32]{1,0:T(8,128)S(1)} %get-tuple-element.26.rows_ref, f32[64,128]{1,0:T(8,128)S(1)} %get-tuple-element.27.second_ref, bf16[96,128]{1,0:T(8,128)(2,1)S(1)} %get-tuple-element.28.rest_0_, bf16[96,128]{1,0:T(8,128)(2,1)S(1)} %collective-permute-done.6.rest_1_), custom_call_target="tpu_custom_call" | custom-call | tf_op jit(solution)/shard_map/correct/pallas_call | solution.py:234
  18.0 0.1 collective-permute-start.7
  18.2 0.5 %collective-permute-done.8.rest_0_ = bf16[96,128]{1,0:T(8,128)(2,1)S(1)} collective-permute-done((bf16[96,128]{1,0:T(8,128)(2,1)S(1)}, bf16[96,128]{1,0:T(8,128)(2,1)S(1)}, u32[]{:S(2)}, u32[]{:S(2)}) %collective-permute-start.8) | collective-permute-done | bytes 24608 | tf_op jit(solution)/shard_map/ppermute | solution.py:254
  18.7 0.7 %collective-permute-done.9.rest_1_ = bf16[96,128]{1,0:T(8,128)(2,1)S(1)} collective-permute-done((bf16[96,128]{1,0:T(8,128)(2,1)S(1)}, bf16[96,128]{1,0:T(8,128)(2,1)S(1)}, u32[]{:S(2)}, u32[]{:S(2)}) %collective-permute-start.9) | collective-permute-done | bytes 24608 | tf_op jit(solution)/shard_map/ppermute | solution.py:254
  19.4 0.3 join.1
  19.7 0.0 collective-permute-done.7
  19.7 1.7 %collective-permute-start.10 = (f16[128,128]{1,0:T(8,128)(2,1)S(1)}, f16[128,128]{1,0:T(8,128)(2,1)S(1)}, u32[]{:S(2)}, u32[]{:S(2)}) collective-permute-start(f16[128,128]{1,0:T(8,128)(2,1)S(1)} %multiply_convert_fusion.1), channel_id=1, source_target_pairs={{0,3},{8,11},{16,19},{24,27},{1,4},{9,12},{17,20},{25,28},{2,7},{1... | collective-permute-start | bytes 98312 | tf_op jit(solution)/shard_map/ppermute | solution.py:263
  21.4 1.7 %collective-permute-done.10 = f16[128,128]{1,0:T(8,128)(2,1)S(1)} collective-permute-done((f16[128,128]{1,0:T(8,128)(2,1)S(1)}, f16[128,128]{1,0:T(8,128)(2,1)S(1)}, u32[]{:S(2)}, u32[]{:S(2)}) %collective-permute-start.10) | collective-permute-done | bytes 32800 | tf_op jit(solution)/shard_map/ppermute | solution.py:263
  23.2 2.7 %collective-permute-start.11 = (f16[128,128]{1,0:T(8,128)(2,1)S(1)}, f16[128,128]{1,0:T(8,128)(2,1)S(1)}, u32[]{:S(2)}, u32[]{:S(2)}) collective-permute-start(f16[128,128]{1,0:T(8,128)(2,1)S(1)} %multiply_convert_fusion), channel_id=1, source_target_pairs={{0,5},{8,13},{16,21},{24,29},{1,2},{9,10},{17,18},{25,26},{2,1},{1... | collective-permute-start | bytes 98312 | tf_op jit(solution)/shard_map/ppermute | solution.py:263
  25.8 1.6 %collective-permute-done.11 = f16[128,128]{1,0:T(8,128)(2,1)S(1)} collective-permute-done((f16[128,128]{1,0:T(8,128)(2,1)S(1)}, f16[128,128]{1,0:T(8,128)(2,1)S(1)}, u32[]{:S(2)}, u32[]{:S(2)}) %collective-permute-start.11) | collective-permute-done | bytes 32800 | tf_op jit(solution)/shard_map/ppermute | solution.py:263
  27.5 0.7 %finish.1 = (f32[64,256]{1,0:T(8,128)}, f32[64,256]{1,0:T(8,128)}) custom-call(f32[32,256]{1,0:T(8,128)S(1)} %get-tuple-element.18.marks_ref, f32[128,128]{1,0:T(8,128)S(1)} %multiply_add_fusion.total_ref, f32[64,256]{1,0:T(8,128)S(1)} %get-tuple-element.30.duals_ref, f32[64,256]{1,0:T(8,128)S(1)} %get-tuple-element.31.velocity_ref), custom_call_target="tpu_custom_call" | custom-call | tf_op jit(solution)/shard_map/finish/pallas_call | solution.py:234
  (12 shorter events, 0.1 us)
Async XLA Ops:
  0.6 4.1 %collective-permute-start = (bf16[32,256]{1,0:T(8,128)(2,1)}, bf16[32,256]{1,0:T(8,128)(2,1)S(1)}, u32[]{:S(2)}, u32[]{:S(2)}) collective-permute-start(bf16[32,256]{1,0:T(8,128)(2,1)} %bitcast.17), channel_id=1, source_target_pairs={{0,1},{1,0},{2,3},{3,2},{4,5},{5,4},{6,7},{7,6},{8,9},{9,8},{10,11... | collective-permute-start | bytes 49160 | tf_op jit(solution)/shard_map/ppermute | solution.py:254
  2.1 5.0 %collective-permute-start.3 = (bf16[96,256]{1,0:T(8,128)(2,1)S(1)}, bf16[96,256]{1,0:T(8,128)(2,1)S(1)}, u32[]{:S(2)}, u32[]{:S(2)}) collective-permute-start(bf16[96,256]{1,0:T(8,128)(2,1)S(1)} %get-tuple-element.22.static_ref), channel_id=1, source_target_pairs={{0,9},{1,8},{2,11},{3,10},{4,13},{5,12},{6,15},{7,14},{8,1},{9,0},... | collective-permute-start | bytes 147464 | tf_op jit(solution)/shard_map/ppermute | solution.py:254
  4.7 4.1 %collective-permute-start.1 = (bf16[64,128]{1,0:T(8,128)(2,1)S(1)}, bf16[64,128]{1,0:T(8,128)(2,1)S(1)}, u32[]{:S(2)}, u32[]{:S(2)}) collective-permute-start(bf16[64,128]{1,0:T(8,128)(2,1)S(1)} %pack.1), channel_id=1, source_target_pairs={{0,5},{1,4},{2,7},{3,6},{4,1},{5,0},{6,3},{7,2},{8,13},{9,12},{10,... | collective-permute-start | bytes 49160 | tf_op jit(solution)/shard_map/ppermute | solution.py:254
  7.0 5.1 %collective-permute-start.4 = (bf16[96,512]{1,0:T(8,128)(2,1)S(1)}, bf16[96,512]{1,0:T(8,128)(2,1)S(1)}, u32[]{:S(2)}, u32[]{:S(2)}) collective-permute-start(bf16[96,512]{1,0:T(8,128)(2,1)S(1)} %constant_dynamic-update-slice_fusion.rest_2_.rest_0_), channel_id=1, source_target_pairs={{0,17},{1,16},{2,19},{3,18},{4,21},{5,20},{6,23},{7,22},{8,25},{9,... | collective-permute-start | bytes 294920 | tf_op jit(solution)/shard_map/ppermute | solution.py:254
  8.9 3.2 %collective-permute-start.2 = (bf16[64,128]{1,0:T(8,128)(2,1)S(1)}, bf16[64,128]{1,0:T(8,128)(2,1)S(1)}, u32[]{:S(2)}, u32[]{:S(2)}) collective-permute-start(bf16[64,128]{1,0:T(8,128)(2,1)S(1)} %add.18.rest_0_), channel_id=1, source_target_pairs={{0,3},{1,2},{2,1},{3,0},{4,7},{5,6},{6,5},{7,4},{8,11},{9,10},{10,... | collective-permute-start | bytes 49160 | tf_op jit(solution)/shard_map/ppermute | solution.py:254
  13.2 1.3 %collective-permute-start.5 = (f32[64,128]{1,0:T(8,128)S(1)}, f32[64,128]{1,0:T(8,128)S(1)}, u32[]{:S(2)}, u32[]{:S(2)}) collective-permute-start(f32[64,128]{1,0:T(8,128)S(1)} %get-tuple-element.23), channel_id=1, source_target_pairs={{0,1},{1,0},{2,3},{3,2},{4,5},{5,4},{6,7},{7,6},{8,9},{9,8},{10,11... | collective-permute-start | bytes 98312 | tf_op jit(solution)/shard_map/ppermute | solution.py:254
  13.3 4.4 %collective-permute-start.6 = (bf16[96,128]{1,0:T(8,128)(2,1)S(1)}, bf16[96,128]{1,0:T(8,128)(2,1)S(1)}, u32[]{:S(2)}, u32[]{:S(2)}) collective-permute-start(bf16[96,128]{1,0:T(8,128)(2,1)S(1)} %get-tuple-element.28.rest_0_), channel_id=1, source_target_pairs={{0,9},{1,8},{2,11},{3,10},{4,13},{5,12},{6,15},{7,14},{8,1},{9,0},... | collective-permute-start | bytes 73736 | tf_op jit(solution)/shard_map/ppermute | solution.py:254
  14.4 4.2 %collective-permute-start.8 = (bf16[96,128]{1,0:T(8,128)(2,1)S(1)}, bf16[96,128]{1,0:T(8,128)(2,1)S(1)}, u32[]{:S(2)}, u32[]{:S(2)}) collective-permute-start(bf16[96,128]{1,0:T(8,128)(2,1)S(1)} %pad_maximum_fusion.1), channel_id=1, source_target_pairs={{0,25},{1,24},{2,27},{3,26},{4,29},{5,28},{6,31},{7,30},{8,17},{9,... | collective-permute-start | bytes 73736 | tf_op jit(solution)/shard_map/ppermute | solution.py:254
  16.1 3.3 %collective-permute-start.9 = (bf16[96,128]{1,0:T(8,128)(2,1)S(1)}, bf16[96,128]{1,0:T(8,128)(2,1)S(1)}, u32[]{:S(2)}, u32[]{:S(2)}) collective-permute-start(bf16[96,128]{1,0:T(8,128)(2,1)S(1)} %pad_maximum_fusion.1), channel_id=1, source_target_pairs={{0,17},{1,16},{2,19},{3,18},{4,21},{5,20},{6,23},{7,22},{8,25},{9,... | collective-permute-start | bytes 73736 | tf_op jit(solution)/shard_map/ppermute | solution.py:254
  18.0 1.6 %collective-permute-start.7 = (f16[64,128]{1,0:T(8,128)(2,1)S(1)}, f16[64,128]{1,0:T(8,128)(2,1)S(1)}, u32[]{:S(2)}, u32[]{:S(2)}) collective-permute-start(f16[64,128]{1,0:T(8,128)(2,1)S(1)} %multiply_convert_fusion.2), channel_id=1, source_target_pairs={{0,1},{1,0},{2,3},{3,2},{4,5},{5,4},{6,7},{7,6},{8,9},{9,8},{10,11... | collective-permute-start | bytes 49160 | tf_op jit(solution)/shard_map/ppermute | solution.py:254
  19.7 3.4 %collective-permute-start.10 = (f16[128,128]{1,0:T(8,128)(2,1)S(1)}, f16[128,128]{1,0:T(8,128)(2,1)S(1)}, u32[]{:S(2)}, u32[]{:S(2)}) collective-permute-start(f16[128,128]{1,0:T(8,128)(2,1)S(1)} %multiply_convert_fusion.1), channel_id=1, source_target_pairs={{0,3},{8,11},{16,19},{24,27},{1,4},{9,12},{17,20},{25,28},{2,7},{1... | collective-permute-start | bytes 98312 | tf_op jit(solution)/shard_map/ppermute | solution.py:263
  23.2 4.3 %collective-permute-start.11 = (f16[128,128]{1,0:T(8,128)(2,1)S(1)}, f16[128,128]{1,0:T(8,128)(2,1)S(1)}, u32[]{:S(2)}, u32[]{:S(2)}) collective-permute-start(f16[128,128]{1,0:T(8,128)(2,1)S(1)} %multiply_convert_fusion), channel_id=1, source_target_pairs={{0,5},{8,13},{16,21},{24,29},{1,2},{9,10},{17,18},{25,26},{2,1},{1... | collective-permute-start | bytes 98312 | tf_op jit(solution)/shard_map/ppermute | solution.py:263

commit v9 on v8

--- a/solution.py
+++ b/solution.py
@@ -69,19 +69,22 @@
     rows_bf = rows.astype(bf16)
     scale = -math.log2(math.e) / depth
     row_part = jnp.sum(rows * rows, axis=1, keepdims=True) * scale + math.log2(amplitude)
+    blocks = [block_ref[...] for block_ref in blocks]
+    if sum(block.shape[1] for block in blocks) <= COLUMNS:
+        blocks = [jnp.concatenate(blocks, axis=1)]
     total = None
-    for block_ref in blocks:
-        values = block_ref.shape[0] - depth
-        size = block_ref.shape[1]
+    for block in blocks:
+        values = block.shape[0] - depth
+        size = block.shape[1]
         step = min(size, COLUMNS)
         for start in range(0, size, step):
             cut = slice(start, start + step)
-            points = block_ref[values:, cut]
+            points = block[values:, cut]
             wide = points.astype(f32)
             norm_part = jnp.sum(wide * wide, axis=0, keepdims=True) * scale
             inner = jnp.dot(rows_bf, points, preferred_element_type=f32)
             kern = jnp.exp2(inner * (-2.0 * scale) + (row_part + norm_part)).astype(bf16)
-            part = across(block_ref[:values, cut], kern)
+            part = across(block[:values, cut], kern)
             total = part if total is None else total + part
     return total
 
@@ -172,8 +175,8 @@
 
 def share_of(scales, step, upright, rows, angle_ref, weight_ref, base_ref, blocks):
     inv_root, prior_scale = scales
+    prior_part = prior_sum(upright, angle_ref, weight_ref)
     kernel_part = kernel_sum(rows, blocks, rows.shape[1])
-    prior_part = prior_sum(upright, angle_ref, weight_ref)
     values = prior_part.shape[0]
     base = base_ref[values * step : values * (step + 1), :]
     return base - (step_size * inv_root) * kernel_part - (step_size * prior_scale) * prior_part

time: 28.3 us -> 28.4 us (level)
  no operation moved by 1% of the time
where the time goes in v9:
time: 28.4 us; the launch traced here: 28.2 us
  starting transfers between devices  16.2 us (57%)
  waiting for transfers between devices  5.65 us (20%)
  Pallas kernels  5.5 us (19%)
  between operations  0.74 us (3%)
    ppermute x10, starting transfers between devices, swap(): return lax.ppermute(array, ('grp', 'feat'), pairs)  12 us
    pallas_call x8, Pallas kernels, call(): pl.pallas_call(kernel, out_shape=[jax.ShapeDtypeStruct(shape, dtype) for...  5.5 us
    ppermute x2, starting transfers between devices, two_ways(): return lax.ppermute(array, ('grp', 'feat'), pairs)  4.24 us
    ppermute x2, waiting for transfers between devices, two_ways(): return lax.ppermute(array, ('grp', 'feat'), pairs)  3.47 us
    ppermute x10, waiting for transfers between devices, swap(): return lax.ppermute(array, ('grp', 'feat'), pairs)  2.18 us
  transfers between devices with their start and end apart: 12, of which 7 were waited for; matrix products, arithmetic and copies ran while one was open for 0% of the time, Pallas kernels for 13%

profile of v9, /device:TPU:0, one launch (start us, length us, event | category | flops | bytes accessed | tf_op | source)
XLA Modules:
  0.0 28.2 jit_solution(7463462929701526129)
XLA Ops:
  0.6 0.5 %collective-permute-start = (bf16[32,256]{1,0:T(8,128)(2,1)}, bf16[32,256]{1,0:T(8,128)(2,1)S(1)}, u32[]{:S(2)}, u32[]{:S(2)}) collective-permute-start(bf16[32,256]{1,0:T(8,128)(2,1)} %bitcast.17), channel_id=1, source_target_pairs={{0,1},{1,0},{2,3},{3,2},{4,5},{5,4},{6,7},{7,6},{8,9},{9,8},{10,11... | collective-permute-start | bytes 49160 | tf_op jit(solution)/shard_map/ppermute | solution.py:257
  1.1 0.9 %place.1 = (f32[32,256]{1,0:T(8,128)S(1)}, bf16[96,256]{1,0:T(8,128)(2,1)S(1)}) custom-call(s32[2]{0:T(128)} %bitcast.21, bf16[32,256]{1,0:T(8,128)(2,1)} %bitcast.18, f32[64,256]{1,0:T(8,128)} %bitcast.11), custom_call_target="tpu_custom_call" | custom-call | flops 2000000000 | bytes 81928 | tf_op jit(solution)/shard_map/place/pallas_call | solution.py:237
  2.1 2.7 %collective-permute-start.3 = (bf16[96,256]{1,0:T(8,128)(2,1)S(1)}, bf16[96,256]{1,0:T(8,128)(2,1)S(1)}, u32[]{:S(2)}, u32[]{:S(2)}) collective-permute-start(bf16[96,256]{1,0:T(8,128)(2,1)S(1)} %get-tuple-element.22.static_ref), channel_id=1, source_target_pairs={{0,9},{1,8},{2,11},{3,10},{4,13},{5,12},{6,15},{7,14},{8,1},{9,0},... | collective-permute-start | bytes 147464 | tf_op jit(solution)/shard_map/ppermute | solution.py:257
  4.7 0.0 collective-permute-done.other_ref
  4.7 2.3 %collective-permute-start.1 = (bf16[64,128]{1,0:T(8,128)(2,1)S(1)}, bf16[64,128]{1,0:T(8,128)(2,1)S(1)}, u32[]{:S(2)}, u32[]{:S(2)}) collective-permute-start(bf16[64,128]{1,0:T(8,128)(2,1)S(1)} %pack.1), channel_id=1, source_target_pairs={{0,5},{1,4},{2,7},{3,6},{4,1},{5,0},{6,3},{7,2},{8,13},{9,12},{10,... | collective-permute-start | bytes 49160 | tf_op jit(solution)/shard_map/ppermute | solution.py:257
  7.0 0.0 collective-permute-done.3
  7.0 1.7 %collective-permute-start.4 = (bf16[96,512]{1,0:T(8,128)(2,1)S(1)}, bf16[96,512]{1,0:T(8,128)(2,1)S(1)}, u32[]{:S(2)}, u32[]{:S(2)}) collective-permute-start(bf16[96,512]{1,0:T(8,128)(2,1)S(1)} %constant_dynamic-update-slice_fusion.rest_2_.rest_0_), channel_id=1, source_target_pairs={{0,17},{1,16},{2,19},{3,18},{4,21},{5,20},{6,23},{7,22},{8,25},{9,... | collective-permute-start | bytes 294920 | tf_op jit(solution)/shard_map/ppermute | solution.py:257
  8.7 0.2 collective-permute-done.1
  8.9 1.4 %collective-permute-start.2 = (bf16[64,128]{1,0:T(8,128)(2,1)S(1)}, bf16[64,128]{1,0:T(8,128)(2,1)S(1)}, u32[]{:S(2)}, u32[]{:S(2)}) collective-permute-start(bf16[64,128]{1,0:T(8,128)(2,1)S(1)} %add.18.rest_0_), channel_id=1, source_target_pairs={{0,3},{1,2},{2,1},{3,0},{4,7},{5,6},{6,5},{7,4},{8,11},{9,10},{10,... | collective-permute-start | bytes 49160 | tf_op jit(solution)/shard_map/ppermute | solution.py:257
  10.2 1.3 %prepare.1 = (bf16[128,2048]{1,0:T(8,128)(2,1)S(1)}, bf16[64,2048]{1,0:T(8,128)(2,1)S(1)}, f32[128,128]{1,0:T(8,128)S(1)}, f32[64,256]{1,0:T(8,128)S(1)}, f32[64,256]{1,0:T(8,128)S(1)}) custom-call(bf16[32,2048]{1,0:T(8,128)(2,1)} %freq_hbm.1, f32[1,2048]{1,0:T(1,128)} %bitcast.19, bf16[64,2048]{1,0:T(8,128)(2,1)} %bitcast.10, f32[1,256]{1,0:T(1,128)} %bitcast.20, ...), custom_call_target="tpu_custom_call" | custom-call | flops 1000000000 | bytes 631808 | tf_op jit(solution)/shard_map/prepare/pallas_call | solution.py:237
  11.5 0.6 %collective-permute-done.2.rest_1_ = bf16[64,128]{1,0:T(8,128)(2,1)S(1)} collective-permute-done((bf16[64,128]{1,0:T(8,128)(2,1)S(1)}, bf16[64,128]{1,0:T(8,128)(2,1)S(1)}, u32[]{:S(2)}, u32[]{:S(2)}) %collective-permute-start.2) | collective-permute-done | bytes 16416 | tf_op jit(solution)/shard_map/ppermute | solution.py:257
  12.1 0.0 collective-permute-done.4.rest_3_.rest_1_
  12.1 1.0 %first.1 = (f32[64,128]{1,0:T(8,128)S(1)}, bf16[96,128]{1,0:T(8,128)(2,1)S(1)}, bf16[64,128]{1,0:T(8,128)(2,1)S(1)}) custom-call(bf16[128,2048]{1,0:T(8,128)(2,1)S(1)} %get-tuple-element.19.angle_ref, bf16[64,2048]{1,0:T(8,128)(2,1)S(1)} %get-tuple-element.20.weight_ref, f32[128,128]{1,0:T(8,128)S(1)} %get-tuple-element.21.base_ref, ...), custom_call_target="tpu_custom_call" | custom-call | flops 1000000000 | bytes 1081344 | tf_op jit(solution)/shard_map/first/pallas_call | solution.py:237
  13.2 0.2 collective-permute-start.5
  13.4 0.9 %collective-permute-start.6 = (bf16[96,128]{1,0:T(8,128)(2,1)S(1)}, bf16[96,128]{1,0:T(8,128)(2,1)S(1)}, u32[]{:S(2)}, u32[]{:S(2)}) collective-permute-start(bf16[96,128]{1,0:T(8,128)(2,1)S(1)} %get-tuple-element.28.rest_0_), channel_id=1, source_target_pairs={{0,9},{1,8},{2,11},{3,10},{4,13},{5,12},{6,15},{7,14},{8,1},{9,0},... | collective-permute-start | bytes 73736 | tf_op jit(solution)/shard_map/ppermute | solution.py:257
  14.2 0.2 collective-permute-done.5
  14.5 1.7 %collective-permute-start.8 = (bf16[96,128]{1,0:T(8,128)(2,1)S(1)}, bf16[96,128]{1,0:T(8,128)(2,1)S(1)}, u32[]{:S(2)}, u32[]{:S(2)}) collective-permute-start(bf16[96,128]{1,0:T(8,128)(2,1)S(1)} %pad_maximum_fusion.1), channel_id=1, source_target_pairs={{0,25},{1,24},{2,27},{3,26},{4,29},{5,28},{6,31},{7,30},{8,17},{9,... | collective-permute-start | bytes 73736 | tf_op jit(solution)/shard_map/ppermute | solution.py:257
  16.2 0.5 %collective-permute-start.9 = (bf16[96,128]{1,0:T(8,128)(2,1)S(1)}, bf16[96,128]{1,0:T(8,128)(2,1)S(1)}, u32[]{:S(2)}, u32[]{:S(2)}) collective-permute-start(bf16[96,128]{1,0:T(8,128)(2,1)S(1)} %pad_maximum_fusion.1), channel_id=1, source_target_pairs={{0,17},{1,16},{2,19},{3,18},{4,21},{5,20},{6,23},{7,22},{8,25},{9,... | collective-permute-start | bytes 73736 | tf_op jit(solution)/shard_map/ppermute | solution.py:257
  16.7 1.0 %second.1 = (f32[64,128]{1,0:T(8,128)S(1)}, f32[128,32]{1,0:T(8,128)S(1)}) custom-call(bf16[128,2048]{1,0:T(8,128)(2,1)S(1)} %get-tuple-element.19.angle_ref, bf16[64,2048]{1,0:T(8,128)(2,1)S(1)} %get-tuple-element.20.weight_ref, f32[128,128]{1,0:T(8,128)S(1)} %get-tuple-element.21.base_ref, bf16[64,128]{1,0:T(8,128)(2,1)S(1)} %get-tuple-element.25.batch_ref, ...), custom_call_target="tpu_custom_call" | custom-call | tf_op jit(solution)/shard_map/second/pallas_call | solution.py:237
  17.7 0.0 collective-permute-done.6.rest_1_
  17.7 0.3 correct.1
  18.0 0.2 collective-permute-start.7
  18.3 0.4 %collective-permute-done.8.rest_0_ = bf16[96,128]{1,0:T(8,128)(2,1)S(1)} collective-permute-done((bf16[96,128]{1,0:T(8,128)(2,1)S(1)}, bf16[96,128]{1,0:T(8,128)(2,1)S(1)}, u32[]{:S(2)}, u32[]{:S(2)}) %collective-permute-start.8) | collective-permute-done | bytes 24608 | tf_op jit(solution)/shard_map/ppermute | solution.py:257
  18.7 0.8 %collective-permute-done.9.rest_1_ = bf16[96,128]{1,0:T(8,128)(2,1)S(1)} collective-permute-done((bf16[96,128]{1,0:T(8,128)(2,1)S(1)}, bf16[96,128]{1,0:T(8,128)(2,1)S(1)}, u32[]{:S(2)}, u32[]{:S(2)}) %collective-permute-start.9) | collective-permute-done | bytes 24608 | tf_op jit(solution)/shard_map/ppermute | solution.py:257
  19.5 0.3 join.1
  19.7 0.0 collective-permute-done.7
  19.8 1.6 %collective-permute-start.10 = (f16[128,128]{1,0:T(8,128)(2,1)S(1)}, f16[128,128]{1,0:T(8,128)(2,1)S(1)}, u32[]{:S(2)}, u32[]{:S(2)}) collective-permute-start(f16[128,128]{1,0:T(8,128)(2,1)S(1)} %multiply_convert_fusion.1), channel_id=1, source_target_pairs={{0,3},{8,11},{16,19},{24,27},{1,4},{9,12},{17,20},{25,28},{2,7},{1... | collective-permute-start | bytes 98312 | tf_op jit(solution)/shard_map/ppermute | solution.py:266
  21.4 1.8 %collective-permute-done.10 = f16[128,128]{1,0:T(8,128)(2,1)S(1)} collective-permute-done((f16[128,128]{1,0:T(8,128)(2,1)S(1)}, f16[128,128]{1,0:T(8,128)(2,1)S(1)}, u32[]{:S(2)}, u32[]{:S(2)}) %collective-permute-start.10) | collective-permute-done | bytes 32800 | tf_op jit(solution)/shard_map/ppermute | solution.py:266
  23.2 2.6 %collective-permute-start.11 = (f16[128,128]{1,0:T(8,128)(2,1)S(1)}, f16[128,128]{1,0:T(8,128)(2,1)S(1)}, u32[]{:S(2)}, u32[]{:S(2)}) collective-permute-start(f16[128,128]{1,0:T(8,128)(2,1)S(1)} %multiply_convert_fusion), channel_id=1, source_target_pairs={{0,5},{8,13},{16,21},{24,29},{1,2},{9,10},{17,18},{25,26},{2,1},{1... | collective-permute-start | bytes 98312 | tf_op jit(solution)/shard_map/ppermute | solution.py:266
  25.9 1.7 %collective-permute-done.11 = f16[128,128]{1,0:T(8,128)(2,1)S(1)} collective-permute-done((f16[128,128]{1,0:T(8,128)(2,1)S(1)}, f16[128,128]{1,0:T(8,128)(2,1)S(1)}, u32[]{:S(2)}, u32[]{:S(2)}) %collective-permute-start.11) | collective-permute-done | bytes 32800 | tf_op jit(solution)/shard_map/ppermute | solution.py:266
  27.5 0.7 %finish.1 = (f32[64,256]{1,0:T(8,128)}, f32[64,256]{1,0:T(8,128)}) custom-call(f32[32,256]{1,0:T(8,128)S(1)} %get-tuple-element.18.marks_ref, f32[128,128]{1,0:T(8,128)S(1)} %multiply_add_fusion.total_ref, f32[64,256]{1,0:T(8,128)S(1)} %get-tuple-element.30.duals_ref, f32[64,256]{1,0:T(8,128)S(1)} %get-tuple-element.31.velocity_ref), custom_call_target="tpu_custom_call" | custom-call | tf_op jit(solution)/shard_map/finish/pallas_call | solution.py:237
  (12 shorter events, 0.1 us)
Async XLA Ops:
  0.6 4.1 %collective-permute-start = (bf16[32,256]{1,0:T(8,128)(2,1)}, bf16[32,256]{1,0:T(8,128)(2,1)S(1)}, u32[]{:S(2)}, u32[]{:S(2)}) collective-permute-start(bf16[32,256]{1,0:T(8,128)(2,1)} %bitcast.17), channel_id=1, source_target_pairs={{0,1},{1,0},{2,3},{3,2},{4,5},{5,4},{6,7},{7,6},{8,9},{9,8},{10,11... | collective-permute-start | bytes 49160 | tf_op jit(solution)/shard_map/ppermute | solution.py:257
  2.1 5.0 %collective-permute-start.3 = (bf16[96,256]{1,0:T(8,128)(2,1)S(1)}, bf16[96,256]{1,0:T(8,128)(2,1)S(1)}, u32[]{:S(2)}, u32[]{:S(2)}) collective-permute-start(bf16[96,256]{1,0:T(8,128)(2,1)S(1)} %get-tuple-element.22.static_ref), channel_id=1, source_target_pairs={{0,9},{1,8},{2,11},{3,10},{4,13},{5,12},{6,15},{7,14},{8,1},{9,0},... | collective-permute-start | bytes 147464 | tf_op jit(solution)/shard_map/ppermute | solution.py:257
  4.7 4.1 %collective-permute-start.1 = (bf16[64,128]{1,0:T(8,128)(2,1)S(1)}, bf16[64,128]{1,0:T(8,128)(2,1)S(1)}, u32[]{:S(2)}, u32[]{:S(2)}) collective-permute-start(bf16[64,128]{1,0:T(8,128)(2,1)S(1)} %pack.1), channel_id=1, source_target_pairs={{0,5},{1,4},{2,7},{3,6},{4,1},{5,0},{6,3},{7,2},{8,13},{9,12},{10,... | collective-permute-start | bytes 49160 | tf_op jit(solution)/shard_map/ppermute | solution.py:257
  7.0 5.1 %collective-permute-start.4 = (bf16[96,512]{1,0:T(8,128)(2,1)S(1)}, bf16[96,512]{1,0:T(8,128)(2,1)S(1)}, u32[]{:S(2)}, u32[]{:S(2)}) collective-permute-start(bf16[96,512]{1,0:T(8,128)(2,1)S(1)} %constant_dynamic-update-slice_fusion.rest_2_.rest_0_), channel_id=1, source_target_pairs={{0,17},{1,16},{2,19},{3,18},{4,21},{5,20},{6,23},{7,22},{8,25},{9,... | collective-permute-start | bytes 294920 | tf_op jit(solution)/shard_map/ppermute | solution.py:257
  8.9 3.2 %collective-permute-start.2 = (bf16[64,128]{1,0:T(8,128)(2,1)S(1)}, bf16[64,128]{1,0:T(8,128)(2,1)S(1)}, u32[]{:S(2)}, u32[]{:S(2)}) collective-permute-start(bf16[64,128]{1,0:T(8,128)(2,1)S(1)} %add.18.rest_0_), channel_id=1, source_target_pairs={{0,3},{1,2},{2,1},{3,0},{4,7},{5,6},{6,5},{7,4},{8,11},{9,10},{10,... | collective-permute-start | bytes 49160 | tf_op jit(solution)/shard_map/ppermute | solution.py:257
  13.2 1.3 %collective-permute-start.5 = (f32[64,128]{1,0:T(8,128)S(1)}, f32[64,128]{1,0:T(8,128)S(1)}, u32[]{:S(2)}, u32[]{:S(2)}) collective-permute-start(f32[64,128]{1,0:T(8,128)S(1)} %get-tuple-element.23), channel_id=1, source_target_pairs={{0,1},{1,0},{2,3},{3,2},{4,5},{5,4},{6,7},{7,6},{8,9},{9,8},{10,11... | collective-permute-start | bytes 98312 | tf_op jit(solution)/shard_map/ppermute | solution.py:257
  13.4 4.4 %collective-permute-start.6 = (bf16[96,128]{1,0:T(8,128)(2,1)S(1)}, bf16[96,128]{1,0:T(8,128)(2,1)S(1)}, u32[]{:S(2)}, u32[]{:S(2)}) collective-permute-start(bf16[96,128]{1,0:T(8,128)(2,1)S(1)} %get-tuple-element.28.rest_0_), channel_id=1, source_target_pairs={{0,9},{1,8},{2,11},{3,10},{4,13},{5,12},{6,15},{7,14},{8,1},{9,0},... | collective-permute-start | bytes 73736 | tf_op jit(solution)/shard_map/ppermute | solution.py:257
  14.5 4.2 %collective-permute-start.8 = (bf16[96,128]{1,0:T(8,128)(2,1)S(1)}, bf16[96,128]{1,0:T(8,128)(2,1)S(1)}, u32[]{:S(2)}, u32[]{:S(2)}) collective-permute-start(bf16[96,128]{1,0:T(8,128)(2,1)S(1)} %pad_maximum_fusion.1), channel_id=1, source_target_pairs={{0,25},{1,24},{2,27},{3,26},{4,29},{5,28},{6,31},{7,30},{8,17},{9,... | collective-permute-start | bytes 73736 | tf_op jit(solution)/shard_map/ppermute | solution.py:257
  16.2 3.3 %collective-permute-start.9 = (bf16[96,128]{1,0:T(8,128)(2,1)S(1)}, bf16[96,128]{1,0:T(8,128)(2,1)S(1)}, u32[]{:S(2)}, u32[]{:S(2)}) collective-permute-start(bf16[96,128]{1,0:T(8,128)(2,1)S(1)} %pad_maximum_fusion.1), channel_id=1, source_target_pairs={{0,17},{1,16},{2,19},{3,18},{4,21},{5,20},{6,23},{7,22},{8,25},{9,... | collective-permute-start | bytes 73736 | tf_op jit(solution)/shard_map/ppermute | solution.py:257
  18.0 1.7 %collective-permute-start.7 = (f16[64,128]{1,0:T(8,128)(2,1)S(1)}, f16[64,128]{1,0:T(8,128)(2,1)S(1)}, u32[]{:S(2)}, u32[]{:S(2)}) collective-permute-start(f16[64,128]{1,0:T(8,128)(2,1)S(1)} %multiply_convert_fusion.2), channel_id=1, source_target_pairs={{0,1},{1,0},{2,3},{3,2},{4,5},{5,4},{6,7},{7,6},{8,9},{9,8},{10,11... | collective-permute-start | bytes 49160 | tf_op jit(solution)/shard_map/ppermute | solution.py:257
  19.8 3.4 %collective-permute-start.10 = (f16[128,128]{1,0:T(8,128)(2,1)S(1)}, f16[128,128]{1,0:T(8,128)(2,1)S(1)}, u32[]{:S(2)}, u32[]{:S(2)}) collective-permute-start(f16[128,128]{1,0:T(8,128)(2,1)S(1)} %multiply_convert_fusion.1), channel_id=1, source_target_pairs={{0,3},{8,11},{16,19},{24,27},{1,4},{9,12},{17,20},{25,28},{2,7},{1... | collective-permute-start | bytes 98312 | tf_op jit(solution)/shard_map/ppermute | solution.py:266
  23.2 4.3 %collective-permute-start.11 = (f16[128,128]{1,0:T(8,128)(2,1)S(1)}, f16[128,128]{1,0:T(8,128)(2,1)S(1)}, u32[]{:S(2)}, u32[]{:S(2)}) collective-permute-start(f16[128,128]{1,0:T(8,128)(2,1)S(1)} %multiply_convert_fusion), channel_id=1, source_target_pairs={{0,5},{8,13},{16,21},{24,29},{1,2},{9,10},{17,18},{25,26},{2,1},{1... | collective-permute-start | bytes 98312 | tf_op jit(solution)/shard_map/ppermute | solution.py:266
